TPU v7x, 32 devices: a whole 2x2x4 slice. The times are simulated.
32 devices in a mesh: rel: 8 (over z, y), dom: 4 (over x, core).
Axes of the slice: x: 2, y: 2, z: 4, core: 2. Of those that a mesh axis runs over, the one named last changes fastest.
Arguments:
- edge_feats: bfloat16 [4, 4096, 1024], P('dom', 'rel'), may hold values from -6 to 6
- gain: float32 [1024], replicated, may hold values from 0.25 to 1.75
- w_in: bfloat16 [8, 1024, 2048], P('rel'), may hold values from -0.1875 to 0.1875
- w_out: bfloat16 [8, 2048, 1024], P('rel'), may hold values from -0.125 to 0.125
- rel_type: int32 [4, 4096, 1], P('dom', 'rel'), may hold values from 0 to 7; in each aligned block of 512 rows (0 to 511, 512 to 1023, ..., all dimensions but the last counted through in order) at most 128 rows name the same one
- dst_node: int32 [4, 4096], P('dom', 'rel'), may hold values from 0 to 1023, as said below
Outputs:
- node_state: float32 [4, 256, 1024], P('dom', 'rel')
Inputs may be any that keep to these rules, and one draw needn't show every extreme that they name: `rel_type`: in the 512 edges of one device (aligned blocks of rows) at most 128 edges have one relation type, and some relation has exactly 128 there; every relation occurs. `dst_node`: node ids; node n belongs to partition group n // 256 and, within it, to owner index (n // 32) % 8. In the 512 edges of one device (aligned blocks of rows) at most 32 point to nodes of one (group, owner index) pair, and some pair has exactly 32 there.
All inputs are finite; a program needn't handle non-finite values.
Results may differ from a plain program's by a relative error of at most 0.011.
Values may be sent and summed in bfloat16 or wider, within the bound.
No kernel may reach another device: no remote copies, remote signals or barrier semaphores. Data moves between devices by JAX's collectives and lax.ppermute only.
A program may use at most 128 MiB of HBM per device.

v0:
```python
import math

import jax
import jax.numpy as jnp
from jax import lax
from jax.sharding import PartitionSpec as P

NODE_DEV = 32


def expert_mlp(rows, w_first, w_second):
    hidden = jax.nn.gelu(
        jnp.einsum("rnd,dh->rnh", rows, w_first, preferred_element_type=jnp.float32),
        approximate=False,
    ).astype(jnp.bfloat16)
    return jnp.einsum("rnh,hd->rnd", hidden, w_second, preferred_element_type=jnp.float32).astype(
        jnp.bfloat16
    )


def send_back(values):
    return lax.all_to_all(values, "rel", split_axis=0, concat_axis=0, tiled=True)


def slot_ranks(labels, count):
    marks = (labels[:, None] == jnp.arange(count, dtype=jnp.int32)[None, :]).astype(jnp.int32)
    return jnp.sum(jnp.cumsum(marks, axis=0) * marks, axis=1) - 1


def local(edge_feats, gain, w_in, w_out, rel_type, dst_node):
    rows = edge_feats.shape[1]
    width = edge_feats.shape[2]
    relations = lax.axis_size("rel")
    groups = lax.axis_size("dom")
    nodes_dev = NODE_DEV
    slots = 2 * rows // relations
    columns = groups * relations * nodes_dev
    w_first = w_in[0]
    w_second = w_out[0]
    feats = edge_feats[0].astype(jnp.float32)
    scale_rows = lax.rsqrt(jnp.mean(feats * feats, axis=1, keepdims=True) + 1e-06)
    normed = (feats * scale_rows * gain[None, :]).astype(jnp.bfloat16)
    kinds = rel_type[0, :, 0]
    rank = slot_ranks(kinds, relations)
    outgoing = jnp.zeros((relations, slots, width), jnp.bfloat16).at[kinds, rank].set(normed)
    dest = dst_node[0]
    factor = 1.0 / math.sqrt(rows / nodes_dev)
    messages = send_back(
        expert_mlp(
            lax.all_to_all(outgoing, "rel", split_axis=0, concat_axis=0, tiled=True),
            w_first,
            w_second,
        )
    )
    col_ids = jnp.arange(columns, dtype=jnp.int32)
    edge_msgs = messages[kinds, rank]
    table = (dest[:, None] == col_ids[None, :]).astype(jnp.bfloat16)
    partial_value = jnp.einsum("ec,ed->cd", table, edge_msgs, preferred_element_type=jnp.float32)
    in_group = lax.psum_scatter(
        partial_value.reshape(groups, relations * nodes_dev, width).astype(jnp.bfloat16),
        "rel",
        scatter_dimension=1,
        tiled=True,
    ).astype(jnp.float32)
    crossed = lax.all_to_all(in_group, "dom", split_axis=0, concat_axis=0, tiled=True)
    total = jnp.sum(crossed, axis=0)
    return (total * factor)[None, :, :]


def solution(mesh):
    in_specs = (
        P("dom", "rel", None),
        P(),
        P("rel", None, None),
        P("rel", None, None),
        P("dom", "rel", None),
        P("dom", "rel"),
    )
    out_specs = P("dom", "rel", None)
    return jax.shard_map(local, mesh=mesh, in_specs=in_specs, out_specs=out_specs, check_vma=False)
```

profile of v0, /device:TPU:0, one launch (start us, length us, event | category | flops | bytes accessed | tf_op | source)
XLA Modules:
  0.0 279.2 jit_solution(17238355311588653609)
XLA Ops:
  6.5 0.0 reduce-scatter.2.cloned.1.call-start
  6.5 1.5 fusion.43
  8.0 0.7 fusion.59
  8.7 1.1 reduce-window.6
  9.9 0.2 slice_reduce_fusion
  10.1 0.8 fusion.58
  10.9 0.7 or_select_fusion
  11.6 1.5 fusion.45
  13.1 0.3 broadcast_in_dim.2
  13.4 33.1 %scatter_fusion = bf16[8,128,1024]{2,1,0:T(8,128)(2,1)S(1)} fusion(bf16[8,128,1024]{2,1,0:T(8,128)(2,1)S(1)} %broadcast_in_dim.2, s32[512]{0:T(512)S(1)} %bitcast.42, bf16[512,1024]{1,0:T(8,128)(2,1)S(1)} %fusion.45), kind=kCustom, calls=%fused_computation.1 | custom fusion | bytes 3149824 | tf_op jit(solution)/shard_map/scatter | solution.py:45
  46.5 55.3 %all_to_all.15 = bf16[8,128,1024]{2,1,0:T(8,128)(2,1)S(1)} all-to-all(bf16[8,128,1024]{2,1,0:T(8,128)(2,1)S(1)} %scatter_fusion), channel_id=1, replica_groups=mesh['rel'=8,'dom'=4] {'rel'}, dimensions={0} | all-to-all | bytes 4194304 | tf_op jit(solution)/shard_map/all_to_all | solution.py:50
  101.8 8.6 %fusion.47 = (u8[128,2048]{1,0:T(8,128)(4,1)S(1)}, u8[128,2048]{1,0:T(8,128)(4,1)S(1)}, f32[8,128,2048]{2,1,0:T(8,128)S(1)}) fusion(bf16[8,128,1024]{2,1,0:T(8,128)(2,1)S(1)} %all_to_all.15, bf16[1,1024,2048]{2,1,0:T(8,128)(2,1)} %param.8), kind=kOutput, calls=%fused_computation.64 | convolution fusion | flops 4321705984 | bytes 15204352 | tf_op jit(solution)/shard_map/rnd,dh->rnh/dot_general | solution.py:13
  110.5 0.0 copy-done
  110.5 22.0 %fusion.50 = bf16[8,128,1024]{2,1,0:T(8,128)(2,1)S(1)} fusion(bf16[1,2048,1024]{2,1,0:T(8,128)(2,1)S(1)} %copy-done, f32[8,128,2048]{2,1,0:T(8,128)S(1)} %get-tuple-element.11, u8[128,2048]{1,0:T(8,128)(4,1)S(1)} %get-tuple-element.6, u8[128,2048]{1,0:T(8,128)(4,1)S(1)} %get-tuple-element.5), kind=kOutput, calls=%fused_computation.67 | convolution fusion | flops 4442816512 | bytes 15204352 | tf_op jit(solution)/shard_map/rnh,hd->rnd/dot_general | solution.py:16
  132.5 0.0 copy-start.1
  132.5 51.4 %all_to_all.16 = bf16[8,128,1024]{2,1,0:T(8,128)(2,1)S(1)} all-to-all(bf16[8,128,1024]{2,1,0:T(8,128)(2,1)S(1)} %fusion.50), channel_id=1, replica_groups=mesh['rel'=8,'dom'=4] {'rel'}, dimensions={0} | all-to-all | bytes 4194304 | tf_op jit(solution)/shard_map/all_to_all | solution.py:22
  183.9 5.3 %gather_fusion = bf16[512,1024]{1,0:T(8,128)(2,1)S(1)} fusion(bf16[8,128,1024]{2,1,0:T(8,128)(2,1)S(1)} %all_to_all.16, s32[512]{0:T(512)S(1)} %bitcast.43), kind=kCustom, calls=%fused_computation | custom fusion | bytes 2101248 | tf_op jit(solution)/shard_map/gather | solution.py:56
  189.2 0.0 copy-done.1
  189.2 2.7 fusion.49
  191.9 0.0 reduce-scatter.2.cloned.1.call-update
  191.9 67.4 %reduce-scatter.2.cloned.1.call-done = bf16[4,32,1024]{2,1,0:T(8,128)(2,1)} async-done(((bf16[4,256,1024]{2,1,0:T(8,128)(2,1)}), bf16[4,32,1024]{2,1,0:T(8,128)(2,1)}) %reduce-scatter.2.cloned.1.call-update) | async-done | bytes 262160 | tf_op jit(solution)/shard_map/reduce_scatter | solution.py:59
  259.3 1.0 convert_element_type.38
  260.3 11.4 %all_to_all.17 = f32[4,32,1024]{2,1,0:T(8,128)S(1)} all-to-all(f32[4,32,1024]{2,1,0:T(8,128)S(1)} %convert_element_type.38), channel_id=1, replica_groups=mesh['rel'=8,'dom'=4] {'dom'}, dimensions={0} | all-to-all | bytes 1048576 | tf_op jit(solution)/shard_map/all_to_all | solution.py:65
  271.7 0.7 multiply_bitcast_fusion
  (6 shorter events, 0.1 us)
Async XLA Ops:
  6.5 252.8 %reduce-scatter.2.cloned.1.call-start = ((), (), s32[]{:S(2)}) async-start(), calls=%async_computation.4 | async-start | bytes 2359296 | tf_op jit(solution)/shard_map/reduce_scatter | solution.py:59
  101.8 8.7 %copy-start = (bf16[1,2048,1024]{2,1,0:T(8,128)(2,1)S(1)}, bf16[1,2048,1024]{2,1,0:T(8,128)(2,1)}, u32[]{:S(2)}) copy-start(bf16[1,2048,1024]{2,1,0:T(8,128)(2,1)} %param.9) | copy-start | bytes 12582916
  132.5 56.6 %copy-start.1 = (s32[1,512]{1,0:T(1,128)S(1)}, s32[1,512]{1,0:T(1,128)}, u32[]{:S(2)}) copy-start(s32[1,512]{1,0:T(1,128)} %param.11) | copy-start | bytes 6148
Sparse Core Ops, SparseCore 0:
  192.0 67.2 reduce-scatter.1
where the time goes:
time: 280 us; the launch traced here: 279 us
  blocking collectives  118 us (42%)
  waiting for transfers between devices  67.4 us (24%)
  local copies, waits for them, and re-layouts  38.8 us (14%)
  matrix products  33.4 us (12%)
  between operations  13.5 us (5%)
  other arithmetic  8.06 us (3%)
    reduce_scatter x1, waiting for transfers between devices, local(): lax.psum_scatter(partial_value.reshape(groups, relations * nodes_dev, wid...  67.4 us
    all_to_all x1, blocking collectives, local(): lax.all_to_all(outgoing, 'rel', split_axis=0, concat_axis=0, tiled=True)  55.3 us
    all_to_all x1, blocking collectives, send_back(): lax.all_to_all(values, 'rel', split_axis=0, concat_axis=0, tiled=True)  51.4 us
    scatter x1, local copies, waits for them, and re-layouts, local(): jnp.zeros((relations, slots, width), jnp.bfloat16).at[kinds, rank]  33.1 us
    dot_general x1, matrix products, expert_mlp(): jnp.einsum('rnh,hd->rnd', hidden, w_second, preferred_element_type=jnp.fl...  22 us
    all_to_all x1, blocking collectives, local(): lax.all_to_all(in_group, 'dom', split_axis=0, concat_axis=0, tiled=True)  11.4 us
    dot_general x1, matrix products, expert_mlp(): jnp.einsum('rnd,dh->rnh', rows, w_first, preferred_element_type=jnp.float32)  8.65 us
  transfers between devices with their start and end apart: 1, of which 1 were waited for; matrix products, arithmetic and copies ran while one was open for 0% of the time, Pallas kernels for 0%

commit v1 on v0

v1 whole, which is shorter than its diff:
```python
import functools
import math

import jax
import jax.numpy as jnp
from jax import lax
from jax.experimental import pallas as pl
from jax.experimental.pallas import tpu as pltpu
from jax.sharding import PartitionSpec as P

NODE_DEV = 32
VMEM_BYTES = 48 * 1024 * 1024
VM = pl.BlockSpec(memory_space=pltpu.VMEM)
SM = pl.BlockSpec(memory_space=pltpu.SMEM)


def pack_kernel(relations, slots, place_ref, kinds_ref, dest_ref, feats_ref, gain_ref, *outs):
    blocks, ids_ref, normed_ref = outs[:relations], outs[relations], outs[relations + 1]
    rows, width = feats_ref.shape
    part = 128
    gain = gain_ref[...]

    def norm(i, carry):
        at = pl.ds(pl.multiple_of(i * part, part), part)
        feats = feats_ref[at, :].astype(jnp.float32)
        scale = lax.rsqrt(jnp.mean(feats * feats, axis=1, keepdims=True) + 1e-06)
        normed_ref[at, :] = (feats * scale * gain).astype(jnp.bfloat16)
        return carry

    lax.fori_loop(0, rows // part, norm, 0)
    offset = kinds_ref[...] ^ place_ref[0]
    lanes = max(relations, 16)
    marks = offset == lax.broadcasted_iota(jnp.int32, (lanes, rows), 0)
    ones = marks.astype(jnp.bfloat16)
    before = (
        lax.broadcasted_iota(jnp.int32, (rows, rows), 0) < lax.broadcasted_iota(jnp.int32, (rows, rows), 1)
    ).astype(jnp.bfloat16)
    count = jnp.dot(ones, before, preferred_element_type=jnp.float32)
    rank = jnp.sum(jnp.where(marks, count, 0.0), axis=0, keepdims=True).astype(jnp.int32)
    slot = offset * slots + rank
    dest = dest_ref[...]
    line = lax.broadcasted_iota(jnp.int32, (16, rows), 0)
    coded = jnp.where(
        line == 0, dest // NODE_DEV, jnp.where(line == 1, dest % NODE_DEV, jnp.where(line == 2, 1, 0))
    ).astype(jnp.bfloat16)
    normed = normed_ref[...]
    for d in range(relations):
        pick = (slot == lax.broadcasted_iota(jnp.int32, (slots, rows), 0) + d * slots).astype(jnp.bfloat16)
        blocks[d][...] = jnp.dot(pick, normed, preferred_element_type=jnp.float32).astype(jnp.bfloat16)
        got = lax.dot_general(
            coded, pick, (((1,), (1,)), ((), ())), preferred_element_type=jnp.float32
        ).astype(jnp.int32)
        ids_ref[d : d + 1, :] = jnp.where(got[2:3] > 0, got[0:1] * NODE_DEV + got[1:2], -1)


def pack(place, kinds, dest, feats, gain, relations, slots):
    rows, width = feats.shape
    shapes = [jax.ShapeDtypeStruct((slots, width), jnp.bfloat16)] * relations
    shapes.append(jax.ShapeDtypeStruct((relations, slots), jnp.int32))
    outs = pl.pallas_call(
        functools.partial(pack_kernel, relations, slots),
        out_shape=shapes,
        in_specs=[SM, VM, VM, VM, VM],
        out_specs=[VM] * len(shapes),
        scratch_shapes=[pltpu.VMEM((rows, width), jnp.bfloat16)],
        compiler_params=pltpu.CompilerParams(vmem_limit_bytes=24 * 1024 * 1024),
        cost_estimate=pl.CostEstimate(
            flops=2 * rows * width * relations * slots, bytes_accessed=4 * rows * width * 2, transcendentals=0
        ),
        name="pack",
    )(place, kinds, dest, feats, gain)
    return outs[:relations], outs[relations]


def gelu(x):
    return 0.5 * x * (1.0 + lax.erf(x * math.sqrt(0.5)))


def expert_kernel(first, count, slots, groups, relations, has_sums, last, place_ref, ids_ref, *refs):
    blocks, refs = refs[:count], refs[count:]
    w_first_ref, w_second_ref, refs = refs[0], refs[1], refs[2:]
    if has_sums:
        sums_ref, refs = refs[0], refs[1:]
    outs, (x_ref, hidden_ref, row_ref) = refs[:-3], refs[-3:]
    width, inner = w_first_ref.shape
    rows = count * slots
    mine, base = place_ref[0], place_ref[1]
    half = relations // 2
    for i in range(count):
        x_ref[i * slots : (i + 1) * slots, :] = blocks[i][...]
        node = ids_ref[mine ^ (first + i), first + i : first + i + 1, :]
        away = node ^ base
        j = away % NODE_DEV
        y = (away // NODE_DEV) % 2
        z = (away // (2 * NODE_DEV)) % half
        g = away // (NODE_DEV * relations)
        at = (((g % 2) * 2 + g // 2) * 2 + y) * half * NODE_DEV + z * NODE_DEV + j
        row_ref[:, i * slots : (i + 1) * slots] = jnp.where(node < 0, -1, at)
    part = 256

    def up(i, carry):
        at = pl.ds(pl.multiple_of(i * part, part), part)
        h = jnp.dot(x_ref[...], w_first_ref[:, at], preferred_element_type=jnp.float32)
        hidden_ref[:, at] = gelu(h).astype(jnp.bfloat16)
        return carry

    lax.fori_loop(0, inner // part, up, 0, unroll=2)
    nodes = groups * relations * NODE_DEV
    piece = nodes // 8

    def down(i, carry):
        at = pl.ds(pl.multiple_of(i * part, part), part)
        message = jnp.dot(hidden_ref[...], w_second_ref[:, at], preferred_element_type=jnp.float32)
        message = message.astype(jnp.bfloat16)
        for b in range(8):
            table = (
                row_ref[...] == lax.broadcasted_iota(jnp.int32, (piece, rows), 0) + b * piece
            ).astype(jnp.bfloat16)
            total = jnp.dot(table, message, preferred_element_type=jnp.float32)
            if has_sums:
                total = total + sums_ref[b * piece : (b + 1) * piece, at]
            if last:
                outs[b][:, at] = total.astype(jnp.bfloat16)
            else:
                outs[0][b * piece : (b + 1) * piece, at] = total
        return carry

    lax.fori_loop(0, width // part, down, 0)


def expert(place, ids, blocks, first, w_first, w_second, sums, groups, relations, last):
    count = len(blocks)
    slots, width = blocks[0].shape
    inner = w_first.shape[1]
    rows = count * slots
    nodes = groups * relations * NODE_DEV
    if last:
        shapes = [jax.ShapeDtypeStruct((nodes // 8, width), jnp.bfloat16)] * 8
    else:
        shapes = [jax.ShapeDtypeStruct((nodes, width), jnp.float32)]
    args = [place, ids, *blocks, w_first, w_second] + ([] if sums is None else [sums])
    return pl.pallas_call(
        functools.partial(
            expert_kernel, first, count, slots, groups, relations, sums is not None, last
        ),
        out_shape=shapes,
        in_specs=[SM] + [VM] * (len(args) - 1),
        out_specs=[VM] * len(shapes),
        scratch_shapes=[
            pltpu.VMEM((rows, width), jnp.bfloat16),
            pltpu.VMEM((rows, inner), jnp.bfloat16),
            pltpu.VMEM((1, rows), jnp.int32),
        ],
        compiler_params=pltpu.CompilerParams(vmem_limit_bytes=VMEM_BYTES),
        cost_estimate=pl.CostEstimate(
            flops=4 * rows * width * inner + 2 * nodes * rows * width,
            bytes_accessed=4 * width * inner + 2 * rows * width + 4 * nodes * width,
            transcendentals=rows * inner,
        ),
        name="expert",
    )(*args)


def local(edge_feats, gain, w_in, w_out, rel_type, dst_node):
    rows = edge_feats.shape[1]
    relations = lax.axis_size("rel")
    groups = lax.axis_size("dom")
    slots = 2 * rows // relations
    half = relations // 2
    mine = lax.axis_index("rel")
    place = jnp.stack([mine, (lax.axis_index("dom") * relations + mine) * NODE_DEV]).astype(jnp.int32)
    blocks, ids = pack(
        place, rel_type.reshape(1, rows), dst_node, edge_feats[0], gain[None, :], relations, slots
    )
    ids = lax.all_gather(ids, "rel")

    def swap(value, d):
        return lax.ppermute(value, "rel", [(i, i ^ d) for i in range(relations)])

    order = list(range(half, relations)) + list(range(1, half))
    held = {0: blocks[0]}
    for d in order:
        held[d] = swap(blocks[d], d)
    cuts = [0, half, half + relations // 4, relations]
    sums = None
    for k in range(3):
        sums = expert(
            place, ids, [held[d] for d in range(cuts[k], cuts[k + 1])], cuts[k], w_in[0], w_out[0],
            None if sums is None else sums[0], groups, relations, k == 2,
        )

    def move(value, dom_bits, rel_bits):
        pairs = [
            (r * groups + g, (r ^ rel_bits) * groups + (g ^ dom_bits))
            for g in range(groups) for r in range(relations)
        ]
        return lax.ppermute(value, ("rel", "dom"), pairs)

    f32, bf16 = jnp.float32, jnp.bfloat16
    sums = [
        sums[b].astype(f32) + move(sums[4 + b], 1, 0).astype(f32) for b in range(4)
    ]
    total = sums[0]
    for b in (1, 2, 3):
        total = total + move(sums[b].astype(bf16), 2 * (b // 2), b % 2).astype(f32)
    total = total.reshape(half, NODE_DEV, -1)
    state = total[0]
    for z in range(1, half):
        state = state + move(total[z].astype(bf16), 0, 2 * z).astype(f32)
    return (state * (1.0 / math.sqrt(rows / NODE_DEV)))[None]


def solution(mesh):
    in_specs = (
        P("dom", "rel", None),
        P(),
        P("rel", None, None),
        P("rel", None, None),
        P("dom", "rel", None),
        P("dom", "rel"),
    )
    out_specs = P("dom", "rel", None)
    return jax.shard_map(local, mesh=mesh, in_specs=in_specs, out_specs=out_specs, check_vma=False)
```

time: 280 us -> 129 us (0.46)
  blocking collectives: 118 us -> 44.7 us
  waiting for transfers between devices: 67.4 us -> 18.5 us
  Pallas kernels: 0 us -> 37.5 us
  matrix products: 33.4 us -> 0 us
  local copies, waits for them, and re-layouts: 38.8 us -> 7.15 us
  starting transfers between devices: 0.01 us -> 20.1 us
  between operations: 13.5 us -> 0.11 us
  other arithmetic: 8.06 us -> 1.19 us
    all_to_all x3 -> x0, blocking collectives: 118 us -> none  [the longest x1 55.3 us: local(): lax.all_to_all(outgoing, 'rel', split_axis=0, concat_axis=0, tiled=True)]
    reduce_scatter x1 -> x0, waiting for transfers between devices: 67.4 us -> none  [local(): lax.psum_scatter(partial_value.reshape(groups, relations * nodes_dev, wid...]
    all_gather x0 -> x1, blocking collectives: none -> 44.7 us  [local(): ids = lax.all_gather(ids, 'rel')]
    pallas_call x0 -> x4, Pallas kernels: none -> 37.5 us  [the longest x3 34.6 us: expert(): pl.pallas_call(functools.partial(expert_kernel, first, count, slots, grou...]
    dot_general x3 -> x0, matrix products: 33.4 us -> none  [the longest x1 22 us: expert_mlp(): jnp.einsum('rnh,hd->rnd', hidden, w_second, preferred_element_type=jnp.fl...]
    scatter x1 -> x0, local copies, waits for them, and re-layouts: 33.1 us -> none  [local(): jnp.zeros((relations, slots, width), jnp.bfloat16).at[kinds, rank]]
    ppermute x0 -> x17, starting transfers between devices: none -> 20.1 us  [the longest x7 11.8 us: swap(): return lax.ppermute(value, 'rel', [(i, i ^ d) for i in range(relations)])]
    ppermute x0 -> x17, waiting for transfers between devices: none -> 18.5 us  [the longest x10 17.3 us: move(): return lax.ppermute(value, ('rel', 'dom'), pairs)]
  transfers between devices with their start and end apart: 1 -> 17, of which waited for: 1 -> 8; matrix products, arithmetic and copies ran while one was open for 0% -> 0% of each run, Pallas kernels for 0% -> 19%
where the time goes in v1:
time: 129 us
  blocking collectives  44.7 us (35%)
  Pallas kernels  37.5 us (29%)
  starting transfers between devices  20.1 us (16%)
  waiting for transfers between devices  18.5 us (14%)
  local copies, waits for them, and re-layouts  7.15 us (6%)
    all_gather x1, blocking collectives, local(): ids = lax.all_gather(ids, 'rel')  44.7 us
    pallas_call x3, Pallas kernels, expert(): pl.pallas_call(functools.partial(expert_kernel, first, count, slots, grou...  34.6 us
    ppermute x10, waiting for transfers between devices, move(): return lax.ppermute(value, ('rel', 'dom'), pairs)  17.3 us
    ppermute x7, starting transfers between devices, swap(): return lax.ppermute(value, 'rel', [(i, i ^ d) for i in range(relations)])  11.8 us
    ppermute x10, starting transfers between devices, move(): return lax.ppermute(value, ('rel', 'dom'), pairs)  8.31 us
    unnamed x12, local copies, waits for them, and re-layouts  7.13 us
    pallas_call x1, Pallas kernels, pack(): pl.pallas_call(functools.partial(pack_kernel, relations, slots), out_shap...  2.93 us
  transfers between devices with their start and end apart: 17, of which 8 were waited for; matrix products, arithmetic and copies ran while one was open for 0% of the time, Pallas kernels for 19%

profile of v1, /device:TPU:0, one launch (start us, length us, event | category | flops | bytes accessed | tf_op | source)
XLA Modules:
  0.0 129.2 jit_solution(16409774637743171827)
XLA Ops:
  0.1 1.2 copy-done.2
  3.4 2.9 %pack.1 = (bf16[128,1024]{1,0:T(8,128)(2,1)S(1)}, bf16[128,1024]{1,0:T(8,128)(2,1)S(1)}, bf16[128,1024]{1,0:T(8,128)(2,1)S(1)}, bf16[128,1024]{1,0:T(8,128)(2,1)...) custom-call(s32[2]{0:T(128)S(1)} %pad_add_fusion.place_ref, ...), custom_call_target="tpu_custom_call" | custom-call | flops 1073741824 | bytes 4194304 | tf_op jit(solution)/shard_map/pack/pallas_call | solution.py:60
  6.3 3.0 %collective-permute-start.4 = (bf16[128,1024]{1,0:T(8,128)(2,1)S(1)}, bf16[128,1024]{1,0:T(8,128)(2,1)S(1)}, u32[]{:S(2)}, u32[]{:S(2)}) collective-permute-start(bf16[128,1024]{1,0:T(8,128)(2,1)S(1)} %get-tuple-element.28), channel_id=1, source_target_pairs={{0,4},{4,0},{8,12},{12,8},{16,20},{20,16},{24,28},{28,24},{1,5},{5... | collective-permute-start | bytes 786440 | tf_op jit(solution)/shard_map/ppermute | solution.py:178
  9.3 1.6 %collective-permute-start.5 = (bf16[128,1024]{1,0:T(8,128)(2,1)S(1)}, bf16[128,1024]{1,0:T(8,128)(2,1)S(1)}, u32[]{:S(2)}, u32[]{:S(2)}) collective-permute-start(bf16[128,1024]{1,0:T(8,128)(2,1)S(1)} %get-tuple-element.29), channel_id=1, source_target_pairs={{0,8},{4,12},{8,0},{12,4},{16,24},{20,28},{24,16},{28,20},{1,9},{5... | collective-permute-start | bytes 786440 | tf_op jit(solution)/shard_map/ppermute | solution.py:178
  10.9 4.0 %collective-permute-start = (bf16[128,1024]{1,0:T(8,128)(2,1)S(1)}, bf16[128,1024]{1,0:T(8,128)(2,1)S(1)}, u32[]{:S(2)}, u32[]{:S(2)}) collective-permute-start(bf16[128,1024]{1,0:T(8,128)(2,1)S(1)} %get-tuple-element.23), channel_id=1, source_target_pairs={{0,24},{4,28},{8,16},{12,20},{16,8},{20,12},{24,0},{28,4},{1,25},{... | collective-permute-start | bytes 786440 | tf_op jit(solution)/shard_map/ppermute | solution.py:178
  14.9 1.2 collective-permute-start.1
  16.1 44.7 %all-gather = s32[64,128]{1,0:T(8,128)S(1)} all-gather(s32[8,128]{1,0:T(8,128)S(1)} %get-tuple-element.22), channel_id=2, replica_groups=mesh['rel'=8,'dom'=4] {'rel'}, dimensions={0}, use_global_device_ids=true | all-gather | bytes 36864 | tf_op jit(solution)/shard_map/all_gather | solution.py:175
  60.7 2.0 %collective-permute-start.3 = (bf16[128,1024]{1,0:T(8,128)(2,1)S(1)}, bf16[128,1024]{1,0:T(8,128)(2,1)S(1)}, u32[]{:S(2)}, u32[]{:S(2)}) collective-permute-start(bf16[128,1024]{1,0:T(8,128)(2,1)S(1)} %get-tuple-element.26), channel_id=1, source_target_pairs={{0,20},{4,16},{8,28},{12,24},{16,4},{20,0},{24,12},{28,8},{1,21},{... | collective-permute-start | bytes 786440 | tf_op jit(solution)/shard_map/ppermute | solution.py:178
  62.7 13.3 %expert.3.refs_4_ = f32[1024,1024]{1,0:T(8,128)S(1)} custom-call(s32[2]{0:T(128)S(1)} %pad_add_fusion.place_ref, s32[8,8,128]{2,1,0:T(8,128)S(1)} %bitcast.10, bf16[128,1024]{1,0:T(8,128)(2,1)S(1)} %get-tuple-element.27.refs_0_, bf16[128,1024]{1,0:T(8,128)(2,1)S(1)} %collective-permute-done.4.refs_1_, bf16[128,1024]{1,0:T(8,128)(2,1)S(1)} %collective-permute-done.5.refs_2_, ...), custom_call_target="tpu_custom_call" | custom-call | flops 5368709120 | bytes 13631488 | tf_op jit(solution)/shard_map/expert/pallas_call | solution.py:142
  76.0 1.9 %copy-done.1 = f32[1024,1024]{1,0:T(8,128)} copy-done((f32[1024,1024]{1,0:T(8,128)}, f32[1024,1024]{1,0:T(8,128)S(1)}, u32[]{:S(2)}) %copy-start.1) | copy-done | bytes 4194328
  77.9 1.2 collective-permute-done.3.refs_1_
  79.1 10.7 %expert.4.refs_4_ = f32[1024,1024]{1,0:T(8,128)S(1)} custom-call(s32[2]{0:T(128)S(1)} %pad_add_fusion.place_ref, s32[8,8,128]{2,1,0:T(8,128)S(1)} %bitcast.11, bf16[128,1024]{1,0:T(8,128)(2,1)S(1)} %collective-permute-done.2.refs_0_, bf16[128,1024]{1,0:T(8,128)(2,1)S(1)} %collective-permute-done.3.refs_1_, bf16[1024,2048]{1,0:T(8,128)(2,1)} %bitcast.17, ...), custom_call_target="tpu_custom_call" | custom-call | flops 2684354560 | bytes 13107200 | tf_op jit(solution)/shard_map/expert/pallas_call | solution.py:142
  89.8 1.9 %copy-done = f32[1024,1024]{1,0:T(8,128)} copy-done((f32[1024,1024]{1,0:T(8,128)}, f32[1024,1024]{1,0:T(8,128)S(1)}, u32[]{:S(2)}) %copy-start) | copy-done | bytes 4194328
  91.7 10.7 %expert.5 = (bf16[128,1024]{1,0:T(8,128)(2,1)S(1)}, bf16[128,1024]{1,0:T(8,128)(2,1)S(1)}, bf16[128,1024]{1,0:T(8,128)(2,1)S(1)}, bf16[128,1024]{1,0:T(8,128)(2,...) custom-call(s32[2]{0:T(128)S(1)} %pad_add_fusion.place_ref, ...), custom_call_target="tpu_custom_call" | custom-call | flops 2684354560 | bytes 13107200 | tf_op jit(solution)/shard_map/expert/pallas_call | solution.py:142
  104.1 1.3 %collective-permute-start.9 = (bf16[128,1024]{1,0:T(8,128)(2,1)S(1)}, bf16[128,1024]{1,0:T(8,128)(2,1)S(1)}, u32[]{:S(2)}, u32[]{:S(2)}) collective-permute-start(bf16[128,1024]{1,0:T(8,128)(2,1)S(1)} %add_convert_fusion.2), channel_id=1, source_target_pairs={{0,4},{4,0},{8,12},{12,8},{16,20},{20,16},{24,28},{28,24},{1,5},{5... | collective-permute-start | bytes 786440 | tf_op jit(solution)/shard_map/ppermute | solution.py:197
  105.5 1.6 %collective-permute-start.11 = (bf16[128,1024]{1,0:T(8,128)(2,1)S(1)}, bf16[128,1024]{1,0:T(8,128)(2,1)S(1)}, u32[]{:S(2)}, u32[]{:S(2)}) collective-permute-start(bf16[128,1024]{1,0:T(8,128)(2,1)S(1)} %add_convert_fusion.1), channel_id=1, source_target_pairs={{0,2},{4,6},{8,10},{12,14},{16,18},{20,22},{24,26},{28,30},{1,3},{... | collective-permute-start | bytes 786440 | tf_op jit(solution)/shard_map/ppermute | solution.py:197
  107.9 4.6 %collective-permute-done.9 = bf16[128,1024]{1,0:T(8,128)(2,1)S(1)} collective-permute-done((bf16[128,1024]{1,0:T(8,128)(2,1)S(1)}, bf16[128,1024]{1,0:T(8,128)(2,1)S(1)}, u32[]{:S(2)}, u32[]{:S(2)}) %collective-permute-start.9) | collective-permute-done | bytes 262176 | tf_op jit(solution)/shard_map/ppermute | solution.py:197
  112.5 2.2 %collective-permute-done.11 = bf16[128,1024]{1,0:T(8,128)(2,1)S(1)} collective-permute-done((bf16[128,1024]{1,0:T(8,128)(2,1)S(1)}, bf16[128,1024]{1,0:T(8,128)(2,1)S(1)}, u32[]{:S(2)}, u32[]{:S(2)}) %collective-permute-start.11) | collective-permute-done | bytes 262176 | tf_op jit(solution)/shard_map/ppermute | solution.py:197
  114.7 4.7 %collective-permute-done.13 = bf16[128,1024]{1,0:T(8,128)(2,1)S(1)} collective-permute-done((bf16[128,1024]{1,0:T(8,128)(2,1)S(1)}, bf16[128,1024]{1,0:T(8,128)(2,1)S(1)}, u32[]{:S(2)}, u32[]{:S(2)}) %collective-permute-start.13) | collective-permute-done | bytes 262176 | tf_op jit(solution)/shard_map/ppermute | solution.py:197
  119.7 2.3 %collective-permute-start.16 = (bf16[32,1024]{1,0:T(8,128)(2,1)S(1)}, bf16[32,1024]{1,0:T(8,128)(2,1)S(1)}, u32[]{:S(2)}, u32[]{:S(2)}) collective-permute-start(bf16[32,1024]{1,0:T(8,128)(2,1)S(1)} %get-tuple-element.42), channel_id=1, source_target_pairs={{0,24},{4,28},{8,16},{12,20},{16,8},{20,12},{24,0},{28,4},{1,25},{... | collective-permute-start | bytes 196616 | tf_op jit(solution)/shard_map/ppermute | solution.py:197
  122.0 1.2 collective-permute-start.15
  123.2 1.7 %collective-permute-done.14 = bf16[32,1024]{1,0:T(8,128)(2,1)S(1)} collective-permute-done((bf16[32,1024]{1,0:T(8,128)(2,1)S(1)}, bf16[32,1024]{1,0:T(8,128)(2,1)S(1)}, u32[]{:S(2)}, u32[]{:S(2)}) %collective-permute-start.14) | collective-permute-done | bytes 65568 | tf_op jit(solution)/shard_map/ppermute | solution.py:197
  124.9 1.1 collective-permute-done.16
  126.0 2.5 %collective-permute-done.15 = bf16[32,1024]{1,0:T(8,128)(2,1)S(1)} collective-permute-done((bf16[32,1024]{1,0:T(8,128)(2,1)S(1)}, bf16[32,1024]{1,0:T(8,128)(2,1)S(1)}, u32[]{:S(2)}, u32[]{:S(2)}) %collective-permute-start.15) | collective-permute-done | bytes 65568 | tf_op jit(solution)/shard_map/ppermute | solution.py:197
  (34 shorter events, 5.8 us)
Async XLA Ops:
  0.1 1.2 copy-start.2
  1.3 0.7 copy-start.3
  2.0 0.7 copy-start.4
  2.7 0.7 copy-start.5
  6.3 54.4 %collective-permute-start.4 = (bf16[128,1024]{1,0:T(8,128)(2,1)S(1)}, bf16[128,1024]{1,0:T(8,128)(2,1)S(1)}, u32[]{:S(2)}, u32[]{:S(2)}) collective-permute-start(bf16[128,1024]{1,0:T(8,128)(2,1)S(1)} %get-tuple-element.28), channel_id=1, source_target_pairs={{0,4},{4,0},{8,12},{12,8},{16,20},{20,16},{24,28},{28,24},{1,5},{5... | collective-permute-start | bytes 786440 | tf_op jit(solution)/shard_map/ppermute | solution.py:178
  9.3 51.4 %collective-permute-start.5 = (bf16[128,1024]{1,0:T(8,128)(2,1)S(1)}, bf16[128,1024]{1,0:T(8,128)(2,1)S(1)}, u32[]{:S(2)}, u32[]{:S(2)}) collective-permute-start(bf16[128,1024]{1,0:T(8,128)(2,1)S(1)} %get-tuple-element.29), channel_id=1, source_target_pairs={{0,8},{4,12},{8,0},{12,4},{16,24},{20,28},{24,16},{28,20},{1,9},{5... | collective-permute-start | bytes 786440 | tf_op jit(solution)/shard_map/ppermute | solution.py:178
  10.9 51.8 %collective-permute-start.6 = (bf16[128,1024]{1,0:T(8,128)(2,1)S(1)}, bf16[128,1024]{1,0:T(8,128)(2,1)S(1)}, u32[]{:S(2)}, u32[]{:S(2)}) collective-permute-start(bf16[128,1024]{1,0:T(8,128)(2,1)S(1)} %get-tuple-element.30), channel_id=1, source_target_pairs={{0,12},{4,8},{8,4},{12,0},{16,28},{20,24},{24,20},{28,16},{1,13},{... | collective-permute-start | bytes 786440 | tf_op jit(solution)/shard_map/ppermute | solution.py:178
  10.9 80.8 %collective-permute-start = (bf16[128,1024]{1,0:T(8,128)(2,1)S(1)}, bf16[128,1024]{1,0:T(8,128)(2,1)S(1)}, u32[]{:S(2)}, u32[]{:S(2)}) collective-permute-start(bf16[128,1024]{1,0:T(8,128)(2,1)S(1)} %get-tuple-element.23), channel_id=1, source_target_pairs={{0,24},{4,28},{8,16},{12,20},{16,8},{20,12},{24,0},{28,4},{1,25},{... | collective-permute-start | bytes 786440 | tf_op jit(solution)/shard_map/ppermute | solution.py:178
  14.9 76.8 %collective-permute-start.1 = (bf16[128,1024]{1,0:T(8,128)(2,1)S(1)}, bf16[128,1024]{1,0:T(8,128)(2,1)S(1)}, u32[]{:S(2)}, u32[]{:S(2)}) collective-permute-start(bf16[128,1024]{1,0:T(8,128)(2,1)S(1)} %get-tuple-element.24), channel_id=1, source_target_pairs={{0,28},{4,24},{8,20},{12,16},{16,12},{20,8},{24,4},{28,0},{1,29},{... | collective-permute-start | bytes 786440 | tf_op jit(solution)/shard_map/ppermute | solution.py:178
  60.7 17.2 %collective-permute-start.2 = (bf16[128,1024]{1,0:T(8,128)(2,1)S(1)}, bf16[128,1024]{1,0:T(8,128)(2,1)S(1)}, u32[]{:S(2)}, u32[]{:S(2)}) collective-permute-start(bf16[128,1024]{1,0:T(8,128)(2,1)S(1)} %get-tuple-element.25), channel_id=1, source_target_pairs={{0,16},{4,20},{8,24},{12,28},{16,0},{20,4},{24,8},{28,12},{1,17},{... | collective-permute-start | bytes 786440 | tf_op jit(solution)/shard_map/ppermute | solution.py:178
  60.7 18.4 %collective-permute-start.3 = (bf16[128,1024]{1,0:T(8,128)(2,1)S(1)}, bf16[128,1024]{1,0:T(8,128)(2,1)S(1)}, u32[]{:S(2)}, u32[]{:S(2)}) collective-permute-start(bf16[128,1024]{1,0:T(8,128)(2,1)S(1)} %get-tuple-element.26), channel_id=1, source_target_pairs={{0,20},{4,16},{8,28},{12,24},{16,4},{20,0},{24,12},{28,8},{1,21},{... | collective-permute-start | bytes 786440 | tf_op jit(solution)/shard_map/ppermute | solution.py:178
  76.0 1.9 %copy-start.1 = (f32[1024,1024]{1,0:T(8,128)}, f32[1024,1024]{1,0:T(8,128)S(1)}, u32[]{:S(2)}) copy-start(f32[1024,1024]{1,0:T(8,128)S(1)} %expert.3.refs_4_) | copy-start | bytes 12582916
  89.8 1.9 %copy-start = (f32[1024,1024]{1,0:T(8,128)}, f32[1024,1024]{1,0:T(8,128)S(1)}, u32[]{:S(2)}) copy-start(f32[1024,1024]{1,0:T(8,128)S(1)} %expert.4.refs_4_) | copy-start | bytes 12582916
  102.4 1.6 %collective-permute-start.8 = (bf16[128,1024]{1,0:T(8,128)(2,1)S(1)}, bf16[128,1024]{1,0:T(8,128)(2,1)S(1)}, u32[]{:S(2)}, u32[]{:S(2)}) collective-permute-start(bf16[128,1024]{1,0:T(8,128)(2,1)S(1)} %get-tuple-element.34), channel_id=1, source_target_pairs={{0,1},{4,5},{8,9},{12,13},{16,17},{20,21},{24,25},{28,29},{1,0},{5... | collective-permute-start | bytes 786440 | tf_op jit(solution)/shard_map/ppermute | solution.py:197
  102.5 2.9 %collective-permute-start.10 = (bf16[128,1024]{1,0:T(8,128)(2,1)S(1)}, bf16[128,1024]{1,0:T(8,128)(2,1)S(1)}, u32[]{:S(2)}, u32[]{:S(2)}) collective-permute-start(bf16[128,1024]{1,0:T(8,128)(2,1)S(1)} %get-tuple-element.36), channel_id=1, source_target_pairs={{0,1},{4,5},{8,9},{12,13},{16,17},{20,21},{24,25},{28,29},{1,0},{5... | collective-permute-start | bytes 786440 | tf_op jit(solution)/shard_map/ppermute | solution.py:197
  103.0 4.9 %collective-permute-start.7 = (bf16[128,1024]{1,0:T(8,128)(2,1)S(1)}, bf16[128,1024]{1,0:T(8,128)(2,1)S(1)}, u32[]{:S(2)}, u32[]{:S(2)}) collective-permute-start(bf16[128,1024]{1,0:T(8,128)(2,1)S(1)} %get-tuple-element.32), channel_id=1, source_target_pairs={{0,1},{4,5},{8,9},{12,13},{16,17},{20,21},{24,25},{28,29},{1,0},{5... | collective-permute-start | bytes 786440 | tf_op jit(solution)/shard_map/ppermute | solution.py:197
  103.0 4.0 %collective-permute-start.12 = (bf16[128,1024]{1,0:T(8,128)(2,1)S(1)}, bf16[128,1024]{1,0:T(8,128)(2,1)S(1)}, u32[]{:S(2)}, u32[]{:S(2)}) collective-permute-start(bf16[128,1024]{1,0:T(8,128)(2,1)S(1)} %get-tuple-element.38), channel_id=1, source_target_pairs={{0,1},{4,5},{8,9},{12,13},{16,17},{20,21},{24,25},{28,29},{1,0},{5... | collective-permute-start | bytes 786440 | tf_op jit(solution)/shard_map/ppermute | solution.py:197
  104.1 8.4 %collective-permute-start.9 = (bf16[128,1024]{1,0:T(8,128)(2,1)S(1)}, bf16[128,1024]{1,0:T(8,128)(2,1)S(1)}, u32[]{:S(2)}, u32[]{:S(2)}) collective-permute-start(bf16[128,1024]{1,0:T(8,128)(2,1)S(1)} %add_convert_fusion.2), channel_id=1, source_target_pairs={{0,4},{4,0},{8,12},{12,8},{16,20},{20,16},{24,28},{28,24},{1,5},{5... | collective-permute-start | bytes 786440 | tf_op jit(solution)/shard_map/ppermute | solution.py:197
  105.5 9.3 %collective-permute-start.11 = (bf16[128,1024]{1,0:T(8,128)(2,1)S(1)}, bf16[128,1024]{1,0:T(8,128)(2,1)S(1)}, u32[]{:S(2)}, u32[]{:S(2)}) collective-permute-start(bf16[128,1024]{1,0:T(8,128)(2,1)S(1)} %add_convert_fusion.1), channel_id=1, source_target_pairs={{0,2},{4,6},{8,10},{12,14},{16,18},{20,22},{24,26},{28,30},{1,3},{... | collective-permute-start | bytes 786440 | tf_op jit(solution)/shard_map/ppermute | solution.py:197
  107.1 12.3 %collective-permute-start.13 = (bf16[128,1024]{1,0:T(8,128)(2,1)S(1)}, bf16[128,1024]{1,0:T(8,128)(2,1)S(1)}, u32[]{:S(2)}, u32[]{:S(2)}) collective-permute-start(bf16[128,1024]{1,0:T(8,128)(2,1)S(1)} %add_convert_fusion), channel_id=1, source_target_pairs={{0,6},{4,2},{8,14},{12,10},{16,22},{20,18},{24,30},{28,26},{1,7},{... | collective-permute-start | bytes 786440 | tf_op jit(solution)/shard_map/ppermute | solution.py:197
  119.7 5.3 %collective-permute-start.14 = (bf16[32,1024]{1,0:T(8,128)(2,1)S(1)}, bf16[32,1024]{1,0:T(8,128)(2,1)S(1)}, u32[]{:S(2)}, u32[]{:S(2)}) collective-permute-start(bf16[32,1024]{1,0:T(8,128)(2,1)S(1)} %get-tuple-element.41), channel_id=1, source_target_pairs={{0,8},{4,12},{8,0},{12,4},{16,24},{20,28},{24,16},{28,20},{1,9},{5... | collective-permute-start | bytes 196616 | tf_op jit(solution)/shard_map/ppermute | solution.py:197
  119.7 6.3 %collective-permute-start.16 = (bf16[32,1024]{1,0:T(8,128)(2,1)S(1)}, bf16[32,1024]{1,0:T(8,128)(2,1)S(1)}, u32[]{:S(2)}, u32[]{:S(2)}) collective-permute-start(bf16[32,1024]{1,0:T(8,128)(2,1)S(1)} %get-tuple-element.42), channel_id=1, source_target_pairs={{0,24},{4,28},{8,16},{12,20},{16,8},{20,12},{24,0},{28,4},{1,25},{... | collective-permute-start | bytes 196616 | tf_op jit(solution)/shard_map/ppermute | solution.py:197
  122.0 6.5 %collective-permute-start.15 = (bf16[32,1024]{1,0:T(8,128)(2,1)S(1)}, bf16[32,1024]{1,0:T(8,128)(2,1)S(1)}, u32[]{:S(2)}, u32[]{:S(2)}) collective-permute-start(bf16[32,1024]{1,0:T(8,128)(2,1)S(1)} %get-tuple-element.43), channel_id=1, source_target_pairs={{0,16},{4,20},{8,24},{12,28},{16,0},{20,4},{24,8},{28,12},{1,17},{... | collective-permute-start | bytes 196616 | tf_op jit(solution)/shard_map/ppermute | solution.py:197

commit v2 on v0

v2 whole, which is shorter than its diff:
```python
import functools
import math

import jax
import jax.numpy as jnp
from jax import lax
from jax.experimental import pallas as pl
from jax.experimental.pallas import tpu as pltpu
from jax.sharding import PartitionSpec as P

NODE_DEV = 32
LANES = 128
EXTRA = 16
CUTS = (0.0, 1.0)
MIB = 1024 * 1024
VM = pl.BlockSpec(memory_space=pltpu.VMEM)
SM = pl.BlockSpec(memory_space=pltpu.SMEM)
HB = pl.BlockSpec(memory_space=pltpu.HBM)
F32 = jnp.float32
BF16 = jnp.bfloat16
I32 = jnp.int32


def write_blocks(first, slots, slot, coded, normed, blocks):
    rows, width = normed.shape
    for i, block in enumerate(blocks):
        at = lax.broadcasted_iota(I32, (slots, rows), 0) + (first + i) * slots
        pick = (slot == at).astype(BF16)
        picked = jnp.dot(pick, normed, preferred_element_type=F32).astype(BF16)
        for c in range(width // LANES):
            block[c * slots : (c + 1) * slots, :] = picked[:, c * LANES : (c + 1) * LANES]
        ids = lax.dot_general(coded, pick, (((1,), (1,)), ((), ())), preferred_element_type=F32)
        block[width // LANES * slots :, :slots] = ids.astype(BF16)


def pack_kernel(relations, slots, first, count, place_ref, kinds_hbm, dest_hbm, feats_hbm, gain_hbm, *refs):
    blocks, (normed_ref, slot_ref, coded_ref), scratch = (
        refs[:count], refs[count:-6], refs[-6:],
    )
    kinds_ref, dest_ref, gain_ref, feats_ref, sems, feat_sems = scratch
    rows, width = feats_ref.shape
    part = rows // 4
    small = [
        pltpu.make_async_copy(kinds_hbm, kinds_ref, sems.at[0]),
        pltpu.make_async_copy(dest_hbm, dest_ref, sems.at[1]),
        pltpu.make_async_copy(gain_hbm, gain_ref, sems.at[2]),
    ]
    large = [
        pltpu.make_async_copy(
            feats_hbm.at[pl.ds(i * part, part), :], feats_ref.at[pl.ds(i * part, part), :], feat_sems.at[i]
        )
        for i in range(4)
    ]
    for copy in small + large:
        copy.start()
    before = (
        lax.broadcasted_iota(I32, (rows, rows), 0) < lax.broadcasted_iota(I32, (rows, rows), 1)
    ).astype(BF16)
    for copy in small:
        copy.wait()
    offset = kinds_ref[...] ^ place_ref[0]
    marks = offset == lax.broadcasted_iota(I32, (max(relations, 16), rows), 0)
    count = jnp.dot(marks.astype(BF16), before, preferred_element_type=F32)
    rank = jnp.sum(jnp.where(marks, count, 0.0), axis=0, keepdims=True).astype(I32)
    slot = offset * slots + rank
    slot_ref[...] = slot
    dest = dest_ref[...]
    line = lax.broadcasted_iota(I32, (EXTRA, rows), 0)
    coded = jnp.where(
        line == 0, dest // NODE_DEV, jnp.where(line == 1, dest % NODE_DEV, jnp.where(line == 2, 1, 0))
    ).astype(BF16)
    coded_ref[...] = coded
    gain = gain_ref[...]
    for i in range(4):
        large[i].wait()
        at = slice(i * part, (i + 1) * part)
        feats = feats_ref[at, :].astype(F32)
        scale = lax.rsqrt(jnp.mean(feats * feats, axis=1, keepdims=True) + 1e-06)
        normed_ref[at, :] = (feats * scale * gain).astype(BF16)
    write_blocks(first, slots, slot, coded, normed_ref[...], blocks)


def pack_more_kernel(slots, first, count, normed_ref, slot_ref, coded_ref, *refs):
    write_blocks(first, slots, slot_ref[...], coded_ref[...], normed_ref[...], refs[-count:])


def pack_more(kept, first, count, slots, after=()):
    rows, width = kept[0].shape
    block = jax.ShapeDtypeStruct((width // LANES * slots + EXTRA, LANES), BF16)
    return pl.pallas_call(
        functools.partial(pack_more_kernel, slots, first, count),
        out_shape=[block] * count,
        in_specs=[VM] * 3 + [HB] * len(after),
        out_specs=[VM] * count,
        compiler_params=pltpu.CompilerParams(vmem_limit_bytes=16 * MIB),
        cost_estimate=pl.CostEstimate(flops=1, bytes_accessed=1, transcendentals=0),
        name="pack_more",
    )(*kept, *after)


def pack(place, kinds, dest, feats, gain, relations, slots, first, count):
    rows, width = feats.shape
    block = jax.ShapeDtypeStruct((width // LANES * slots + EXTRA, LANES), BF16)
    shapes = [block] * count + [
        jax.ShapeDtypeStruct((rows, width), BF16),
        jax.ShapeDtypeStruct((1, rows), I32),
        jax.ShapeDtypeStruct((EXTRA, rows), BF16),
    ]
    outs = pl.pallas_call(
        functools.partial(pack_kernel, relations, slots, first, count),
        out_shape=shapes,
        in_specs=[SM, HB, HB, HB, HB],
        out_specs=[VM] * len(shapes),
        scratch_shapes=[
            pltpu.VMEM((1, rows), I32),
            pltpu.VMEM((1, rows), I32),
            pltpu.VMEM((1, width), F32),
            pltpu.VMEM((rows, width), BF16),
            pltpu.SemaphoreType.DMA((3,)),
            pltpu.SemaphoreType.DMA((4,)),
        ],
        compiler_params=pltpu.CompilerParams(vmem_limit_bytes=16 * MIB),
        cost_estimate=pl.CostEstimate(flops=1, bytes_accessed=1, transcendentals=0),
        name="pack_far",
    )(place, *[pltpu.with_memory_space_constraint(a, pltpu.HBM) for a in (kinds, dest, feats, gain)])
    return outs[:count], outs[count:]


def gelu(x):
    return 0.5 * x * (1.0 + lax.erf(x * math.sqrt(0.5)))


def load_block(block_ref, x_ref, row, base, groups, relations):
    width = x_ref.shape[1]
    slots = (block_ref.shape[0] - EXTRA) * LANES // width
    for c in range(width // LANES):
        x_ref[row : row + slots, c * LANES : (c + 1) * LANES] = block_ref[c * slots : (c + 1) * slots, :]
    ids = block_ref[width // LANES * slots :, :slots].astype(F32).astype(I32)
    owner = ids[0:1] ^ base
    half = relations // 2
    y, z, g = owner % 2, owner // 2 % half, owner // relations
    at = ((((g % 2) * 2 + g // 2) * 2 + y) * half + z) * NODE_DEV + ids[1:2]
    return jnp.where(ids[2:3] > 0, at, -1)


def up(x_ref, w_first_ref, hidden_ref):
    inner = w_first_ref.shape[1]
    part = 256

    def step(i, carry):
        at = pl.ds(pl.multiple_of(i * part, part), part)
        h = jnp.dot(x_ref[...], w_first_ref[:, at], preferred_element_type=F32)
        hidden_ref[:, at] = gelu(h).astype(BF16)
        return carry

    lax.fori_loop(0, inner // part, step, 0, unroll=8)


def down(hidden_ref, w_second_ref, table_ref, sums_ref, outs, left, right):
    part = 256
    nodes = table_ref.shape[0]
    piece = nodes // len(outs)
    messages = [
        jnp.dot(
            hidden_ref[...], w_second_ref[:, start : min(start + part, right)], preferred_element_type=F32
        ).astype(BF16)
        for start in range(left, right, part)
    ]
    for i, message in enumerate(messages):
        start = left + i * part
        size = message.shape[1]
        total = jnp.dot(table_ref[...], message, preferred_element_type=F32)
        if sums_ref is not None:
            total = total + sums_ref[:, start : start + size]
        for b, out in enumerate(outs):
            out[:, start - left : start - left + size] = total[b * piece : (b + 1) * piece].astype(out.dtype)


def expert_kernel(count, slots, groups, relations, has_sums, right, place_ref, *refs):
    blocks, refs = refs[:count], refs[count:]
    w_first_ref, w_second_ref, refs = refs[0], refs[1], refs[2:]
    sums_ref = None
    if has_sums:
        sums_ref, refs = refs[0], refs[1:]
    outs, (token_ref, hidden_ref, table_ref, x_ref) = refs[:-4], refs[-4:]
    token_ref[...] = jnp.zeros_like(token_ref)
    nodes = table_ref.shape[0]
    for i in range(count):
        line = load_block(blocks[i], x_ref, i * slots, place_ref[1], groups, relations)
        table_ref[:, i * slots : (i + 1) * slots] = (
            line == lax.broadcasted_iota(I32, (nodes, slots), 0)
        ).astype(BF16)
    up(x_ref, w_first_ref, hidden_ref)
    down(hidden_ref, w_second_ref, table_ref, sums_ref, outs, 0, right)


def more_kernel(left, right, hidden_ref, table_ref, w_second_ref, sums_ref, *outs):
    down(hidden_ref, w_second_ref, table_ref, sums_ref, outs, left, right)


def expert(place, blocks, w_first, w_second, sums, groups, relations, edges):
    count = len(blocks)
    width, inner = w_first.shape
    slots = (blocks[0].shape[0] - EXTRA) * LANES // width
    rows = count * slots
    nodes = groups * relations * NODE_DEV
    if edges is None:
        right, shapes = width, [jax.ShapeDtypeStruct((nodes, width), F32)]
    else:
        right, shapes = edges[1], [jax.ShapeDtypeStruct((nodes // 8, edges[1]), BF16)] * 8
    shapes.append(jax.ShapeDtypeStruct((8, LANES), F32))
    kept = [jax.ShapeDtypeStruct((rows, inner), BF16), jax.ShapeDtypeStruct((nodes, rows), BF16)]
    scratch = [pltpu.VMEM(s.shape, s.dtype) for s in kept]
    args = [place, *blocks, w_first, w_second] + ([] if sums is None else [sums])
    keep = edges is not None
    params = pltpu.CompilerParams(vmem_limit_bytes=16 * MIB if relations <= 8 else 48 * MIB)
    outs = pl.pallas_call(
        functools.partial(expert_kernel, count, slots, groups, relations, sums is not None, right),
        out_shape=shapes + kept * keep,
        in_specs=[SM] + [VM] * (len(args) - 1),
        out_specs=[VM] * (len(shapes) + 2 * keep),
        scratch_shapes=scratch * (not keep) + [pltpu.VMEM((rows, width), BF16)],
        compiler_params=params,
        cost_estimate=pl.CostEstimate(flops=1, bytes_accessed=1, transcendentals=0),
        name="expert",
    )(*args)
    if edges is None:
        return outs
    pieces = [outs[:8]]
    for left, right in zip(edges[1:-1], edges[2:]):
        pieces.append(
            pl.pallas_call(
                functools.partial(more_kernel, left, right),
                out_shape=[jax.ShapeDtypeStruct((nodes // 8, right - left), BF16)] * 8,
                in_specs=[VM] * 4,
                out_specs=[VM] * 8,
                compiler_params=params,
                cost_estimate=pl.CostEstimate(flops=1, bytes_accessed=1, transcendentals=0),
                name="expert_more",
            )(outs[9], outs[10], w_second, sums)
        )
    return pieces


def local(edge_feats, gain, w_in, w_out, rel_type, dst_node):
    rows = edge_feats.shape[1]
    width = edge_feats.shape[2]
    relations = lax.axis_size("rel")
    groups = lax.axis_size("dom")
    slots = 2 * rows // relations
    half = relations // 2
    mine = lax.axis_index("rel")
    place = jnp.stack([mine, lax.axis_index("dom") * relations + mine]).astype(I32)
    def move(value, dom_bits, rel_bits):
        pairs = [
            (r * groups + g, (r ^ rel_bits) * groups + (g ^ dom_bits))
            for r in range(relations) for g in range(groups)
        ]
        return lax.ppermute(value, ("rel", "dom"), pairs)

    step = half // 4
    far = [list(range(half + k * step, half + (k + 1) * step)) for k in range(4)]
    first, kept = pack(
        place, rel_type.reshape(1, rows), dst_node, edge_feats[0], gain[None, :], relations, slots, half, 2 * step
    )
    held = {d: move(first[d - half], 0, d) for d in far[0] + far[1]}
    near = pack_more(kept, 0, half, slots)
    held[0] = near[0]
    held.update({d: move(near[d], 0, d) for d in range(1, half)})
    edges = [int(c * width) for c in CUTS]

    def run(turn, sums, last=False):
        blocks = [held[d] for d in turn]
        return expert(place, blocks, w_in[0], w_out[0], sums, groups, relations, edges if last else None)

    sums, token = run([0], None)
    for k in (2, 3):
        late = pack_more(kept, far[k][0], step, slots, [held[far[k - 2][-1]], token])
        held.update({d: move(block, 0, d) for d, block in zip(far[k], late)})
    for turn in (far[0] + far[1], list(range(1, half)), far[2]):
        sums, token = run(turn, sums)
    sums = run(far[3], sums, True)

    states = []
    for piece in sums:
        near = [piece[b].astype(F32) + move(piece[4 + b], 1, 0).astype(F32) for b in range(4)]
        total = near[0]
        for b in (3, 2, 1):
            total = total + move(near[b].astype(BF16), 2 * (b // 2), b % 2).astype(F32)
        total = total.reshape(half, NODE_DEV, -1)
        state = total[0]
        for z in range(half - 1, 0, -1):
            state = state + move(total[z].astype(BF16), 0, 2 * z).astype(F32)
        states.append(state)
    state = jnp.concatenate(states, axis=1)
    return (state * (1.0 / math.sqrt(rows / NODE_DEV)))[None]


def solution(mesh):
    in_specs = (
        P("dom", "rel", None),
        P(),
        P("rel", None, None),
        P("rel", None, None),
        P("dom", "rel", None),
        P("dom", "rel"),
    )
    out_specs = P("dom", "rel", None)
    return jax.shard_map(local, mesh=mesh, in_specs=in_specs, out_specs=out_specs, check_vma=False)
```

time: 280 us -> 86.2 us (0.31)
  blocking collectives: 118 us -> 0 us
  local copies, waits for them, and re-layouts: 38.8 us -> 4.4 us
  matrix products: 33.4 us -> 0 us
  waiting for transfers between devices: 67.4 us -> 34.4 us
  starting transfers between devices: 0.01 us -> 24 us
  Pallas kernels: 0 us -> 21.9 us
  between operations: 13.5 us -> 0.13 us
  other arithmetic: 8.06 us -> 1.19 us
    all_to_all x3 -> x0, blocking collectives: 118 us -> none  [the longest x1 55.3 us: local(): lax.all_to_all(outgoing, 'rel', split_axis=0, concat_axis=0, tiled=True)]
    reduce_scatter x1 -> x0, waiting for transfers between devices: 67.4 us -> none  [local(): lax.psum_scatter(partial_value.reshape(groups, relations * nodes_dev, wid...]
    ppermute x0 -> x17, waiting for transfers between devices: none -> 34.4 us  [move(): return lax.ppermute(value, ('rel', 'dom'), pairs)]
    dot_general x3 -> x0, matrix products: 33.4 us -> none  [the longest x1 22 us: expert_mlp(): jnp.einsum('rnh,hd->rnd', hidden, w_second, preferred_element_type=jnp.fl...]
    scatter x1 -> x0, local copies, waits for them, and re-layouts: 33.1 us -> none  [local(): jnp.zeros((relations, slots, width), jnp.bfloat16).at[kinds, rank]]
    ppermute x0 -> x17, starting transfers between devices: none -> 24 us  [move(): return lax.ppermute(value, ('rel', 'dom'), pairs)]
    pallas_call x0 -> x9, Pallas kernels: none -> 21.9 us  [the longest x5 17.5 us: expert(): pl.pallas_call(functools.partial(expert_kernel, count, slots, groups, rel...]
    gather x1 -> x0, local copies, waits for them, and re-layouts: 5.26 us -> none  [local(): edge_msgs = messages[kinds, rank]]
  transfers between devices with their start and end apart: 1 -> 17, of which waited for: 1 -> 9; matrix products, arithmetic and copies ran while one was open for 0% -> 0% of each run, Pallas kernels for 0% -> 18%
where the time goes in v2:
time: 86.2 us; the launch traced here: 86 us
  waiting for transfers between devices  34.4 us (40%)
  starting transfers between devices  24 us (28%)
  Pallas kernels  21.9 us (25%)
  local copies, waits for them, and re-layouts  4.4 us (5%)
  other arithmetic  1.19 us (1%)
    ppermute x17, waiting for transfers between devices, move(): return lax.ppermute(value, ('rel', 'dom'), pairs)  34.4 us
    ppermute x17, starting transfers between devices, move(): return lax.ppermute(value, ('rel', 'dom'), pairs)  24 us
    pallas_call x5, Pallas kernels, expert(): pl.pallas_call(functools.partial(expert_kernel, count, slots, groups, rel...  17.5 us
    unnamed x8, local copies, waits for them, and re-layouts  4.38 us
    pallas_call x1, Pallas kernels, pack(): pl.pallas_call(functools.partial(pack_kernel, relations, slots, first, co...  2.85 us
  transfers between devices with their start and end apart: 17, of which 9 were waited for; matrix products, arithmetic and copies ran while one was open for 0% of the time, Pallas kernels for 18%

profile of v2, /device:TPU:0, one launch (start us, length us, event | category | flops | bytes accessed | tf_op | source)
XLA Modules:
  0.0 86.0 jit_solution(10392891855576291991)
XLA Ops:
  0.1 2.8 %pack_far.1 = (bf16[1040,128]{1,0:T(8,128)(2,1)S(1)}, bf16[1040,128]{1,0:T(8,128)(2,1)S(1)}, bf16[512,1024]{1,0:T(8,128)(2,1)S(1)}, s32[1,512]{1,0:T(1,128)S(1)}, bf16[16,512]{1,0:T(8,128)(2,1)S(1)}) custom-call(s32[2]{0:T(128)S(1)} %pad_add_fusion.place_ref, s32[1,512]{1,0:T(1,128)} %bitcast.21, s32[1,512]{1,0:T(1,128)} %dest_hbm.1, ...), custom_call_target="tpu_custom_call" | custom-call | flops 1 | bytes 1 | tf_op jit(solution)/shard_map/pack_far/pallas_call | solution.py:109
  2.9 4.1 %collective-permute-start.2 = (bf16[1040,128]{1,0:T(8,128)(2,1)S(1)}, bf16[1040,128]{1,0:T(8,128)(2,1)S(1)}, u32[]{:S(2)}, u32[]{:S(2)}) collective-permute-start(bf16[1040,128]{1,0:T(8,128)(2,1)S(1)} %get-tuple-element.33), channel_id=1, source_target_pairs={{0,16},{1,17},{2,18},{3,19},{4,20},{5,21},{6,22},{7,23},{8,24},{9,... | collective-permute-start | bytes 798728 | tf_op jit(solution)/shard_map/ppermute | solution.py:259
  9.5 1.8 %collective-permute-start.5 = (bf16[1040,128]{1,0:T(8,128)(2,1)S(1)}, bf16[1040,128]{1,0:T(8,128)(2,1)S(1)}, u32[]{:S(2)}, u32[]{:S(2)}) collective-permute-start(bf16[1040,128]{1,0:T(8,128)(2,1)S(1)} %get-tuple-element.35), channel_id=1, source_target_pairs={{0,8},{1,9},{2,10},{3,11},{4,12},{5,13},{6,14},{7,15},{8,0},{9,1},... | collective-permute-start | bytes 798728 | tf_op jit(solution)/shard_map/ppermute | solution.py:259
  12.8 2.2 %copy-done = bf16[1,1024,2048]{2,1,0:T(8,128)(2,1)S(1)} copy-done((bf16[1,1024,2048]{2,1,0:T(8,128)(2,1)S(1)}, bf16[1,1024,2048]{2,1,0:T(8,128)(2,1)}, u32[]{:S(2)}) %copy-start) | copy-done | bytes 4194328
  15.0 2.2 %copy-done.2 = bf16[1,2048,1024]{2,1,0:T(8,128)(2,1)S(1)} copy-done((bf16[1,2048,1024]{2,1,0:T(8,128)(2,1)S(1)}, bf16[1,2048,1024]{2,1,0:T(8,128)(2,1)}, u32[]{:S(2)}) %copy-start.2) | copy-done | bytes 4194328
  17.2 2.5 %expert.5 = (f32[1024,1024]{1,0:T(8,128)S(1)}, f32[8,128]{1,0:T(8,128)S(1)}) custom-call(s32[2]{0:T(128)S(1)} %pad_add_fusion.place_ref, bf16[1040,128]{1,0:T(8,128)(2,1)S(1)} %get-tuple-element.31.refs_0_, bf16[1024,2048]{1,0:T(8,128)(2,1)S(1)} %bitcast.9, bf16[2048,1024]{1,0:T(8,128)(2,1)S(1)} %bitcast.14), custom_call_target="tpu_custom_call" | custom-call | flops 1 | bytes 1 | tf_op jit(solution)/shard_map/expert/pallas_call | solution.py:217
  19.7 6.1 %collective-permute-done.2.refs_0_ = bf16[1040,128]{1,0:T(8,128)(2,1)S(1)} collective-permute-done((bf16[1040,128]{1,0:T(8,128)(2,1)S(1)}, bf16[1040,128]{1,0:T(8,128)(2,1)S(1)}, u32[]{:S(2)}, u32[]{:S(2)}) %collective-permute-start.2) | collective-permute-done | bytes 266272 | tf_op jit(solution)/shard_map/ppermute | solution.py:259
  26.1 2.9 %collective-permute-start.3 = (bf16[1040,128]{1,0:T(8,128)(2,1)S(1)}, bf16[1040,128]{1,0:T(8,128)(2,1)S(1)}, u32[]{:S(2)}, u32[]{:S(2)}) collective-permute-start(bf16[1040,128]{1,0:T(8,128)(2,1)S(1)} %pack_more.5), channel_id=1, source_target_pairs={{0,24},{1,25},{2,26},{3,27},{4,28},{5,29},{6,30},{7,31},{8,16},{9,... | collective-permute-start | bytes 798728 | tf_op jit(solution)/shard_map/ppermute | solution.py:259
  29.0 4.9 %collective-permute-done.refs_0_.refs_1_ = bf16[1040,128]{1,0:T(8,128)(2,1)S(1)} collective-permute-done((bf16[1040,128]{1,0:T(8,128)(2,1)S(1)}, bf16[1040,128]{1,0:T(8,128)(2,1)S(1)}, u32[]{:S(2)}, u32[]{:S(2)}) %collective-permute-start) | collective-permute-done | bytes 266272 | tf_op jit(solution)/shard_map/ppermute | solution.py:259
  34.2 2.2 %collective-permute-start.1 = (bf16[1040,128]{1,0:T(8,128)(2,1)S(1)}, bf16[1040,128]{1,0:T(8,128)(2,1)S(1)}, u32[]{:S(2)}, u32[]{:S(2)}) collective-permute-start(bf16[1040,128]{1,0:T(8,128)(2,1)S(1)} %pack_more.4), channel_id=1, source_target_pairs={{0,28},{1,29},{2,30},{3,31},{4,24},{5,25},{6,26},{7,27},{8,20},{9,... | collective-permute-start | bytes 798728 | tf_op jit(solution)/shard_map/ppermute | solution.py:259
  36.4 3.7 %expert.6 = (f32[1024,1024]{1,0:T(8,128)S(1)}, f32[8,128]{1,0:T(8,128)}) custom-call(s32[2]{0:T(128)S(1)} %pad_add_fusion.place_ref, bf16[1040,128]{1,0:T(8,128)(2,1)S(1)} %collective-permute-done.2.refs_0_, bf16[1040,128]{1,0:T(8,128)(2,1)S(1)} %collective-permute-done.refs_0_.refs_1_, bf16[1024,2048]{1,0:T(8,128)(2,1)S(1)} %bitcast.10, ...), custom_call_target="tpu_custom_call" | custom-call | flops 1 | bytes 1 | tf_op jit(solution)/shard_map/expert/pallas_call | solution.py:217
  40.1 5.4 %collective-permute-done.6.refs_2_ = bf16[1040,128]{1,0:T(8,128)(2,1)S(1)} collective-permute-done((bf16[1040,128]{1,0:T(8,128)(2,1)S(1)}, bf16[1040,128]{1,0:T(8,128)(2,1)S(1)}, u32[]{:S(2)}, u32[]{:S(2)}) %collective-permute-start.6) | collective-permute-done | bytes 266272 | tf_op jit(solution)/shard_map/ppermute | solution.py:259
  45.5 5.2 %expert.7 = (f32[1024,1024]{1,0:T(8,128)S(1)}, f32[8,128]{1,0:T(8,128)}) custom-call(s32[2]{0:T(128)S(1)} %pad_add_fusion.place_ref, bf16[1040,128]{1,0:T(8,128)(2,1)S(1)} %collective-permute-done.4.refs_0_, bf16[1040,128]{1,0:T(8,128)(2,1)S(1)} %collective-permute-done.5.refs_1_, bf16[1040,128]{1,0:T(8,128)(2,1)S(1)} %collective-permute-done.6.refs_2_, ...), custom_call_target="tpu_custom_call" | custom-call | flops 1 | bytes 1 | tf_op jit(solution)/shard_map/expert/pallas_call | solution.py:217
  50.7 2.8 %expert.8 = (f32[1024,1024]{1,0:T(8,128)S(1)}, f32[8,128]{1,0:T(8,128)}) custom-call(s32[2]{0:T(128)S(1)} %pad_add_fusion.place_ref, bf16[1040,128]{1,0:T(8,128)(2,1)S(1)} %collective-permute-done.3.refs_0_, bf16[1024,2048]{1,0:T(8,128)(2,1)S(1)} %bitcast.12, bf16[2048,1024]{1,0:T(8,128)(2,1)S(1)} %bitcast.17, f32[1024,1024]{1,0:T(8,128)S(1)} %get-tuple-element.39.refs_3_), custom_call_target="tpu_custom_call" | custom-call | flops 1 | bytes 1 | tf_op jit(solution)/shard_map/expert/pallas_call | solution.py:217
  53.5 3.4 %expert.9 = (bf16[128,1024]{1,0:T(8,128)(2,1)S(1)}, bf16[128,1024]{1,0:T(8,128)(2,1)S(1)}, bf16[128,1024]{1,0:T(8,128)(2,1)S(1)}, bf16[128,1024]{1,0:T(8,128)(2,...) custom-call(s32[2]{0:T(128)S(1)} %pad_add_fusion.place_ref, ...), custom_call_target="tpu_custom_call" | custom-call | flops 1 | bytes 1 | tf_op jit(solution)/shard_map/expert/pallas_call | solution.py:217
  59.0 1.6 %collective-permute-start.11 = (bf16[128,1024]{1,0:T(8,128)(2,1)S(1)}, bf16[128,1024]{1,0:T(8,128)(2,1)S(1)}, u32[]{:S(2)}, u32[]{:S(2)}) collective-permute-start(bf16[128,1024]{1,0:T(8,128)(2,1)S(1)} %add_convert_fusion.1), channel_id=1, source_target_pairs={{0,2},{1,3},{2,0},{3,1},{4,6},{5,7},{6,4},{7,5},{8,10},{9,11},{10,... | collective-permute-start | bytes 786440 | tf_op jit(solution)/shard_map/ppermute | solution.py:259
  60.7 1.5 %collective-permute-start.9 = (bf16[128,1024]{1,0:T(8,128)(2,1)S(1)}, bf16[128,1024]{1,0:T(8,128)(2,1)S(1)}, u32[]{:S(2)}, u32[]{:S(2)}) collective-permute-start(bf16[128,1024]{1,0:T(8,128)(2,1)S(1)} %add_convert_fusion.2), channel_id=1, source_target_pairs={{0,6},{1,7},{2,4},{3,5},{4,2},{5,3},{6,0},{7,1},{8,14},{9,15},{10,... | collective-permute-start | bytes 786440 | tf_op jit(solution)/shard_map/ppermute | solution.py:259
  62.3 4.6 %collective-permute-done.13 = bf16[128,1024]{1,0:T(8,128)(2,1)S(1)} collective-permute-done((bf16[128,1024]{1,0:T(8,128)(2,1)S(1)}, bf16[128,1024]{1,0:T(8,128)(2,1)S(1)}, u32[]{:S(2)}, u32[]{:S(2)}) %collective-permute-start.13) | collective-permute-done | bytes 262176 | tf_op jit(solution)/shard_map/ppermute | solution.py:259
  66.8 1.5 %collective-permute-done.11 = bf16[128,1024]{1,0:T(8,128)(2,1)S(1)} collective-permute-done((bf16[128,1024]{1,0:T(8,128)(2,1)S(1)}, bf16[128,1024]{1,0:T(8,128)(2,1)S(1)}, u32[]{:S(2)}, u32[]{:S(2)}) %collective-permute-start.11) | collective-permute-done | bytes 262176 | tf_op jit(solution)/shard_map/ppermute | solution.py:259
  68.3 5.5 %collective-permute-done.9 = bf16[128,1024]{1,0:T(8,128)(2,1)S(1)} collective-permute-done((bf16[128,1024]{1,0:T(8,128)(2,1)S(1)}, bf16[128,1024]{1,0:T(8,128)(2,1)S(1)}, u32[]{:S(2)}, u32[]{:S(2)}) %collective-permute-start.9) | collective-permute-done | bytes 262176 | tf_op jit(solution)/shard_map/ppermute | solution.py:259
  74.0 1.6 %collective-permute-start.16 = (bf16[32,1024]{1,0:T(8,128)(2,1)S(1)}, bf16[32,1024]{1,0:T(8,128)(2,1)S(1)}, u32[]{:S(2)}, u32[]{:S(2)}) collective-permute-start(bf16[32,1024]{1,0:T(8,128)(2,1)S(1)} %get-tuple-element.52), channel_id=1, source_target_pairs={{0,8},{1,9},{2,10},{3,11},{4,12},{5,13},{6,14},{7,15},{8,0},{9,1},... | collective-permute-start | bytes 196616 | tf_op jit(solution)/shard_map/ppermute | solution.py:259
  75.6 3.6 %collective-permute-start.15 = (bf16[32,1024]{1,0:T(8,128)(2,1)S(1)}, bf16[32,1024]{1,0:T(8,128)(2,1)S(1)}, u32[]{:S(2)}, u32[]{:S(2)}) collective-permute-start(bf16[32,1024]{1,0:T(8,128)(2,1)S(1)} %get-tuple-element.53), channel_id=1, source_target_pairs={{0,16},{1,17},{2,18},{3,19},{4,20},{5,21},{6,22},{7,23},{8,24},{9,... | collective-permute-start | bytes 196616 | tf_op jit(solution)/shard_map/ppermute | solution.py:259
  79.3 3.8 %collective-permute-done.15 = bf16[32,1024]{1,0:T(8,128)(2,1)S(1)} collective-permute-done((bf16[32,1024]{1,0:T(8,128)(2,1)S(1)}, bf16[32,1024]{1,0:T(8,128)(2,1)S(1)}, u32[]{:S(2)}, u32[]{:S(2)}) %collective-permute-start.15) | collective-permute-done | bytes 65568 | tf_op jit(solution)/shard_map/ppermute | solution.py:259
  83.0 2.3 %collective-permute-done.14 = bf16[32,1024]{1,0:T(8,128)(2,1)S(1)} collective-permute-done((bf16[32,1024]{1,0:T(8,128)(2,1)S(1)}, bf16[32,1024]{1,0:T(8,128)(2,1)S(1)}, u32[]{:S(2)}, u32[]{:S(2)}) %collective-permute-start.14) | collective-permute-done | bytes 65568 | tf_op jit(solution)/shard_map/ppermute | solution.py:259
  (34 shorter events, 7.8 us)
Async XLA Ops:
  2.9 22.8 %collective-permute-start.2 = (bf16[1040,128]{1,0:T(8,128)(2,1)S(1)}, bf16[1040,128]{1,0:T(8,128)(2,1)S(1)}, u32[]{:S(2)}, u32[]{:S(2)}) collective-permute-start(bf16[1040,128]{1,0:T(8,128)(2,1)S(1)} %get-tuple-element.33), channel_id=1, source_target_pairs={{0,16},{1,17},{2,18},{3,19},{4,20},{5,21},{6,22},{7,23},{8,24},{9,... | collective-permute-start | bytes 798728 | tf_op jit(solution)/shard_map/ppermute | solution.py:259
  7.0 26.8 %collective-permute-start = (bf16[1040,128]{1,0:T(8,128)(2,1)S(1)}, bf16[1040,128]{1,0:T(8,128)(2,1)S(1)}, u32[]{:S(2)}, u32[]{:S(2)}) collective-permute-start(bf16[1040,128]{1,0:T(8,128)(2,1)S(1)} %get-tuple-element.30), channel_id=1, source_target_pairs={{0,20},{1,21},{2,22},{3,23},{4,16},{5,17},{6,18},{7,19},{8,28},{9,... | collective-permute-start | bytes 798728 | tf_op jit(solution)/shard_map/ppermute | solution.py:259
  9.2 30.9 %collective-permute-start.4 = (bf16[1040,128]{1,0:T(8,128)(2,1)S(1)}, bf16[1040,128]{1,0:T(8,128)(2,1)S(1)}, u32[]{:S(2)}, u32[]{:S(2)}) collective-permute-start(bf16[1040,128]{1,0:T(8,128)(2,1)S(1)} %get-tuple-element.34), channel_id=1, source_target_pairs={{0,4},{1,5},{2,6},{3,7},{4,0},{5,1},{6,2},{7,3},{8,12},{9,13},{10,... | collective-permute-start | bytes 798728 | tf_op jit(solution)/shard_map/ppermute | solution.py:259
  9.5 30.6 %collective-permute-start.5 = (bf16[1040,128]{1,0:T(8,128)(2,1)S(1)}, bf16[1040,128]{1,0:T(8,128)(2,1)S(1)}, u32[]{:S(2)}, u32[]{:S(2)}) collective-permute-start(bf16[1040,128]{1,0:T(8,128)(2,1)S(1)} %get-tuple-element.35), channel_id=1, source_target_pairs={{0,8},{1,9},{2,10},{3,11},{4,12},{5,13},{6,14},{7,15},{8,0},{9,1},... | collective-permute-start | bytes 798728 | tf_op jit(solution)/shard_map/ppermute | solution.py:259
  11.4 34.1 %collective-permute-start.6 = (bf16[1040,128]{1,0:T(8,128)(2,1)S(1)}, bf16[1040,128]{1,0:T(8,128)(2,1)S(1)}, u32[]{:S(2)}, u32[]{:S(2)}) collective-permute-start(bf16[1040,128]{1,0:T(8,128)(2,1)S(1)} %get-tuple-element.36), channel_id=1, source_target_pairs={{0,12},{1,13},{2,14},{3,15},{4,8},{5,9},{6,10},{7,11},{8,4},{9,5},... | collective-permute-start | bytes 798728 | tf_op jit(solution)/shard_map/ppermute | solution.py:259
  12.8 2.2 %copy-start = (bf16[1,1024,2048]{2,1,0:T(8,128)(2,1)S(1)}, bf16[1,1024,2048]{2,1,0:T(8,128)(2,1)}, u32[]{:S(2)}) copy-start(bf16[1,1024,2048]{2,1,0:T(8,128)(2,1)} %param.8) | copy-start | bytes 12582916
  15.0 2.2 %copy-start.2 = (bf16[1,2048,1024]{2,1,0:T(8,128)(2,1)S(1)}, bf16[1,2048,1024]{2,1,0:T(8,128)(2,1)}, u32[]{:S(2)}) copy-start(bf16[1,2048,1024]{2,1,0:T(8,128)(2,1)} %param.9) | copy-start | bytes 12582916
  17.1 19.3 %copy-start.1 = (bf16[1,1024,2048]{2,1,0:T(8,128)(2,1)S(1)}, bf16[1,1024,2048]{2,1,0:T(8,128)(2,1)}, u32[]{:S(2)}) copy-start(bf16[1,1024,2048]{2,1,0:T(8,128)(2,1)} %param.8) | copy-start | bytes 12582916
  17.2 19.3 %copy-start.3 = (bf16[1,2048,1024]{2,1,0:T(8,128)(2,1)S(1)}, bf16[1,2048,1024]{2,1,0:T(8,128)(2,1)}, u32[]{:S(2)}) copy-start(bf16[1,2048,1024]{2,1,0:T(8,128)(2,1)} %param.9) | copy-start | bytes 12582916
  26.1 24.6 %collective-permute-start.3 = (bf16[1040,128]{1,0:T(8,128)(2,1)S(1)}, bf16[1040,128]{1,0:T(8,128)(2,1)S(1)}, u32[]{:S(2)}, u32[]{:S(2)}) collective-permute-start(bf16[1040,128]{1,0:T(8,128)(2,1)S(1)} %pack_more.5), channel_id=1, source_target_pairs={{0,24},{1,25},{2,26},{3,27},{4,28},{5,29},{6,30},{7,31},{8,16},{9,... | collective-permute-start | bytes 798728 | tf_op jit(solution)/shard_map/ppermute | solution.py:259
  34.2 19.3 %collective-permute-start.1 = (bf16[1040,128]{1,0:T(8,128)(2,1)S(1)}, bf16[1040,128]{1,0:T(8,128)(2,1)S(1)}, u32[]{:S(2)}, u32[]{:S(2)}) collective-permute-start(bf16[1040,128]{1,0:T(8,128)(2,1)S(1)} %pack_more.4), channel_id=1, source_target_pairs={{0,28},{1,29},{2,30},{3,31},{4,24},{5,25},{6,26},{7,27},{8,20},{9,... | collective-permute-start | bytes 798728 | tf_op jit(solution)/shard_map/ppermute | solution.py:259
  56.8 1.5 %collective-permute-start.12 = (bf16[128,1024]{1,0:T(8,128)(2,1)S(1)}, bf16[128,1024]{1,0:T(8,128)(2,1)S(1)}, u32[]{:S(2)}, u32[]{:S(2)}) collective-permute-start(bf16[128,1024]{1,0:T(8,128)(2,1)S(1)} %get-tuple-element.48), channel_id=1, source_target_pairs={{0,1},{1,0},{2,3},{3,2},{4,5},{5,4},{6,7},{7,6},{8,9},{9,8},{10,11... | collective-permute-start | bytes 786440 | tf_op jit(solution)/shard_map/ppermute | solution.py:259
  56.8 2.2 %collective-permute-start.10 = (bf16[128,1024]{1,0:T(8,128)(2,1)S(1)}, bf16[128,1024]{1,0:T(8,128)(2,1)S(1)}, u32[]{:S(2)}, u32[]{:S(2)}) collective-permute-start(bf16[128,1024]{1,0:T(8,128)(2,1)S(1)} %get-tuple-element.46), channel_id=1, source_target_pairs={{0,1},{1,0},{2,3},{3,2},{4,5},{5,4},{6,7},{7,6},{8,9},{9,8},{10,11... | collective-permute-start | bytes 786440 | tf_op jit(solution)/shard_map/ppermute | solution.py:259
  57.3 3.3 %collective-permute-start.8 = (bf16[128,1024]{1,0:T(8,128)(2,1)S(1)}, bf16[128,1024]{1,0:T(8,128)(2,1)S(1)}, u32[]{:S(2)}, u32[]{:S(2)}) collective-permute-start(bf16[128,1024]{1,0:T(8,128)(2,1)S(1)} %get-tuple-element.44), channel_id=1, source_target_pairs={{0,1},{1,0},{2,3},{3,2},{4,5},{5,4},{6,7},{7,6},{8,9},{9,8},{10,11... | collective-permute-start | bytes 786440 | tf_op jit(solution)/shard_map/ppermute | solution.py:259
  57.3 4.9 %collective-permute-start.7 = (bf16[128,1024]{1,0:T(8,128)(2,1)S(1)}, bf16[128,1024]{1,0:T(8,128)(2,1)S(1)}, u32[]{:S(2)}, u32[]{:S(2)}) collective-permute-start(bf16[128,1024]{1,0:T(8,128)(2,1)S(1)} %get-tuple-element.42), channel_id=1, source_target_pairs={{0,1},{1,0},{2,3},{3,2},{4,5},{5,4},{6,7},{7,6},{8,9},{9,8},{10,11... | collective-permute-start | bytes 786440 | tf_op jit(solution)/shard_map/ppermute | solution.py:259
  58.4 8.4 %collective-permute-start.13 = (bf16[128,1024]{1,0:T(8,128)(2,1)S(1)}, bf16[128,1024]{1,0:T(8,128)(2,1)S(1)}, u32[]{:S(2)}, u32[]{:S(2)}) collective-permute-start(bf16[128,1024]{1,0:T(8,128)(2,1)S(1)} %add_convert_fusion), channel_id=1, source_target_pairs={{0,4},{1,5},{2,6},{3,7},{4,0},{5,1},{6,2},{7,3},{8,12},{9,13},{10,... | collective-permute-start | bytes 786440 | tf_op jit(solution)/shard_map/ppermute | solution.py:259
  59.0 9.3 %collective-permute-start.11 = (bf16[128,1024]{1,0:T(8,128)(2,1)S(1)}, bf16[128,1024]{1,0:T(8,128)(2,1)S(1)}, u32[]{:S(2)}, u32[]{:S(2)}) collective-permute-start(bf16[128,1024]{1,0:T(8,128)(2,1)S(1)} %add_convert_fusion.1), channel_id=1, source_target_pairs={{0,2},{1,3},{2,0},{3,1},{4,6},{5,7},{6,4},{7,5},{8,10},{9,11},{10,... | collective-permute-start | bytes 786440 | tf_op jit(solution)/shard_map/ppermute | solution.py:259
  60.7 13.0 %collective-permute-start.9 = (bf16[128,1024]{1,0:T(8,128)(2,1)S(1)}, bf16[128,1024]{1,0:T(8,128)(2,1)S(1)}, u32[]{:S(2)}, u32[]{:S(2)}) collective-permute-start(bf16[128,1024]{1,0:T(8,128)(2,1)S(1)} %add_convert_fusion.2), channel_id=1, source_target_pairs={{0,6},{1,7},{2,4},{3,5},{4,2},{5,3},{6,0},{7,1},{8,14},{9,15},{10,... | collective-permute-start | bytes 786440 | tf_op jit(solution)/shard_map/ppermute | solution.py:259
  74.0 5.2 %collective-permute-start.16 = (bf16[32,1024]{1,0:T(8,128)(2,1)S(1)}, bf16[32,1024]{1,0:T(8,128)(2,1)S(1)}, u32[]{:S(2)}, u32[]{:S(2)}) collective-permute-start(bf16[32,1024]{1,0:T(8,128)(2,1)S(1)} %get-tuple-element.52), channel_id=1, source_target_pairs={{0,8},{1,9},{2,10},{3,11},{4,12},{5,13},{6,14},{7,15},{8,0},{9,1},... | collective-permute-start | bytes 196616 | tf_op jit(solution)/shard_map/ppermute | solution.py:259
  75.6 7.4 %collective-permute-start.15 = (bf16[32,1024]{1,0:T(8,128)(2,1)S(1)}, bf16[32,1024]{1,0:T(8,128)(2,1)S(1)}, u32[]{:S(2)}, u32[]{:S(2)}) collective-permute-start(bf16[32,1024]{1,0:T(8,128)(2,1)S(1)} %get-tuple-element.53), channel_id=1, source_target_pairs={{0,16},{1,17},{2,18},{3,19},{4,20},{5,21},{6,22},{7,23},{8,24},{9,... | collective-permute-start | bytes 196616 | tf_op jit(solution)/shard_map/ppermute | solution.py:259
  79.3 6.1 %collective-permute-start.14 = (bf16[32,1024]{1,0:T(8,128)(2,1)S(1)}, bf16[32,1024]{1,0:T(8,128)(2,1)S(1)}, u32[]{:S(2)}, u32[]{:S(2)}) collective-permute-start(bf16[32,1024]{1,0:T(8,128)(2,1)S(1)} %get-tuple-element.51), channel_id=1, source_target_pairs={{0,24},{1,25},{2,26},{3,27},{4,28},{5,29},{6,30},{7,31},{8,16},{9,... | collective-permute-start | bytes 196616 | tf_op jit(solution)/shard_map/ppermute | solution.py:259

commit v3 on v2

--- a/solution.py
+++ b/solution.py
@@ -137,9 +137,9 @@
         x_ref[row : row + slots, c * LANES : (c + 1) * LANES] = block_ref[c * slots : (c + 1) * slots, :]
     ids = block_ref[width // LANES * slots :, :slots].astype(F32).astype(I32)
     owner = ids[0:1] ^ base
-    half = relations // 2
-    y, z, g = owner % 2, owner // 2 % half, owner // relations
-    at = ((((g % 2) * 2 + g // 2) * 2 + y) * half + z) * NODE_DEV + ids[1:2]
+    far = relations // 4
+    y, z, f, g = owner % 2, owner // 2 % 2, owner // 4 % far, owner // relations
+    at = (((((g % 2) * 2 + g // 2) * 2 + y) * 2 + z) * far + f) * NODE_DEV + ids[1:2]
     return jnp.where(ids[2:3] > 0, at, -1)
 
 
@@ -207,13 +207,13 @@
     if edges is None:
         right, shapes = width, [jax.ShapeDtypeStruct((nodes, width), F32)]
     else:
-        right, shapes = edges[1], [jax.ShapeDtypeStruct((nodes // 8, edges[1]), BF16)] * 8
+        right, shapes = edges[1], [jax.ShapeDtypeStruct((nodes // 16, edges[1]), BF16)] * 16
     shapes.append(jax.ShapeDtypeStruct((8, LANES), F32))
     kept = [jax.ShapeDtypeStruct((rows, inner), BF16), jax.ShapeDtypeStruct((nodes, rows), BF16)]
     scratch = [pltpu.VMEM(s.shape, s.dtype) for s in kept]
     args = [place, *blocks, w_first, w_second] + ([] if sums is None else [sums])
-    keep = edges is not None
-    params = pltpu.CompilerParams(vmem_limit_bytes=16 * MIB if relations <= 8 else 48 * MIB)
+    keep = edges is not None and len(edges) > 2
+    params = pltpu.CompilerParams(vmem_limit_bytes=16 * MIB if relations <= 8 else 58 * MIB)
     outs = pl.pallas_call(
         functools.partial(expert_kernel, count, slots, groups, relations, sums is not None, right),
         out_shape=shapes + kept * keep,
@@ -226,18 +226,18 @@
     )(*args)
     if edges is None:
         return outs
-    pieces = [outs[:8]]
+    pieces = [outs[:16]]
     for left, right in zip(edges[1:-1], edges[2:]):
         pieces.append(
             pl.pallas_call(
                 functools.partial(more_kernel, left, right),
-                out_shape=[jax.ShapeDtypeStruct((nodes // 8, right - left), BF16)] * 8,
+                out_shape=[jax.ShapeDtypeStruct((nodes // 16, right - left), BF16)] * 16,
                 in_specs=[VM] * 4,
-                out_specs=[VM] * 8,
+                out_specs=[VM] * 16,
                 compiler_params=params,
                 cost_estimate=pl.CostEstimate(flops=1, bytes_accessed=1, transcendentals=0),
                 name="expert_more",
-            )(outs[9], outs[10], w_second, sums)
+            )(outs[17], outs[18], w_second, sums)
         )
     return pieces
 
@@ -277,20 +277,25 @@
     for k in (2, 3):
         late = pack_more(kept, far[k][0], step, slots, [held[far[k - 2][-1]], token])
         held.update({d: move(block, 0, d) for d, block in zip(far[k], late)})
-    for turn in (far[0] + far[1], list(range(1, half)), far[2]):
+    for turn in (far[0] + [1], far[1] + list(range(2, half)), far[2]):
         sums, token = run(turn, sums)
     sums = run(far[3], sums, True)
 
     states = []
     for piece in sums:
-        near = [piece[b].astype(F32) + move(piece[4 + b], 1, 0).astype(F32) for b in range(4)]
+        away = [move(jnp.concatenate(piece[b : b + 4]), 1, 0) for b in (8, 12)]
+        lines = piece[0].shape[0]
+        near = [
+            piece[b].astype(F32) + away[b // 4][b % 4 * lines : (b % 4 + 1) * lines].astype(F32)
+            for b in range(8)
+        ]
         total = near[0]
-        for b in (3, 2, 1):
-            total = total + move(near[b].astype(BF16), 2 * (b // 2), b % 2).astype(F32)
-        total = total.reshape(half, NODE_DEV, -1)
+        for b in (7, 6, 5, 3, 4, 2, 1):
+            total = total + move(near[b].astype(BF16), 2 * (b // 4), b // 2 % 2 + 2 * (b % 2)).astype(F32)
+        total = total.reshape(relations // 4, NODE_DEV, -1)
         state = total[0]
-        for z in range(half - 1, 0, -1):
-            state = state + move(total[z].astype(BF16), 0, 2 * z).astype(F32)
+        for f in range(relations // 4 - 1, 0, -1):
+            state = state + move(total[f].astype(BF16), 0, 4 * f).astype(F32)
         states.append(state)
     state = jnp.concatenate(states, axis=1)
     return (state * (1.0 / math.sqrt(rows / NODE_DEV)))[None]

time: 86.2 us -> 82.1 us (0.952)
  waiting for transfers between devices: 34.4 us -> 26.1 us
  starting transfers between devices: 24 us -> 28.3 us
    ppermute x17, waiting for transfers between devices: 34.4 us -> 26.1 us  [move(): return lax.ppermute(value, ('rel', 'dom'), pairs)]
    ppermute x17, starting transfers between devices: 24 us -> 28.3 us  [move(): return lax.ppermute(value, ('rel', 'dom'), pairs)]
  transfers between devices with their start and end apart: 17 -> 17, of which waited for: 9 -> 8; matrix products, arithmetic and copies ran while one was open for 0% -> 0% of each run, Pallas kernels for 18% -> 19%
where the time goes in v3:
time: 82.1 us; the launch traced here: 81.9 us
  starting transfers between devices  28.3 us (34%)
  waiting for transfers between devices  26.1 us (32%)
  Pallas kernels  21.7 us (26%)
  local copies, waits for them, and re-layouts  4.39 us (5%)
  other arithmetic  1.32 us (2%)
    ppermute x17, starting transfers between devices, move(): return lax.ppermute(value, ('rel', 'dom'), pairs)  28.3 us
    ppermute x17, waiting for transfers between devices, move(): return lax.ppermute(value, ('rel', 'dom'), pairs)  26.1 us
    pallas_call x5, Pallas kernels, expert(): pl.pallas_call(functools.partial(expert_kernel, count, slots, groups, rel...  17.3 us
    unnamed x8, local copies, waits for them, and re-layouts  4.38 us
    pallas_call x1, Pallas kernels, pack(): pl.pallas_call(functools.partial(pack_kernel, relations, slots, first, co...  2.85 us
  transfers between devices with their start and end apart: 17, of which 8 were waited for; matrix products, arithmetic and copies ran while one was open for 0% of the time, Pallas kernels for 19%

profile of v3, /device:TPU:0, one launch (start us, length us, event | category | flops | bytes accessed | tf_op | source)
XLA Modules:
  0.0 81.9 jit_solution(13262062285499563638)
XLA Ops:
  0.1 2.8 %pack_far.1 = (bf16[1040,128]{1,0:T(8,128)(2,1)S(1)}, bf16[1040,128]{1,0:T(8,128)(2,1)S(1)}, bf16[512,1024]{1,0:T(8,128)(2,1)S(1)}, s32[1,512]{1,0:T(1,128)S(1)}, bf16[16,512]{1,0:T(8,128)(2,1)S(1)}) custom-call(s32[2]{0:T(128)S(1)} %pad_add_fusion.place_ref, s32[1,512]{1,0:T(1,128)} %bitcast.21, s32[1,512]{1,0:T(1,128)} %dest_hbm.1, ...), custom_call_target="tpu_custom_call" | custom-call | flops 1 | bytes 1 | tf_op jit(solution)/shard_map/pack_far/pallas_call | solution.py:109
  2.9 4.1 %collective-permute-start.2 = (bf16[1040,128]{1,0:T(8,128)(2,1)S(1)}, bf16[1040,128]{1,0:T(8,128)(2,1)S(1)}, u32[]{:S(2)}, u32[]{:S(2)}) collective-permute-start(bf16[1040,128]{1,0:T(8,128)(2,1)S(1)} %get-tuple-element.41), channel_id=1, source_target_pairs={{0,16},{1,17},{2,18},{3,19},{4,20},{5,21},{6,22},{7,23},{8,24},{9,... | collective-permute-start | bytes 798728 | tf_op jit(solution)/shard_map/ppermute | solution.py:259
  9.2 1.7 %collective-permute-start.4 = (bf16[1040,128]{1,0:T(8,128)(2,1)S(1)}, bf16[1040,128]{1,0:T(8,128)(2,1)S(1)}, u32[]{:S(2)}, u32[]{:S(2)}) collective-permute-start(bf16[1040,128]{1,0:T(8,128)(2,1)S(1)} %get-tuple-element.42), channel_id=1, source_target_pairs={{0,8},{1,9},{2,10},{3,11},{4,12},{5,13},{6,14},{7,15},{8,0},{9,1},... | collective-permute-start | bytes 798728 | tf_op jit(solution)/shard_map/ppermute | solution.py:259
  11.0 1.8 %collective-permute-start.6 = (bf16[1040,128]{1,0:T(8,128)(2,1)S(1)}, bf16[1040,128]{1,0:T(8,128)(2,1)S(1)}, u32[]{:S(2)}, u32[]{:S(2)}) collective-permute-start(bf16[1040,128]{1,0:T(8,128)(2,1)S(1)} %get-tuple-element.44), channel_id=1, source_target_pairs={{0,4},{1,5},{2,6},{3,7},{4,0},{5,1},{6,2},{7,3},{8,12},{9,13},{10,... | collective-permute-start | bytes 798728 | tf_op jit(solution)/shard_map/ppermute | solution.py:259
  12.8 2.2 %copy-done = bf16[1,1024,2048]{2,1,0:T(8,128)(2,1)S(1)} copy-done((bf16[1,1024,2048]{2,1,0:T(8,128)(2,1)S(1)}, bf16[1,1024,2048]{2,1,0:T(8,128)(2,1)}, u32[]{:S(2)}) %copy-start) | copy-done | bytes 4194328
  15.0 2.2 %copy-done.2 = bf16[1,2048,1024]{2,1,0:T(8,128)(2,1)S(1)} copy-done((bf16[1,2048,1024]{2,1,0:T(8,128)(2,1)S(1)}, bf16[1,2048,1024]{2,1,0:T(8,128)(2,1)}, u32[]{:S(2)}) %copy-start.2) | copy-done | bytes 4194328
  17.1 2.5 %expert.5 = (f32[1024,1024]{1,0:T(8,128)S(1)}, f32[8,128]{1,0:T(8,128)S(1)}) custom-call(s32[2]{0:T(128)S(1)} %pad_add_fusion.place_ref, bf16[1040,128]{1,0:T(8,128)(2,1)S(1)} %get-tuple-element.39.refs_0_, bf16[1024,2048]{1,0:T(8,128)(2,1)S(1)} %bitcast.9, bf16[2048,1024]{1,0:T(8,128)(2,1)S(1)} %bitcast.14), custom_call_target="tpu_custom_call" | custom-call | flops 1 | bytes 1 | tf_op jit(solution)/shard_map/expert/pallas_call | solution.py:217
  19.7 6.1 %collective-permute-done.2.refs_0_ = bf16[1040,128]{1,0:T(8,128)(2,1)S(1)} collective-permute-done((bf16[1040,128]{1,0:T(8,128)(2,1)S(1)}, bf16[1040,128]{1,0:T(8,128)(2,1)S(1)}, u32[]{:S(2)}, u32[]{:S(2)}) %collective-permute-start.2) | collective-permute-done | bytes 266272 | tf_op jit(solution)/shard_map/ppermute | solution.py:259
  26.1 2.9 %collective-permute-start.3 = (bf16[1040,128]{1,0:T(8,128)(2,1)S(1)}, bf16[1040,128]{1,0:T(8,128)(2,1)S(1)}, u32[]{:S(2)}, u32[]{:S(2)}) collective-permute-start(bf16[1040,128]{1,0:T(8,128)(2,1)S(1)} %pack_more.5), channel_id=1, source_target_pairs={{0,24},{1,25},{2,26},{3,27},{4,28},{5,29},{6,30},{7,31},{8,16},{9,... | collective-permute-start | bytes 798728 | tf_op jit(solution)/shard_map/ppermute | solution.py:259
  29.0 4.9 %collective-permute-done.refs_0_ = bf16[1040,128]{1,0:T(8,128)(2,1)S(1)} collective-permute-done((bf16[1040,128]{1,0:T(8,128)(2,1)S(1)}, bf16[1040,128]{1,0:T(8,128)(2,1)S(1)}, u32[]{:S(2)}, u32[]{:S(2)}) %collective-permute-start) | collective-permute-done | bytes 266272 | tf_op jit(solution)/shard_map/ppermute | solution.py:259
  34.2 2.2 %collective-permute-start.1 = (bf16[1040,128]{1,0:T(8,128)(2,1)S(1)}, bf16[1040,128]{1,0:T(8,128)(2,1)S(1)}, u32[]{:S(2)}, u32[]{:S(2)}) collective-permute-start(bf16[1040,128]{1,0:T(8,128)(2,1)S(1)} %pack_more.4), channel_id=1, source_target_pairs={{0,28},{1,29},{2,30},{3,31},{4,24},{5,25},{6,26},{7,27},{8,20},{9,... | collective-permute-start | bytes 798728 | tf_op jit(solution)/shard_map/ppermute | solution.py:259
  36.4 3.7 %expert.6 = (f32[1024,1024]{1,0:T(8,128)S(1)}, f32[8,128]{1,0:T(8,128)}) custom-call(s32[2]{0:T(128)S(1)} %pad_add_fusion.place_ref, bf16[1040,128]{1,0:T(8,128)(2,1)S(1)} %collective-permute-done.2.refs_0_, bf16[1040,128]{1,0:T(8,128)(2,1)S(1)} %collective-permute-done.6.refs_1_, bf16[1024,2048]{1,0:T(8,128)(2,1)S(1)} %bitcast.10, ...), custom_call_target="tpu_custom_call" | custom-call | flops 1 | bytes 1 | tf_op jit(solution)/shard_map/expert/pallas_call | solution.py:217
  40.1 4.2 %collective-permute-done.5.refs_2_ = bf16[1040,128]{1,0:T(8,128)(2,1)S(1)} collective-permute-done((bf16[1040,128]{1,0:T(8,128)(2,1)S(1)}, bf16[1040,128]{1,0:T(8,128)(2,1)S(1)}, u32[]{:S(2)}, u32[]{:S(2)}) %collective-permute-start.5) | collective-permute-done | bytes 266272 | tf_op jit(solution)/shard_map/ppermute | solution.py:259
  44.3 5.2 %expert.7 = (f32[1024,1024]{1,0:T(8,128)S(1)}, f32[8,128]{1,0:T(8,128)}) custom-call(s32[2]{0:T(128)S(1)} %pad_add_fusion.place_ref, bf16[1040,128]{1,0:T(8,128)(2,1)S(1)} %collective-permute-done.refs_0_, bf16[1040,128]{1,0:T(8,128)(2,1)S(1)} %collective-permute-done.4.refs_1_, bf16[1040,128]{1,0:T(8,128)(2,1)S(1)} %collective-permute-done.5.refs_2_, ...), custom_call_target="tpu_custom_call" | custom-call | flops 1 | bytes 1 | tf_op jit(solution)/shard_map/expert/pallas_call | solution.py:217
  49.5 2.8 %expert.8 = (f32[1024,1024]{1,0:T(8,128)S(1)}, f32[8,128]{1,0:T(8,128)}) custom-call(s32[2]{0:T(128)S(1)} %pad_add_fusion.place_ref, bf16[1040,128]{1,0:T(8,128)(2,1)S(1)} %collective-permute-done.3.refs_0_, bf16[1024,2048]{1,0:T(8,128)(2,1)S(1)} %bitcast.12, bf16[2048,1024]{1,0:T(8,128)(2,1)S(1)} %bitcast.17, f32[1024,1024]{1,0:T(8,128)S(1)} %get-tuple-element.47.refs_3_), custom_call_target="tpu_custom_call" | custom-call | flops 1 | bytes 1 | tf_op jit(solution)/shard_map/expert/pallas_call | solution.py:217
  52.3 3.1 %expert.9 = (bf16[64,1024]{1,0:T(8,128)(2,1)S(1)}, bf16[64,1024]{1,0:T(8,128)(2,1)S(1)}, bf16[64,1024]{1,0:T(8,128)(2,1)S(1)}, bf16[64,1024]{1,0:T(8,128)(2,1)S(...) custom-call(s32[2]{0:T(128)S(1)} %pad_add_fusion.place_ref, ...), custom_call_target="tpu_custom_call" | custom-call | flops 1 | bytes 1 | tf_op jit(solution)/shard_map/expert/pallas_call | solution.py:217
  57.5 2.8 %collective-permute-start.15 = (bf16[64,1024]{1,0:T(8,128)(2,1)S(1)}, bf16[64,1024]{1,0:T(8,128)(2,1)S(1)}, u32[]{:S(2)}, u32[]{:S(2)}) collective-permute-start(bf16[64,1024]{1,0:T(8,128)(2,1)S(1)} %get-tuple-element.70), channel_id=1, source_target_pairs={{0,8},{1,9},{2,10},{3,11},{4,12},{5,13},{6,14},{7,15},{8,0},{9,1},... | collective-permute-start | bytes 393224 | tf_op jit(solution)/shard_map/ppermute | solution.py:259
  63.6 1.9 %collective-permute-start.11 = (bf16[64,1024]{1,0:T(8,128)(2,1)S(1)}, bf16[64,1024]{1,0:T(8,128)(2,1)S(1)}, u32[]{:S(2)}, u32[]{:S(2)}) collective-permute-start(bf16[64,1024]{1,0:T(8,128)(2,1)S(1)} %get-tuple-element.67), channel_id=1, source_target_pairs={{0,10},{1,11},{2,8},{3,9},{4,14},{5,15},{6,12},{7,13},{8,2},{9,3},... | collective-permute-start | bytes 393224 | tf_op jit(solution)/shard_map/ppermute | solution.py:259
  65.5 1.6 %collective-permute-start.10 = (bf16[64,1024]{1,0:T(8,128)(2,1)S(1)}, bf16[64,1024]{1,0:T(8,128)(2,1)S(1)}, u32[]{:S(2)}, u32[]{:S(2)}) collective-permute-start(bf16[64,1024]{1,0:T(8,128)(2,1)S(1)} %get-tuple-element.68), channel_id=1, source_target_pairs={{0,6},{1,7},{2,4},{3,5},{4,2},{5,3},{6,0},{7,1},{8,14},{9,15},{10,... | collective-permute-start | bytes 393224 | tf_op jit(solution)/shard_map/ppermute | solution.py:259
  68.2 1.9 %collective-permute-done.12 = bf16[64,1024]{1,0:T(8,128)(2,1)S(1)} collective-permute-done((bf16[64,1024]{1,0:T(8,128)(2,1)S(1)}, bf16[64,1024]{1,0:T(8,128)(2,1)S(1)}, u32[]{:S(2)}, u32[]{:S(2)}) %collective-permute-start.12) | collective-permute-done | bytes 131104 | tf_op jit(solution)/shard_map/ppermute | solution.py:259
  70.1 2.1 %collective-permute-done.11 = bf16[64,1024]{1,0:T(8,128)(2,1)S(1)} collective-permute-done((bf16[64,1024]{1,0:T(8,128)(2,1)S(1)}, bf16[64,1024]{1,0:T(8,128)(2,1)S(1)}, u32[]{:S(2)}, u32[]{:S(2)}) %collective-permute-start.11) | collective-permute-done | bytes 131104 | tf_op jit(solution)/shard_map/ppermute | solution.py:259
  72.2 3.5 %collective-permute-done.10 = bf16[64,1024]{1,0:T(8,128)(2,1)S(1)} collective-permute-done((bf16[64,1024]{1,0:T(8,128)(2,1)S(1)}, bf16[64,1024]{1,0:T(8,128)(2,1)S(1)}, u32[]{:S(2)}, u32[]{:S(2)}) %collective-permute-start.10) | collective-permute-done | bytes 131104 | tf_op jit(solution)/shard_map/ppermute | solution.py:259
  75.8 3.2 %collective-permute-start.16 = (bf16[32,1024]{1,0:T(8,128)(2,1)S(1)}, bf16[32,1024]{1,0:T(8,128)(2,1)S(1)}, u32[]{:S(2)}, u32[]{:S(2)}) collective-permute-start(bf16[32,1024]{1,0:T(8,128)(2,1)S(1)} %slice.67), channel_id=1, source_target_pairs={{0,16},{1,17},{2,18},{3,19},{4,20},{5,21},{6,22},{7,23},{8,24},{9,... | collective-permute-start | bytes 196616 | tf_op jit(solution)/shard_map/ppermute | solution.py:259
  79.0 2.2 %collective-permute-done.16 = bf16[32,1024]{1,0:T(8,128)(2,1)S(1)} collective-permute-done((bf16[32,1024]{1,0:T(8,128)(2,1)S(1)}, bf16[32,1024]{1,0:T(8,128)(2,1)S(1)}, u32[]{:S(2)}, u32[]{:S(2)}) %collective-permute-start.16) | collective-permute-done | bytes 65568 | tf_op jit(solution)/shard_map/ppermute | solution.py:259
  (35 shorter events, 10.4 us)
Async XLA Ops:
  2.9 22.8 %collective-permute-start.2 = (bf16[1040,128]{1,0:T(8,128)(2,1)S(1)}, bf16[1040,128]{1,0:T(8,128)(2,1)S(1)}, u32[]{:S(2)}, u32[]{:S(2)}) collective-permute-start(bf16[1040,128]{1,0:T(8,128)(2,1)S(1)} %get-tuple-element.41), channel_id=1, source_target_pairs={{0,16},{1,17},{2,18},{3,19},{4,20},{5,21},{6,22},{7,23},{8,24},{9,... | collective-permute-start | bytes 798728 | tf_op jit(solution)/shard_map/ppermute | solution.py:259
  7.0 26.8 %collective-permute-start = (bf16[1040,128]{1,0:T(8,128)(2,1)S(1)}, bf16[1040,128]{1,0:T(8,128)(2,1)S(1)}, u32[]{:S(2)}, u32[]{:S(2)}) collective-permute-start(bf16[1040,128]{1,0:T(8,128)(2,1)S(1)} %get-tuple-element.38), channel_id=1, source_target_pairs={{0,20},{1,21},{2,22},{3,23},{4,16},{5,17},{6,18},{7,19},{8,28},{9,... | collective-permute-start | bytes 798728 | tf_op jit(solution)/shard_map/ppermute | solution.py:259
  9.2 30.9 %collective-permute-start.4 = (bf16[1040,128]{1,0:T(8,128)(2,1)S(1)}, bf16[1040,128]{1,0:T(8,128)(2,1)S(1)}, u32[]{:S(2)}, u32[]{:S(2)}) collective-permute-start(bf16[1040,128]{1,0:T(8,128)(2,1)S(1)} %get-tuple-element.42), channel_id=1, source_target_pairs={{0,8},{1,9},{2,10},{3,11},{4,12},{5,13},{6,14},{7,15},{8,0},{9,1},... | collective-permute-start | bytes 798728 | tf_op jit(solution)/shard_map/ppermute | solution.py:259
  10.9 33.4 %collective-permute-start.5 = (bf16[1040,128]{1,0:T(8,128)(2,1)S(1)}, bf16[1040,128]{1,0:T(8,128)(2,1)S(1)}, u32[]{:S(2)}, u32[]{:S(2)}) collective-permute-start(bf16[1040,128]{1,0:T(8,128)(2,1)S(1)} %get-tuple-element.43), channel_id=1, source_target_pairs={{0,12},{1,13},{2,14},{3,15},{4,8},{5,9},{6,10},{7,11},{8,4},{9,5},... | collective-permute-start | bytes 798728 | tf_op jit(solution)/shard_map/ppermute | solution.py:259
  11.0 25.4 %collective-permute-start.6 = (bf16[1040,128]{1,0:T(8,128)(2,1)S(1)}, bf16[1040,128]{1,0:T(8,128)(2,1)S(1)}, u32[]{:S(2)}, u32[]{:S(2)}) collective-permute-start(bf16[1040,128]{1,0:T(8,128)(2,1)S(1)} %get-tuple-element.44), channel_id=1, source_target_pairs={{0,4},{1,5},{2,6},{3,7},{4,0},{5,1},{6,2},{7,3},{8,12},{9,13},{10,... | collective-permute-start | bytes 798728 | tf_op jit(solution)/shard_map/ppermute | solution.py:259
  12.8 2.2 %copy-start = (bf16[1,1024,2048]{2,1,0:T(8,128)(2,1)S(1)}, bf16[1,1024,2048]{2,1,0:T(8,128)(2,1)}, u32[]{:S(2)}) copy-start(bf16[1,1024,2048]{2,1,0:T(8,128)(2,1)} %param.8) | copy-start | bytes 12582916
  14.9 2.2 %copy-start.2 = (bf16[1,2048,1024]{2,1,0:T(8,128)(2,1)S(1)}, bf16[1,2048,1024]{2,1,0:T(8,128)(2,1)}, u32[]{:S(2)}) copy-start(bf16[1,2048,1024]{2,1,0:T(8,128)(2,1)} %param.9) | copy-start | bytes 12582916
  17.1 19.3 %copy-start.1 = (bf16[1,1024,2048]{2,1,0:T(8,128)(2,1)S(1)}, bf16[1,1024,2048]{2,1,0:T(8,128)(2,1)}, u32[]{:S(2)}) copy-start(bf16[1,1024,2048]{2,1,0:T(8,128)(2,1)} %param.8) | copy-start | bytes 12582916
  17.1 19.3 %copy-start.3 = (bf16[1,2048,1024]{2,1,0:T(8,128)(2,1)S(1)}, bf16[1,2048,1024]{2,1,0:T(8,128)(2,1)}, u32[]{:S(2)}) copy-start(bf16[1,2048,1024]{2,1,0:T(8,128)(2,1)} %param.9) | copy-start | bytes 12582916
  26.1 23.4 %collective-permute-start.3 = (bf16[1040,128]{1,0:T(8,128)(2,1)S(1)}, bf16[1040,128]{1,0:T(8,128)(2,1)S(1)}, u32[]{:S(2)}, u32[]{:S(2)}) collective-permute-start(bf16[1040,128]{1,0:T(8,128)(2,1)S(1)} %pack_more.5), channel_id=1, source_target_pairs={{0,24},{1,25},{2,26},{3,27},{4,28},{5,29},{6,30},{7,31},{8,16},{9,... | collective-permute-start | bytes 798728 | tf_op jit(solution)/shard_map/ppermute | solution.py:259
  34.2 18.1 %collective-permute-start.1 = (bf16[1040,128]{1,0:T(8,128)(2,1)S(1)}, bf16[1040,128]{1,0:T(8,128)(2,1)S(1)}, u32[]{:S(2)}, u32[]{:S(2)}) collective-permute-start(bf16[1040,128]{1,0:T(8,128)(2,1)S(1)} %pack_more.4), channel_id=1, source_target_pairs={{0,28},{1,29},{2,30},{3,31},{4,24},{5,25},{6,26},{7,27},{8,20},{9,... | collective-permute-start | bytes 798728 | tf_op jit(solution)/shard_map/ppermute | solution.py:259
  55.4 2.0 %collective-permute-start.7 = (bf16[256,1024]{1,0:T(8,128)(2,1)S(1)}, bf16[256,1024]{1,0:T(8,128)(2,1)S(1)}, u32[]{:S(2)}, u32[]{:S(2)}) collective-permute-start(bf16[256,1024]{1,0:T(8,128)(2,1)S(1)} %pad_maximum_fusion), channel_id=1, source_target_pairs={{0,1},{1,0},{2,3},{3,2},{4,5},{5,4},{6,7},{7,6},{8,9},{9,8},{10,11... | collective-permute-start | bytes 1572872 | tf_op jit(solution)/shard_map/ppermute | solution.py:259
  55.6 5.4 %collective-permute-start.8 = (bf16[256,1024]{1,0:T(8,128)(2,1)S(1)}, bf16[256,1024]{1,0:T(8,128)(2,1)S(1)}, u32[]{:S(2)}, u32[]{:S(2)}) collective-permute-start(bf16[256,1024]{1,0:T(8,128)(2,1)S(1)} %pad_maximum_fusion.1), channel_id=1, source_target_pairs={{0,1},{1,0},{2,3},{3,2},{4,5},{5,4},{6,7},{7,6},{8,9},{9,8},{10,11... | collective-permute-start | bytes 1572872 | tf_op jit(solution)/shard_map/ppermute | solution.py:259
  57.5 8.0 %collective-permute-start.15 = (bf16[64,1024]{1,0:T(8,128)(2,1)S(1)}, bf16[64,1024]{1,0:T(8,128)(2,1)S(1)}, u32[]{:S(2)}, u32[]{:S(2)}) collective-permute-start(bf16[64,1024]{1,0:T(8,128)(2,1)S(1)} %get-tuple-element.70), channel_id=1, source_target_pairs={{0,8},{1,9},{2,10},{3,11},{4,12},{5,13},{6,14},{7,15},{8,0},{9,1},... | collective-permute-start | bytes 393224 | tf_op jit(solution)/shard_map/ppermute | solution.py:259
  60.3 6.8 %collective-permute-start.14 = (bf16[64,1024]{1,0:T(8,128)(2,1)S(1)}, bf16[64,1024]{1,0:T(8,128)(2,1)S(1)}, u32[]{:S(2)}, u32[]{:S(2)}) collective-permute-start(bf16[64,1024]{1,0:T(8,128)(2,1)S(1)} %get-tuple-element.71), channel_id=1, source_target_pairs={{0,4},{1,5},{2,6},{3,7},{4,0},{5,1},{6,2},{7,3},{8,12},{9,13},{10,... | collective-permute-start | bytes 393224 | tf_op jit(solution)/shard_map/ppermute | solution.py:259
  61.2 7.0 %collective-permute-start.13 = (bf16[64,1024]{1,0:T(8,128)(2,1)S(1)}, bf16[64,1024]{1,0:T(8,128)(2,1)S(1)}, u32[]{:S(2)}, u32[]{:S(2)}) collective-permute-start(bf16[64,1024]{1,0:T(8,128)(2,1)S(1)} %get-tuple-element.66), channel_id=1, source_target_pairs={{0,2},{1,3},{2,0},{3,1},{4,6},{5,7},{6,4},{7,5},{8,10},{9,11},{10,... | collective-permute-start | bytes 393224 | tf_op jit(solution)/shard_map/ppermute | solution.py:259
  62.7 7.3 %collective-permute-start.12 = (bf16[64,1024]{1,0:T(8,128)(2,1)S(1)}, bf16[64,1024]{1,0:T(8,128)(2,1)S(1)}, u32[]{:S(2)}, u32[]{:S(2)}) collective-permute-start(bf16[64,1024]{1,0:T(8,128)(2,1)S(1)} %get-tuple-element.69), channel_id=1, source_target_pairs={{0,12},{1,13},{2,14},{3,15},{4,8},{5,9},{6,10},{7,11},{8,4},{9,5},... | collective-permute-start | bytes 393224 | tf_op jit(solution)/shard_map/ppermute | solution.py:259
  63.6 8.6 %collective-permute-start.11 = (bf16[64,1024]{1,0:T(8,128)(2,1)S(1)}, bf16[64,1024]{1,0:T(8,128)(2,1)S(1)}, u32[]{:S(2)}, u32[]{:S(2)}) collective-permute-start(bf16[64,1024]{1,0:T(8,128)(2,1)S(1)} %get-tuple-element.67), channel_id=1, source_target_pairs={{0,10},{1,11},{2,8},{3,9},{4,14},{5,15},{6,12},{7,13},{8,2},{9,3},... | collective-permute-start | bytes 393224 | tf_op jit(solution)/shard_map/ppermute | solution.py:259
  65.5 10.1 %collective-permute-start.10 = (bf16[64,1024]{1,0:T(8,128)(2,1)S(1)}, bf16[64,1024]{1,0:T(8,128)(2,1)S(1)}, u32[]{:S(2)}, u32[]{:S(2)}) collective-permute-start(bf16[64,1024]{1,0:T(8,128)(2,1)S(1)} %get-tuple-element.68), channel_id=1, source_target_pairs={{0,6},{1,7},{2,4},{3,5},{4,2},{5,3},{6,0},{7,1},{8,14},{9,15},{10,... | collective-permute-start | bytes 393224 | tf_op jit(solution)/shard_map/ppermute | solution.py:259
  67.1 8.5 %collective-permute-start.9 = (bf16[64,1024]{1,0:T(8,128)(2,1)S(1)}, bf16[64,1024]{1,0:T(8,128)(2,1)S(1)}, u32[]{:S(2)}, u32[]{:S(2)}) collective-permute-start(bf16[64,1024]{1,0:T(8,128)(2,1)S(1)} %get-tuple-element.65), channel_id=1, source_target_pairs={{0,14},{1,15},{2,12},{3,13},{4,10},{5,11},{6,8},{7,9},{8,6},{9,7},... | collective-permute-start | bytes 393224 | tf_op jit(solution)/shard_map/ppermute | solution.py:259
  75.8 5.4 %collective-permute-start.16 = (bf16[32,1024]{1,0:T(8,128)(2,1)S(1)}, bf16[32,1024]{1,0:T(8,128)(2,1)S(1)}, u32[]{:S(2)}, u32[]{:S(2)}) collective-permute-start(bf16[32,1024]{1,0:T(8,128)(2,1)S(1)} %slice.67), channel_id=1, source_target_pairs={{0,16},{1,17},{2,18},{3,19},{4,20},{5,21},{6,22},{7,23},{8,24},{9,... | collective-permute-start | bytes 196616 | tf_op jit(solution)/shard_map/ppermute | solution.py:259

commit v4 on v3

v4 whole, which is shorter than its diff:
```python
import functools
import math

import jax
import jax.numpy as jnp
from jax import lax
from jax.experimental import pallas as pl
from jax.experimental.pallas import tpu as pltpu
from jax.sharding import PartitionSpec as P

NODE_DEV = 32
LANES = 128
EXTRA = 16
PAIRS = ((1, 2), (4, 3), (5, 6), (7, 0))
MIB = 1024 * 1024
VM = pl.BlockSpec(memory_space=pltpu.VMEM)
SM = pl.BlockSpec(memory_space=pltpu.SMEM)
HB = pl.BlockSpec(memory_space=pltpu.HBM)
F32 = jnp.float32
BF16 = jnp.bfloat16
I32 = jnp.int32


def write_blocks(labels, slots, slot, coded, normed, blocks):
    rows, width = normed.shape
    for label, block in zip(labels, blocks):
        at = lax.broadcasted_iota(I32, (slots, rows), 0) + label * slots
        pick = (slot == at).astype(BF16)
        picked = jnp.dot(pick, normed, preferred_element_type=F32).astype(BF16)
        for c in range(width // LANES):
            block[c * slots : (c + 1) * slots, :] = picked[:, c * LANES : (c + 1) * LANES]
        ids = lax.dot_general(coded, pick, (((1,), (1,)), ((), ())), preferred_element_type=F32)
        block[width // LANES * slots :, :slots] = ids.astype(BF16)


def pack_kernel(relations, slots, labels, place_ref, kinds_hbm, dest_hbm, feats_hbm, gain_hbm, *refs):
    blocks, (normed_ref, slot_ref, coded_ref), scratch = (
        refs[: len(labels)], refs[len(labels) : -6], refs[-6:],
    )
    kinds_ref, dest_ref, gain_ref, feats_ref, sems, feat_sems = scratch
    rows, width = feats_ref.shape
    part = rows // 4
    small = [
        pltpu.make_async_copy(kinds_hbm, kinds_ref, sems.at[0]),
        pltpu.make_async_copy(dest_hbm, dest_ref, sems.at[1]),
        pltpu.make_async_copy(gain_hbm, gain_ref, sems.at[2]),
    ]
    large = [
        pltpu.make_async_copy(
            feats_hbm.at[pl.ds(i * part, part), :], feats_ref.at[pl.ds(i * part, part), :], feat_sems.at[i]
        )
        for i in range(4)
    ]
    for copy in small + large:
        copy.start()
    before = (
        lax.broadcasted_iota(I32, (rows, rows), 0) < lax.broadcasted_iota(I32, (rows, rows), 1)
    ).astype(BF16)
    for copy in small:
        copy.wait()
    offset = kinds_ref[...] ^ place_ref[0]
    marks = offset == lax.broadcasted_iota(I32, (max(relations, 16), rows), 0)
    count = jnp.dot(marks.astype(BF16), before, preferred_element_type=F32)
    rank = jnp.sum(jnp.where(marks, count, 0.0), axis=0, keepdims=True).astype(I32)
    slot = offset * slots + rank
    slot_ref[...] = slot
    dest = dest_ref[...]
    line = lax.broadcasted_iota(I32, (EXTRA, rows), 0)
    coded = jnp.where(
        line == 0, dest // NODE_DEV, jnp.where(line == 1, dest % NODE_DEV, jnp.where(line == 2, 1, 0))
    ).astype(BF16)
    coded_ref[...] = coded
    gain = gain_ref[...]
    for i in range(4):
        large[i].wait()
        at = slice(i * part, (i + 1) * part)
        feats = feats_ref[at, :].astype(F32)
        scale = lax.rsqrt(jnp.mean(feats * feats, axis=1, keepdims=True) + 1e-06)
        normed_ref[at, :] = (feats * scale * gain).astype(BF16)
    write_blocks(labels, slots, slot, coded, normed_ref[...], blocks)


def pack_more_kernel(slots, labels, normed_ref, slot_ref, coded_ref, *refs):
    write_blocks(labels, slots, slot_ref[...], coded_ref[...], normed_ref[...], refs[-len(labels) :])


def pack_more(kept, labels, slots, after=()):
    rows, width = kept[0].shape
    block = jax.ShapeDtypeStruct((width // LANES * slots + EXTRA, LANES), BF16)
    return pl.pallas_call(
        functools.partial(pack_more_kernel, slots, labels),
        out_shape=[block] * len(labels),
        in_specs=[VM] * 3 + [HB] * len(after),
        out_specs=[VM] * len(labels),
        compiler_params=pltpu.CompilerParams(vmem_limit_bytes=16 * MIB),
        cost_estimate=pl.CostEstimate(flops=1, bytes_accessed=1, transcendentals=0),
        name="pack_more",
    )(*kept, *after)


def pack(place, kinds, dest, feats, gain, relations, slots, labels):
    rows, width = feats.shape
    block = jax.ShapeDtypeStruct((width // LANES * slots + EXTRA, LANES), BF16)
    shapes = [block] * len(labels) + [
        jax.ShapeDtypeStruct((rows, width), BF16),
        jax.ShapeDtypeStruct((1, rows), I32),
        jax.ShapeDtypeStruct((EXTRA, rows), BF16),
    ]
    outs = pl.pallas_call(
        functools.partial(pack_kernel, relations, slots, labels),
        out_shape=shapes,
        in_specs=[SM, HB, HB, HB, HB],
        out_specs=[VM] * len(shapes),
        scratch_shapes=[
            pltpu.VMEM((1, rows), I32),
            pltpu.VMEM((1, rows), I32),
            pltpu.VMEM((1, width), F32),
            pltpu.VMEM((rows, width), BF16),
            pltpu.SemaphoreType.DMA((3,)),
            pltpu.SemaphoreType.DMA((4,)),
        ],
        compiler_params=pltpu.CompilerParams(vmem_limit_bytes=16 * MIB),
        cost_estimate=pl.CostEstimate(flops=1, bytes_accessed=1, transcendentals=0),
        name="pack_far",
    )(place, *[pltpu.with_memory_space_constraint(a, pltpu.HBM) for a in (kinds, dest, feats, gain)])
    return outs[: len(labels)], outs[len(labels) :]


def gelu(x):
    return 0.5 * x * (1.0 + lax.erf(x * math.sqrt(0.5)))


def load_block(block_ref, x_ref, row, base, groups, relations):
    width = x_ref.shape[1]
    slots = (block_ref.shape[0] - EXTRA) * LANES // width
    for c in range(width // LANES):
        x_ref[row : row + slots, c * LANES : (c + 1) * LANES] = block_ref[c * slots : (c + 1) * slots, :]
    ids = block_ref[width // LANES * slots :, :slots].astype(F32).astype(I32)
    owner = ids[0:1] ^ base
    far = relations // 4
    y, z, f, g = owner % 2, owner // 2 % 2, owner // 4 % far, owner // relations
    at = (((((g % 2) * 2 + g // 2) * 2 + y) * 2 + z) * far + f) * NODE_DEV + ids[1:2]
    return jnp.where(ids[2:3] > 0, at, -1)


def up(x_ref, w_first_ref, hidden_ref):
    inner = w_first_ref.shape[1]
    part = 256

    def step(i, carry):
        at = pl.ds(pl.multiple_of(i * part, part), part)
        h = jnp.dot(x_ref[...], w_first_ref[:, at], preferred_element_type=F32)
        hidden_ref[:, at] = gelu(h).astype(BF16)
        return carry

    lax.fori_loop(0, inner // part, step, 0, unroll=8)


def down(hidden_ref, w_second_ref, table_ref, sums_ref, outs):
    part = 256
    width = w_second_ref.shape[1]
    piece = table_ref.shape[0] // len(outs)
    messages = [
        jnp.dot(hidden_ref[...], w_second_ref[:, at : at + part], preferred_element_type=F32).astype(BF16)
        for at in range(0, width, part)
    ]
    for i, message in enumerate(messages):
        columns = slice(i * part, (i + 1) * part)
        total = jnp.dot(table_ref[...], message, preferred_element_type=F32)
        if sums_ref is not None:
            total = total + sums_ref[:, columns]
        for b, out in enumerate(outs):
            out[:, columns] = total[b * piece : (b + 1) * piece].astype(out.dtype)


def expert_kernel(count, slots, groups, relations, has_sums, last, place_ref, *refs):
    blocks, refs = refs[:count], refs[count:]
    w_first_ref, w_second_ref, refs = refs[0], refs[1], refs[2:]
    sums_ref = None
    if has_sums:
        sums_ref, refs = refs[0], refs[1:]
    outs, (hidden_ref, table_ref, x_ref) = refs[:-3], refs[-3:]
    if not last:
        outs[-1][...] = jnp.zeros_like(outs[-1])
        outs = outs[:-1]
    nodes = table_ref.shape[0]
    for i in range(count):
        line = load_block(blocks[i], x_ref, i * slots, place_ref[1], groups, relations)
        table_ref[:, i * slots : (i + 1) * slots] = (
            line == lax.broadcasted_iota(I32, (nodes, slots), 0)
        ).astype(BF16)
    up(x_ref, w_first_ref, hidden_ref)
    down(hidden_ref, w_second_ref, table_ref, sums_ref, outs)


def expert(place, blocks, w_first, w_second, sums, groups, relations, last):
    count = len(blocks)
    width, inner = w_first.shape
    slots = (blocks[0].shape[0] - EXTRA) * LANES // width
    rows = count * slots
    nodes = groups * relations * NODE_DEV
    if last:
        shapes = [jax.ShapeDtypeStruct((nodes // 16, width), BF16)] * 16
    else:
        shapes = [jax.ShapeDtypeStruct((nodes, width), F32), jax.ShapeDtypeStruct((8, LANES), F32)]
    args = [place, *blocks, w_first, w_second] + ([] if sums is None else [sums])
    return pl.pallas_call(
        functools.partial(expert_kernel, count, slots, groups, relations, sums is not None, last),
        out_shape=shapes,
        in_specs=[SM] + [VM] * (len(args) - 1),
        out_specs=[VM] * len(shapes),
        scratch_shapes=[
            pltpu.VMEM((rows, inner), BF16), pltpu.VMEM((nodes, rows), BF16), pltpu.VMEM((rows, width), BF16),
        ],
        compiler_params=pltpu.CompilerParams(vmem_limit_bytes=(16 if relations <= 8 else 58) * MIB),
        cost_estimate=pl.CostEstimate(flops=1, bytes_accessed=1, transcendentals=0),
        name="expert",
    )(*args)


def local(edge_feats, gain, w_in, w_out, rel_type, dst_node):
    rows = edge_feats.shape[1]
    width = edge_feats.shape[2]
    relations = lax.axis_size("rel")
    groups = lax.axis_size("dom")
    slots = 2 * rows // relations
    half = relations // 2
    mine = lax.axis_index("rel")
    place = jnp.stack([mine, lax.axis_index("dom") * relations + mine]).astype(I32)

    def move(value, dom_bits, rel_bits):
        pairs = [
            (r * groups + g, (r ^ rel_bits) * groups + (g ^ dom_bits))
            for r in range(relations) for g in range(groups)
        ]
        return lax.ppermute(value, ("rel", "dom"), pairs)

    step = half // 4
    far = [list(range(half + k * step, half + (k + 1) * step)) for k in range(4)]
    first, kept = pack(
        place, rel_type.reshape(1, rows), dst_node, edge_feats[0], gain[None, :], relations, slots, far[0] + far[1]
    )
    held = {d: move(block, 0, d) for d, block in zip(far[0] + far[1], first)}
    near = pack_more(kept, list(range(half)), slots)
    held[0] = near[0]
    held.update({d: move(near[d], 0, d) for d in range(1, half)})

    def run(turn, sums, last=False):
        blocks = [held[d] for d in turn]
        return expert(place, blocks, w_in[0], w_out[0], sums, groups, relations, last)

    sums, token = run([0], None)
    for k in (2, 3):
        late = pack_more(kept, far[k], slots, [held[far[k - 2][-1]], token])
        held.update({d: move(block, 0, d) for d, block in zip(far[k], late)})
    for turn in (far[0] + [1], far[1] + list(range(2, half)), far[2]):
        sums, token = run(turn, sums)
    sums = run(far[3], sums, True)

    lines = sums[0].shape[0]
    away = {}
    for pair in PAIRS:
        got = move(jnp.concatenate([sums[8 + b] for b in pair]), 1, 0)
        away.update({b: got[i * lines : (i + 1) * lines] for i, b in enumerate(pair)})
    near = [sums[b].astype(F32) + away[b].astype(F32) for b in range(8)]
    total = near[0]
    for b in (7, 6, 5, 3, 4, 2, 1):
        total = total + move(near[b].astype(BF16), 2 * (b // 4), b // 2 % 2 + 2 * (b % 2)).astype(F32)
    total = total.reshape(relations // 4, NODE_DEV, -1)
    state = total[0]
    for f in range(relations // 4 - 1, 0, -1):
        state = state + move(total[f].astype(BF16), 0, 4 * f).astype(F32)
    return (state * (1.0 / math.sqrt(rows / NODE_DEV)))[None]


def solution(mesh):
    in_specs = (
        P("dom", "rel", None),
        P(),
        P("rel", None, None),
        P("rel", None, None),
        P("dom", "rel", None),
        P("dom", "rel"),
    )
    out_specs = P("dom", "rel", None)
    return jax.shard_map(local, mesh=mesh, in_specs=in_specs, out_specs=out_specs, check_vma=False)
```

time: 82.1 us -> 81.2 us (0.989)
  waiting for transfers between devices: 26.1 us -> 24.9 us
    ppermute x17 -> x19, waiting for transfers between devices: 26.1 us -> 24.9 us  [move(): return lax.ppermute(value, ('rel', 'dom'), pairs)]
    ppermute x17 -> x19, starting transfers between devices: 28.3 us -> 29.1 us  [move(): return lax.ppermute(value, ('rel', 'dom'), pairs)]
  transfers between devices with their start and end apart: 17 -> 19, of which waited for: 8 -> 8; matrix products, arithmetic and copies ran while one was open for 0% -> 0% of each run, Pallas kernels for 19% -> 19%
where the time goes in v4:
time: 81.2 us; the launch traced here: 81 us
  starting transfers between devices  29.1 us (36%)
  waiting for transfers between devices  24.9 us (31%)
  Pallas kernels  21.1 us (26%)
  local copies, waits for them, and re-layouts  4.39 us (5%)
  other arithmetic  1.24 us (2%)
    ppermute x19, starting transfers between devices, move(): return lax.ppermute(value, ('rel', 'dom'), pairs)  29.1 us
    ppermute x19, waiting for transfers between devices, move(): return lax.ppermute(value, ('rel', 'dom'), pairs)  24.9 us
    pallas_call x5, Pallas kernels, expert(): pl.pallas_call(functools.partial(expert_kernel, count, slots, groups, rel...  16.8 us
    unnamed x8, local copies, waits for them, and re-layouts  4.38 us
    pallas_call x1, Pallas kernels, pack(): pl.pallas_call(functools.partial(pack_kernel, relations, slots, labels),...  2.85 us
  transfers between devices with their start and end apart: 19, of which 8 were waited for; matrix products, arithmetic and copies ran while one was open for 0% of the time, Pallas kernels for 19%

profile of v4, /device:TPU:0, one launch (start us, length us, event | category | flops | bytes accessed | tf_op | source)
XLA Modules:
  0.0 81.0 jit_solution(17503007509691455906)
XLA Ops:
  0.1 2.8 %pack_far.1 = (bf16[1040,128]{1,0:T(8,128)(2,1)S(1)}, bf16[1040,128]{1,0:T(8,128)(2,1)S(1)}, bf16[512,1024]{1,0:T(8,128)(2,1)S(1)}, s32[1,512]{1,0:T(1,128)S(1)}, bf16[16,512]{1,0:T(8,128)(2,1)S(1)}) custom-call(s32[2]{0:T(128)S(1)} %pad_add_fusion.place_ref, s32[1,512]{1,0:T(1,128)} %bitcast.21, s32[1,512]{1,0:T(1,128)} %dest_hbm.1, ...), custom_call_target="tpu_custom_call" | custom-call | flops 1 | bytes 1 | tf_op jit(solution)/shard_map/pack_far/pallas_call | solution.py:109
  2.9 4.1 %collective-permute-start.2 = (bf16[1040,128]{1,0:T(8,128)(2,1)S(1)}, bf16[1040,128]{1,0:T(8,128)(2,1)S(1)}, u32[]{:S(2)}, u32[]{:S(2)}) collective-permute-start(bf16[1040,128]{1,0:T(8,128)(2,1)S(1)} %get-tuple-element.41), channel_id=1, source_target_pairs={{0,16},{1,17},{2,18},{3,19},{4,20},{5,21},{6,22},{7,23},{8,24},{9,... | collective-permute-start | bytes 798728 | tf_op jit(solution)/shard_map/ppermute | solution.py:236
  9.2 1.7 %collective-permute-start.4 = (bf16[1040,128]{1,0:T(8,128)(2,1)S(1)}, bf16[1040,128]{1,0:T(8,128)(2,1)S(1)}, u32[]{:S(2)}, u32[]{:S(2)}) collective-permute-start(bf16[1040,128]{1,0:T(8,128)(2,1)S(1)} %get-tuple-element.42), channel_id=1, source_target_pairs={{0,8},{1,9},{2,10},{3,11},{4,12},{5,13},{6,14},{7,15},{8,0},{9,1},... | collective-permute-start | bytes 798728 | tf_op jit(solution)/shard_map/ppermute | solution.py:236
  11.0 1.8 %collective-permute-start.6 = (bf16[1040,128]{1,0:T(8,128)(2,1)S(1)}, bf16[1040,128]{1,0:T(8,128)(2,1)S(1)}, u32[]{:S(2)}, u32[]{:S(2)}) collective-permute-start(bf16[1040,128]{1,0:T(8,128)(2,1)S(1)} %get-tuple-element.44), channel_id=1, source_target_pairs={{0,4},{1,5},{2,6},{3,7},{4,0},{5,1},{6,2},{7,3},{8,12},{9,13},{10,... | collective-permute-start | bytes 798728 | tf_op jit(solution)/shard_map/ppermute | solution.py:236
  12.8 2.2 %copy-done = bf16[1,1024,2048]{2,1,0:T(8,128)(2,1)S(1)} copy-done((bf16[1,1024,2048]{2,1,0:T(8,128)(2,1)S(1)}, bf16[1,1024,2048]{2,1,0:T(8,128)(2,1)}, u32[]{:S(2)}) %copy-start) | copy-done | bytes 4194328
  15.0 2.2 %copy-done.2 = bf16[1,2048,1024]{2,1,0:T(8,128)(2,1)S(1)} copy-done((bf16[1,2048,1024]{2,1,0:T(8,128)(2,1)S(1)}, bf16[1,2048,1024]{2,1,0:T(8,128)(2,1)}, u32[]{:S(2)}) %copy-start.2) | copy-done | bytes 4194328
  17.1 2.5 %expert.5 = (f32[1024,1024]{1,0:T(8,128)S(1)}, f32[8,128]{1,0:T(8,128)S(1)}) custom-call(s32[2]{0:T(128)S(1)} %pad_add_fusion.place_ref, bf16[1040,128]{1,0:T(8,128)(2,1)S(1)} %get-tuple-element.39.refs_0_, bf16[1024,2048]{1,0:T(8,128)(2,1)S(1)} %bitcast.9, bf16[2048,1024]{1,0:T(8,128)(2,1)S(1)} %bitcast.14), custom_call_target="tpu_custom_call" | custom-call | flops 1 | bytes 1 | tf_op jit(solution)/shard_map/expert/pallas_call | solution.py:207
  19.7 6.1 %collective-permute-done.2.refs_0_ = bf16[1040,128]{1,0:T(8,128)(2,1)S(1)} collective-permute-done((bf16[1040,128]{1,0:T(8,128)(2,1)S(1)}, bf16[1040,128]{1,0:T(8,128)(2,1)S(1)}, u32[]{:S(2)}, u32[]{:S(2)}) %collective-permute-start.2) | collective-permute-done | bytes 266272 | tf_op jit(solution)/shard_map/ppermute | solution.py:236
  26.1 2.9 %collective-permute-start.3 = (bf16[1040,128]{1,0:T(8,128)(2,1)S(1)}, bf16[1040,128]{1,0:T(8,128)(2,1)S(1)}, u32[]{:S(2)}, u32[]{:S(2)}) collective-permute-start(bf16[1040,128]{1,0:T(8,128)(2,1)S(1)} %pack_more.5), channel_id=1, source_target_pairs={{0,24},{1,25},{2,26},{3,27},{4,28},{5,29},{6,30},{7,31},{8,16},{9,... | collective-permute-start | bytes 798728 | tf_op jit(solution)/shard_map/ppermute | solution.py:236
  29.0 4.9 %collective-permute-done.refs_0_ = bf16[1040,128]{1,0:T(8,128)(2,1)S(1)} collective-permute-done((bf16[1040,128]{1,0:T(8,128)(2,1)S(1)}, bf16[1040,128]{1,0:T(8,128)(2,1)S(1)}, u32[]{:S(2)}, u32[]{:S(2)}) %collective-permute-start) | collective-permute-done | bytes 266272 | tf_op jit(solution)/shard_map/ppermute | solution.py:236
  34.2 2.2 %collective-permute-start.1 = (bf16[1040,128]{1,0:T(8,128)(2,1)S(1)}, bf16[1040,128]{1,0:T(8,128)(2,1)S(1)}, u32[]{:S(2)}, u32[]{:S(2)}) collective-permute-start(bf16[1040,128]{1,0:T(8,128)(2,1)S(1)} %pack_more.4), channel_id=1, source_target_pairs={{0,28},{1,29},{2,30},{3,31},{4,24},{5,25},{6,26},{7,27},{8,20},{9,... | collective-permute-start | bytes 798728 | tf_op jit(solution)/shard_map/ppermute | solution.py:236
  36.4 3.7 %expert.6 = (f32[1024,1024]{1,0:T(8,128)S(1)}, f32[8,128]{1,0:T(8,128)}) custom-call(s32[2]{0:T(128)S(1)} %pad_add_fusion.place_ref, bf16[1040,128]{1,0:T(8,128)(2,1)S(1)} %collective-permute-done.2.refs_0_, bf16[1040,128]{1,0:T(8,128)(2,1)S(1)} %collective-permute-done.6.refs_1_, bf16[1024,2048]{1,0:T(8,128)(2,1)S(1)} %bitcast.10, ...), custom_call_target="tpu_custom_call" | custom-call | flops 1 | bytes 1 | tf_op jit(solution)/shard_map/expert/pallas_call | solution.py:207
  40.1 4.1 %collective-permute-done.5.refs_2_ = bf16[1040,128]{1,0:T(8,128)(2,1)S(1)} collective-permute-done((bf16[1040,128]{1,0:T(8,128)(2,1)S(1)}, bf16[1040,128]{1,0:T(8,128)(2,1)S(1)}, u32[]{:S(2)}, u32[]{:S(2)}) %collective-permute-start.5) | collective-permute-done | bytes 266272 | tf_op jit(solution)/shard_map/ppermute | solution.py:236
  44.3 5.2 %expert.7 = (f32[1024,1024]{1,0:T(8,128)S(1)}, f32[8,128]{1,0:T(8,128)}) custom-call(s32[2]{0:T(128)S(1)} %pad_add_fusion.place_ref, bf16[1040,128]{1,0:T(8,128)(2,1)S(1)} %collective-permute-done.refs_0_, bf16[1040,128]{1,0:T(8,128)(2,1)S(1)} %collective-permute-done.4.refs_1_, bf16[1040,128]{1,0:T(8,128)(2,1)S(1)} %collective-permute-done.5.refs_2_, ...), custom_call_target="tpu_custom_call" | custom-call | flops 1 | bytes 1 | tf_op jit(solution)/shard_map/expert/pallas_call | solution.py:207
  49.5 2.8 %expert.8 = (f32[1024,1024]{1,0:T(8,128)S(1)}, f32[8,128]{1,0:T(8,128)}) custom-call(s32[2]{0:T(128)S(1)} %pad_add_fusion.place_ref, bf16[1040,128]{1,0:T(8,128)(2,1)S(1)} %collective-permute-done.3.refs_0_, bf16[1024,2048]{1,0:T(8,128)(2,1)S(1)} %bitcast.12, bf16[2048,1024]{1,0:T(8,128)(2,1)S(1)} %bitcast.17, f32[1024,1024]{1,0:T(8,128)S(1)} %get-tuple-element.47.refs_3_), custom_call_target="tpu_custom_call" | custom-call | flops 1 | bytes 1 | tf_op jit(solution)/shard_map/expert/pallas_call | solution.py:207
  52.3 2.6 %expert.9 = (bf16[64,1024]{1,0:T(8,128)(2,1)S(1)}, bf16[64,1024]{1,0:T(8,128)(2,1)S(1)}, bf16[64,1024]{1,0:T(8,128)(2,1)S(1)}, bf16[64,1024]{1,0:T(8,128)(2,1)S(...) custom-call(s32[2]{0:T(128)S(1)} %pad_add_fusion.place_ref, ...), custom_call_target="tpu_custom_call" | custom-call | flops 1 | bytes 1 | tf_op jit(solution)/shard_map/expert/pallas_call | solution.py:207
  56.5 2.8 %collective-permute-start.17 = (bf16[64,1024]{1,0:T(8,128)(2,1)S(1)}, bf16[64,1024]{1,0:T(8,128)(2,1)S(1)}, u32[]{:S(2)}, u32[]{:S(2)}) collective-permute-start(bf16[64,1024]{1,0:T(8,128)(2,1)S(1)} %get-tuple-element.70), channel_id=1, source_target_pairs={{0,8},{1,9},{2,10},{3,11},{4,12},{5,13},{6,14},{7,15},{8,0},{9,1},... | collective-permute-start | bytes 393224 | tf_op jit(solution)/shard_map/ppermute | solution.py:236
  62.6 2.0 %collective-permute-start.11 = (bf16[64,1024]{1,0:T(8,128)(2,1)S(1)}, bf16[64,1024]{1,0:T(8,128)(2,1)S(1)}, u32[]{:S(2)}, u32[]{:S(2)}) collective-permute-start(bf16[64,1024]{1,0:T(8,128)(2,1)S(1)} %get-tuple-element.66), channel_id=1, source_target_pairs={{0,10},{1,11},{2,8},{3,9},{4,14},{5,15},{6,12},{7,13},{8,2},{9,3},... | collective-permute-start | bytes 393224 | tf_op jit(solution)/shard_map/ppermute | solution.py:236
  64.6 1.7 %collective-permute-start.10 = (bf16[64,1024]{1,0:T(8,128)(2,1)S(1)}, bf16[64,1024]{1,0:T(8,128)(2,1)S(1)}, u32[]{:S(2)}, u32[]{:S(2)}) collective-permute-start(bf16[64,1024]{1,0:T(8,128)(2,1)S(1)} %get-tuple-element.65), channel_id=1, source_target_pairs={{0,6},{1,7},{2,4},{3,5},{4,2},{5,3},{6,0},{7,1},{8,14},{9,15},{10,... | collective-permute-start | bytes 393224 | tf_op jit(solution)/shard_map/ppermute | solution.py:236
  67.4 1.6 %collective-permute-done.13 = bf16[64,1024]{1,0:T(8,128)(2,1)S(1)} collective-permute-done((bf16[64,1024]{1,0:T(8,128)(2,1)S(1)}, bf16[64,1024]{1,0:T(8,128)(2,1)S(1)}, u32[]{:S(2)}, u32[]{:S(2)}) %collective-permute-start.13) | collective-permute-done | bytes 131104 | tf_op jit(solution)/shard_map/ppermute | solution.py:236
  69.0 1.9 %collective-permute-done.11 = bf16[64,1024]{1,0:T(8,128)(2,1)S(1)} collective-permute-done((bf16[64,1024]{1,0:T(8,128)(2,1)S(1)}, bf16[64,1024]{1,0:T(8,128)(2,1)S(1)}, u32[]{:S(2)}, u32[]{:S(2)}) %collective-permute-start.11) | collective-permute-done | bytes 131104 | tf_op jit(solution)/shard_map/ppermute | solution.py:236
  70.9 3.7 %collective-permute-done.10 = bf16[64,1024]{1,0:T(8,128)(2,1)S(1)} collective-permute-done((bf16[64,1024]{1,0:T(8,128)(2,1)S(1)}, bf16[64,1024]{1,0:T(8,128)(2,1)S(1)}, u32[]{:S(2)}, u32[]{:S(2)}) %collective-permute-start.10) | collective-permute-done | bytes 131104 | tf_op jit(solution)/shard_map/ppermute | solution.py:236
  74.9 3.2 %collective-permute-start.18 = (bf16[32,1024]{1,0:T(8,128)(2,1)S(1)}, bf16[32,1024]{1,0:T(8,128)(2,1)S(1)}, u32[]{:S(2)}, u32[]{:S(2)}) collective-permute-start(bf16[32,1024]{1,0:T(8,128)(2,1)S(1)} %slice.67), channel_id=1, source_target_pairs={{0,16},{1,17},{2,18},{3,19},{4,20},{5,21},{6,22},{7,23},{8,24},{9,... | collective-permute-start | bytes 196616 | tf_op jit(solution)/shard_map/ppermute | solution.py:236
  78.1 2.2 %collective-permute-done.18 = bf16[32,1024]{1,0:T(8,128)(2,1)S(1)} collective-permute-done((bf16[32,1024]{1,0:T(8,128)(2,1)S(1)}, bf16[32,1024]{1,0:T(8,128)(2,1)S(1)}, u32[]{:S(2)}, u32[]{:S(2)}) %collective-permute-start.18) | collective-permute-done | bytes 65568 | tf_op jit(solution)/shard_map/ppermute | solution.py:236
  (43 shorter events, 9.9 us)
Async XLA Ops:
  2.9 22.8 %collective-permute-start.2 = (bf16[1040,128]{1,0:T(8,128)(2,1)S(1)}, bf16[1040,128]{1,0:T(8,128)(2,1)S(1)}, u32[]{:S(2)}, u32[]{:S(2)}) collective-permute-start(bf16[1040,128]{1,0:T(8,128)(2,1)S(1)} %get-tuple-element.41), channel_id=1, source_target_pairs={{0,16},{1,17},{2,18},{3,19},{4,20},{5,21},{6,22},{7,23},{8,24},{9,... | collective-permute-start | bytes 798728 | tf_op jit(solution)/shard_map/ppermute | solution.py:236
  7.0 26.8 %collective-permute-start = (bf16[1040,128]{1,0:T(8,128)(2,1)S(1)}, bf16[1040,128]{1,0:T(8,128)(2,1)S(1)}, u32[]{:S(2)}, u32[]{:S(2)}) collective-permute-start(bf16[1040,128]{1,0:T(8,128)(2,1)S(1)} %get-tuple-element.38), channel_id=1, source_target_pairs={{0,20},{1,21},{2,22},{3,23},{4,16},{5,17},{6,18},{7,19},{8,28},{9,... | collective-permute-start | bytes 798728 | tf_op jit(solution)/shard_map/ppermute | solution.py:236
  9.2 30.9 %collective-permute-start.4 = (bf16[1040,128]{1,0:T(8,128)(2,1)S(1)}, bf16[1040,128]{1,0:T(8,128)(2,1)S(1)}, u32[]{:S(2)}, u32[]{:S(2)}) collective-permute-start(bf16[1040,128]{1,0:T(8,128)(2,1)S(1)} %get-tuple-element.42), channel_id=1, source_target_pairs={{0,8},{1,9},{2,10},{3,11},{4,12},{5,13},{6,14},{7,15},{8,0},{9,1},... | collective-permute-start | bytes 798728 | tf_op jit(solution)/shard_map/ppermute | solution.py:236
  10.9 33.4 %collective-permute-start.5 = (bf16[1040,128]{1,0:T(8,128)(2,1)S(1)}, bf16[1040,128]{1,0:T(8,128)(2,1)S(1)}, u32[]{:S(2)}, u32[]{:S(2)}) collective-permute-start(bf16[1040,128]{1,0:T(8,128)(2,1)S(1)} %get-tuple-element.43), channel_id=1, source_target_pairs={{0,12},{1,13},{2,14},{3,15},{4,8},{5,9},{6,10},{7,11},{8,4},{9,5},... | collective-permute-start | bytes 798728 | tf_op jit(solution)/shard_map/ppermute | solution.py:236
  11.0 25.4 %collective-permute-start.6 = (bf16[1040,128]{1,0:T(8,128)(2,1)S(1)}, bf16[1040,128]{1,0:T(8,128)(2,1)S(1)}, u32[]{:S(2)}, u32[]{:S(2)}) collective-permute-start(bf16[1040,128]{1,0:T(8,128)(2,1)S(1)} %get-tuple-element.44), channel_id=1, source_target_pairs={{0,4},{1,5},{2,6},{3,7},{4,0},{5,1},{6,2},{7,3},{8,12},{9,13},{10,... | collective-permute-start | bytes 798728 | tf_op jit(solution)/shard_map/ppermute | solution.py:236
  12.8 2.2 %copy-start = (bf16[1,1024,2048]{2,1,0:T(8,128)(2,1)S(1)}, bf16[1,1024,2048]{2,1,0:T(8,128)(2,1)}, u32[]{:S(2)}) copy-start(bf16[1,1024,2048]{2,1,0:T(8,128)(2,1)} %param.8) | copy-start | bytes 12582916
  14.9 2.2 %copy-start.2 = (bf16[1,2048,1024]{2,1,0:T(8,128)(2,1)S(1)}, bf16[1,2048,1024]{2,1,0:T(8,128)(2,1)}, u32[]{:S(2)}) copy-start(bf16[1,2048,1024]{2,1,0:T(8,128)(2,1)} %param.9) | copy-start | bytes 12582916
  17.1 19.3 %copy-start.1 = (bf16[1,1024,2048]{2,1,0:T(8,128)(2,1)S(1)}, bf16[1,1024,2048]{2,1,0:T(8,128)(2,1)}, u32[]{:S(2)}) copy-start(bf16[1,1024,2048]{2,1,0:T(8,128)(2,1)} %param.8) | copy-start | bytes 12582916
  17.1 19.3 %copy-start.3 = (bf16[1,2048,1024]{2,1,0:T(8,128)(2,1)S(1)}, bf16[1,2048,1024]{2,1,0:T(8,128)(2,1)}, u32[]{:S(2)}) copy-start(bf16[1,2048,1024]{2,1,0:T(8,128)(2,1)} %param.9) | copy-start | bytes 12582916
  26.1 23.4 %collective-permute-start.3 = (bf16[1040,128]{1,0:T(8,128)(2,1)S(1)}, bf16[1040,128]{1,0:T(8,128)(2,1)S(1)}, u32[]{:S(2)}, u32[]{:S(2)}) collective-permute-start(bf16[1040,128]{1,0:T(8,128)(2,1)S(1)} %pack_more.5), channel_id=1, source_target_pairs={{0,24},{1,25},{2,26},{3,27},{4,28},{5,29},{6,30},{7,31},{8,16},{9,... | collective-permute-start | bytes 798728 | tf_op jit(solution)/shard_map/ppermute | solution.py:236
  34.2 18.1 %collective-permute-start.1 = (bf16[1040,128]{1,0:T(8,128)(2,1)S(1)}, bf16[1040,128]{1,0:T(8,128)(2,1)S(1)}, u32[]{:S(2)}, u32[]{:S(2)}) collective-permute-start(bf16[1040,128]{1,0:T(8,128)(2,1)S(1)} %pack_more.4), channel_id=1, source_target_pairs={{0,28},{1,29},{2,30},{3,31},{4,24},{5,25},{6,26},{7,27},{8,20},{9,... | collective-permute-start | bytes 798728 | tf_op jit(solution)/shard_map/ppermute | solution.py:236
  54.9 1.6 %collective-permute-start.15 = (bf16[128,1024]{1,0:T(8,128)(2,1)S(1)}, bf16[128,1024]{1,0:T(8,128)(2,1)S(1)}, u32[]{:S(2)}, u32[]{:S(2)}) collective-permute-start(bf16[128,1024]{1,0:T(8,128)(2,1)S(1)} %pad_maximum_fusion.3), channel_id=1, source_target_pairs={{0,1},{1,0},{2,3},{3,2},{4,5},{5,4},{6,7},{7,6},{8,9},{9,8},{10,11... | collective-permute-start | bytes 786440 | tf_op jit(solution)/shard_map/ppermute | solution.py:236
  55.0 5.0 %collective-permute-start.12 = (bf16[128,1024]{1,0:T(8,128)(2,1)S(1)}, bf16[128,1024]{1,0:T(8,128)(2,1)S(1)}, u32[]{:S(2)}, u32[]{:S(2)}) collective-permute-start(bf16[128,1024]{1,0:T(8,128)(2,1)S(1)} %pad_maximum_fusion.2), channel_id=1, source_target_pairs={{0,1},{1,0},{2,3},{3,2},{4,5},{5,4},{6,7},{7,6},{8,9},{9,8},{10,11... | collective-permute-start | bytes 786440 | tf_op jit(solution)/shard_map/ppermute | solution.py:236
  55.6 6.1 %collective-permute-start.9 = (bf16[128,1024]{1,0:T(8,128)(2,1)S(1)}, bf16[128,1024]{1,0:T(8,128)(2,1)S(1)}, u32[]{:S(2)}, u32[]{:S(2)}) collective-permute-start(bf16[128,1024]{1,0:T(8,128)(2,1)S(1)} %pad_maximum_fusion.1), channel_id=1, source_target_pairs={{0,1},{1,0},{2,3},{3,2},{4,5},{5,4},{6,7},{7,6},{8,9},{9,8},{10,11... | collective-permute-start | bytes 786440 | tf_op jit(solution)/shard_map/ppermute | solution.py:236
  55.7 6.9 %collective-permute-start.7 = (bf16[128,1024]{1,0:T(8,128)(2,1)S(1)}, bf16[128,1024]{1,0:T(8,128)(2,1)S(1)}, u32[]{:S(2)}, u32[]{:S(2)}) collective-permute-start(bf16[128,1024]{1,0:T(8,128)(2,1)S(1)} %pad_maximum_fusion), channel_id=1, source_target_pairs={{0,1},{1,0},{2,3},{3,2},{4,5},{5,4},{6,7},{7,6},{8,9},{9,8},{10,11... | collective-permute-start | bytes 786440 | tf_op jit(solution)/shard_map/ppermute | solution.py:236
  56.5 8.1 %collective-permute-start.17 = (bf16[64,1024]{1,0:T(8,128)(2,1)S(1)}, bf16[64,1024]{1,0:T(8,128)(2,1)S(1)}, u32[]{:S(2)}, u32[]{:S(2)}) collective-permute-start(bf16[64,1024]{1,0:T(8,128)(2,1)S(1)} %get-tuple-element.70), channel_id=1, source_target_pairs={{0,8},{1,9},{2,10},{3,11},{4,12},{5,13},{6,14},{7,15},{8,0},{9,1},... | collective-permute-start | bytes 393224 | tf_op jit(solution)/shard_map/ppermute | solution.py:236
  59.3 7.0 %collective-permute-start.16 = (bf16[64,1024]{1,0:T(8,128)(2,1)S(1)}, bf16[64,1024]{1,0:T(8,128)(2,1)S(1)}, u32[]{:S(2)}, u32[]{:S(2)}) collective-permute-start(bf16[64,1024]{1,0:T(8,128)(2,1)S(1)} %get-tuple-element.69), channel_id=1, source_target_pairs={{0,4},{1,5},{2,6},{3,7},{4,0},{5,1},{6,2},{7,3},{8,12},{9,13},{10,... | collective-permute-start | bytes 393224 | tf_op jit(solution)/shard_map/ppermute | solution.py:236
  60.1 7.3 %collective-permute-start.14 = (bf16[64,1024]{1,0:T(8,128)(2,1)S(1)}, bf16[64,1024]{1,0:T(8,128)(2,1)S(1)}, u32[]{:S(2)}, u32[]{:S(2)}) collective-permute-start(bf16[64,1024]{1,0:T(8,128)(2,1)S(1)} %get-tuple-element.68), channel_id=1, source_target_pairs={{0,2},{1,3},{2,0},{3,1},{4,6},{5,7},{6,4},{7,5},{8,10},{9,11},{10,... | collective-permute-start | bytes 393224 | tf_op jit(solution)/shard_map/ppermute | solution.py:236
  61.6 7.3 %collective-permute-start.13 = (bf16[64,1024]{1,0:T(8,128)(2,1)S(1)}, bf16[64,1024]{1,0:T(8,128)(2,1)S(1)}, u32[]{:S(2)}, u32[]{:S(2)}) collective-permute-start(bf16[64,1024]{1,0:T(8,128)(2,1)S(1)} %get-tuple-element.67), channel_id=1, source_target_pairs={{0,12},{1,13},{2,14},{3,15},{4,8},{5,9},{6,10},{7,11},{8,4},{9,5},... | collective-permute-start | bytes 393224 | tf_op jit(solution)/shard_map/ppermute | solution.py:236
  62.6 8.3 %collective-permute-start.11 = (bf16[64,1024]{1,0:T(8,128)(2,1)S(1)}, bf16[64,1024]{1,0:T(8,128)(2,1)S(1)}, u32[]{:S(2)}, u32[]{:S(2)}) collective-permute-start(bf16[64,1024]{1,0:T(8,128)(2,1)S(1)} %get-tuple-element.66), channel_id=1, source_target_pairs={{0,10},{1,11},{2,8},{3,9},{4,14},{5,15},{6,12},{7,13},{8,2},{9,3},... | collective-permute-start | bytes 393224 | tf_op jit(solution)/shard_map/ppermute | solution.py:236
  64.6 10.0 %collective-permute-start.10 = (bf16[64,1024]{1,0:T(8,128)(2,1)S(1)}, bf16[64,1024]{1,0:T(8,128)(2,1)S(1)}, u32[]{:S(2)}, u32[]{:S(2)}) collective-permute-start(bf16[64,1024]{1,0:T(8,128)(2,1)S(1)} %get-tuple-element.65), channel_id=1, source_target_pairs={{0,6},{1,7},{2,4},{3,5},{4,2},{5,3},{6,0},{7,1},{8,14},{9,15},{10,... | collective-permute-start | bytes 393224 | tf_op jit(solution)/shard_map/ppermute | solution.py:236
  66.3 8.4 %collective-permute-start.8 = (bf16[64,1024]{1,0:T(8,128)(2,1)S(1)}, bf16[64,1024]{1,0:T(8,128)(2,1)S(1)}, u32[]{:S(2)}, u32[]{:S(2)}) collective-permute-start(bf16[64,1024]{1,0:T(8,128)(2,1)S(1)} %add_convert_fusion.6), channel_id=1, source_target_pairs={{0,14},{1,15},{2,12},{3,13},{4,10},{5,11},{6,8},{7,9},{8,6},{9,7},... | collective-permute-start | bytes 393224 | tf_op jit(solution)/shard_map/ppermute | solution.py:236
  74.9 5.4 %collective-permute-start.18 = (bf16[32,1024]{1,0:T(8,128)(2,1)S(1)}, bf16[32,1024]{1,0:T(8,128)(2,1)S(1)}, u32[]{:S(2)}, u32[]{:S(2)}) collective-permute-start(bf16[32,1024]{1,0:T(8,128)(2,1)S(1)} %slice.67), channel_id=1, source_target_pairs={{0,16},{1,17},{2,18},{3,19},{4,20},{5,21},{6,22},{7,23},{8,24},{9,... | collective-permute-start | bytes 196616 | tf_op jit(solution)/shard_map/ppermute | solution.py:236

commit v5 on v4

--- a/solution.py
+++ b/solution.py
@@ -39,7 +39,8 @@
     )
     kinds_ref, dest_ref, gain_ref, feats_ref, sems, feat_sems = scratch
     rows, width = feats_ref.shape
-    part = rows // 4
+    parts = 2
+    part = rows // parts
     small = [
         pltpu.make_async_copy(kinds_hbm, kinds_ref, sems.at[0]),
         pltpu.make_async_copy(dest_hbm, dest_ref, sems.at[1]),
@@ -49,7 +50,7 @@
         pltpu.make_async_copy(
             feats_hbm.at[pl.ds(i * part, part), :], feats_ref.at[pl.ds(i * part, part), :], feat_sems.at[i]
         )
-        for i in range(4)
+        for i in range(parts)
     ]
     for copy in small + large:
         copy.start()
@@ -71,7 +72,7 @@
     ).astype(BF16)
     coded_ref[...] = coded
     gain = gain_ref[...]
-    for i in range(4):
+    for i in range(parts):
         large[i].wait()
         at = slice(i * part, (i + 1) * part)
         feats = feats_ref[at, :].astype(F32)
@@ -117,7 +118,7 @@
             pltpu.VMEM((1, width), F32),
             pltpu.VMEM((rows, width), BF16),
             pltpu.SemaphoreType.DMA((3,)),
-            pltpu.SemaphoreType.DMA((4,)),
+            pltpu.SemaphoreType.DMA((2,)),
         ],
         compiler_params=pltpu.CompilerParams(vmem_limit_bytes=16 * MIB),
         cost_estimate=pl.CostEstimate(flops=1, bytes_accessed=1, transcendentals=0),
@@ -237,13 +238,12 @@
 
     step = half // 4
     far = [list(range(half + k * step, half + (k + 1) * step)) for k in range(4)]
+    early, rest = far[0], list(range(half)) + far[1]
     first, kept = pack(
-        place, rel_type.reshape(1, rows), dst_node, edge_feats[0], gain[None, :], relations, slots, far[0] + far[1]
+        place, rel_type.reshape(1, rows), dst_node, edge_feats[0], gain[None, :], relations, slots, early
     )
-    held = {d: move(block, 0, d) for d, block in zip(far[0] + far[1], first)}
-    near = pack_more(kept, list(range(half)), slots)
-    held[0] = near[0]
-    held.update({d: move(near[d], 0, d) for d in range(1, half)})
+    held = {d: move(block, 0, d) for d, block in zip(early, first)}
+    held.update({d: move(block, 0, d) if d else block for d, block in zip(rest, pack_more(kept, rest, slots))})
 
     def run(turn, sums, last=False):
         blocks = [held[d] for d in turn]

time: 81.2 us -> 80.7 us (level)
  transfers between devices with their start and end apart: 19 -> 19, of which waited for: 8 -> 8; matrix products, arithmetic and copies ran while one was open for 0% -> 0% of each run, Pallas kernels for 19% -> 20%
where the time goes in v5:
time: 80.7 us; the launch traced here: 80.5 us
  starting transfers between devices  28.9 us (36%)
  waiting for transfers between devices  25 us (31%)
  Pallas kernels  20.8 us (26%)
  local copies, waits for them, and re-layouts  4.39 us (5%)
  other arithmetic  1.24 us (2%)
    ppermute x19, starting transfers between devices, move(): return lax.ppermute(value, ('rel', 'dom'), pairs)  28.9 us
    ppermute x19, waiting for transfers between devices, move(): return lax.ppermute(value, ('rel', 'dom'), pairs)  25 us
    pallas_call x5, Pallas kernels, expert(): pl.pallas_call(functools.partial(expert_kernel, count, slots, groups, rel...  16.7 us
    unnamed x8, local copies, waits for them, and re-layouts  4.38 us
    pallas_call x1, Pallas kernels, pack(): pl.pallas_call(functools.partial(pack_kernel, relations, slots, labels),...  2.39 us
    pallas_call x3, Pallas kernels, pack_more(): pl.pallas_call(functools.partial(pack_more_kernel, slots, labels), out_sh...  1.65 us
  transfers between devices with their start and end apart: 19, of which 8 were waited for; matrix products, arithmetic and copies ran while one was open for 0% of the time, Pallas kernels for 20%

profile of v5, /device:TPU:0, one launch (start us, length us, event | category | flops | bytes accessed | tf_op | source)
XLA Modules:
  0.0 80.5 jit_solution(12065028975264500178)
XLA Ops:
  0.1 2.4 %pack_far.1 = (bf16[1040,128]{1,0:T(8,128)(2,1)S(1)}, bf16[512,1024]{1,0:T(8,128)(2,1)S(1)}, s32[1,512]{1,0:T(1,128)S(1)}, bf16[16,512]{1,0:T(8,128)(2,1)S(1)}) custom-call(s32[2]{0:T(128)S(1)} %pad_add_fusion.place_ref, s32[1,512]{1,0:T(1,128)} %bitcast.21, s32[1,512]{1,0:T(1,128)} %dest_hbm.1, bf16[512,1024]{1,0:T(8,128)(2,1)} %bitcast.19, f32[1,1024]{1,0:T(1,128)} %bitcast.20), custom_call_target="tpu_custom_call" | custom-call | flops 1 | bytes 1 | tf_op jit(solution)/shard_map/pack_far/pallas_call | solution.py:110
  2.5 4.1 %collective-permute-start.2 = (bf16[1040,128]{1,0:T(8,128)(2,1)S(1)}, bf16[1040,128]{1,0:T(8,128)(2,1)S(1)}, u32[]{:S(2)}, u32[]{:S(2)}) collective-permute-start(bf16[1040,128]{1,0:T(8,128)(2,1)S(1)} %get-tuple-element.41), channel_id=1, source_target_pairs={{0,16},{1,17},{2,18},{3,19},{4,20},{5,21},{6,22},{7,23},{8,24},{9,... | collective-permute-start | bytes 798728 | tf_op jit(solution)/shard_map/ppermute | solution.py:237
  9.0 1.6 %collective-permute-start.4 = (bf16[1040,128]{1,0:T(8,128)(2,1)S(1)}, bf16[1040,128]{1,0:T(8,128)(2,1)S(1)}, u32[]{:S(2)}, u32[]{:S(2)}) collective-permute-start(bf16[1040,128]{1,0:T(8,128)(2,1)S(1)} %get-tuple-element.42), channel_id=1, source_target_pairs={{0,8},{1,9},{2,10},{3,11},{4,12},{5,13},{6,14},{7,15},{8,0},{9,1},... | collective-permute-start | bytes 798728 | tf_op jit(solution)/shard_map/ppermute | solution.py:237
  10.7 1.7 %collective-permute-start.6 = (bf16[1040,128]{1,0:T(8,128)(2,1)S(1)}, bf16[1040,128]{1,0:T(8,128)(2,1)S(1)}, u32[]{:S(2)}, u32[]{:S(2)}) collective-permute-start(bf16[1040,128]{1,0:T(8,128)(2,1)S(1)} %get-tuple-element.44), channel_id=1, source_target_pairs={{0,4},{1,5},{2,6},{3,7},{4,0},{5,1},{6,2},{7,3},{8,12},{9,13},{10,... | collective-permute-start | bytes 798728 | tf_op jit(solution)/shard_map/ppermute | solution.py:237
  12.5 2.2 %copy-done = bf16[1,1024,2048]{2,1,0:T(8,128)(2,1)S(1)} copy-done((bf16[1,1024,2048]{2,1,0:T(8,128)(2,1)S(1)}, bf16[1,1024,2048]{2,1,0:T(8,128)(2,1)}, u32[]{:S(2)}) %copy-start) | copy-done | bytes 4194328
  14.6 2.2 %copy-done.2 = bf16[1,2048,1024]{2,1,0:T(8,128)(2,1)S(1)} copy-done((bf16[1,2048,1024]{2,1,0:T(8,128)(2,1)S(1)}, bf16[1,2048,1024]{2,1,0:T(8,128)(2,1)}, u32[]{:S(2)}) %copy-start.2) | copy-done | bytes 4194328
  16.8 2.5 %expert.5 = (f32[1024,1024]{1,0:T(8,128)S(1)}, f32[8,128]{1,0:T(8,128)S(1)}) custom-call(s32[2]{0:T(128)S(1)} %pad_add_fusion.place_ref, bf16[1040,128]{1,0:T(8,128)(2,1)S(1)} %get-tuple-element.39.refs_0_, bf16[1024,2048]{1,0:T(8,128)(2,1)S(1)} %bitcast.9, bf16[2048,1024]{1,0:T(8,128)(2,1)S(1)} %bitcast.14), custom_call_target="tpu_custom_call" | custom-call | flops 1 | bytes 1 | tf_op jit(solution)/shard_map/expert/pallas_call | solution.py:208
  19.4 5.9 %collective-permute-done.2.refs_0_ = bf16[1040,128]{1,0:T(8,128)(2,1)S(1)} collective-permute-done((bf16[1040,128]{1,0:T(8,128)(2,1)S(1)}, bf16[1040,128]{1,0:T(8,128)(2,1)S(1)}, u32[]{:S(2)}, u32[]{:S(2)}) %collective-permute-start.2) | collective-permute-done | bytes 266272 | tf_op jit(solution)/shard_map/ppermute | solution.py:237
  25.6 2.9 %collective-permute-start.3 = (bf16[1040,128]{1,0:T(8,128)(2,1)S(1)}, bf16[1040,128]{1,0:T(8,128)(2,1)S(1)}, u32[]{:S(2)}, u32[]{:S(2)}) collective-permute-start(bf16[1040,128]{1,0:T(8,128)(2,1)S(1)} %pack_more.5), channel_id=1, source_target_pairs={{0,24},{1,25},{2,26},{3,27},{4,28},{5,29},{6,30},{7,31},{8,16},{9,... | collective-permute-start | bytes 798728 | tf_op jit(solution)/shard_map/ppermute | solution.py:237
  28.5 4.9 %collective-permute-done.refs_0_ = bf16[1040,128]{1,0:T(8,128)(2,1)S(1)} collective-permute-done((bf16[1040,128]{1,0:T(8,128)(2,1)S(1)}, bf16[1040,128]{1,0:T(8,128)(2,1)S(1)}, u32[]{:S(2)}, u32[]{:S(2)}) %collective-permute-start) | collective-permute-done | bytes 266272 | tf_op jit(solution)/shard_map/ppermute | solution.py:237
  33.7 2.2 %collective-permute-start.1 = (bf16[1040,128]{1,0:T(8,128)(2,1)S(1)}, bf16[1040,128]{1,0:T(8,128)(2,1)S(1)}, u32[]{:S(2)}, u32[]{:S(2)}) collective-permute-start(bf16[1040,128]{1,0:T(8,128)(2,1)S(1)} %pack_more.4), channel_id=1, source_target_pairs={{0,28},{1,29},{2,30},{3,31},{4,24},{5,25},{6,26},{7,27},{8,20},{9,... | collective-permute-start | bytes 798728 | tf_op jit(solution)/shard_map/ppermute | solution.py:237
  36.0 3.7 %expert.6 = (f32[1024,1024]{1,0:T(8,128)S(1)}, f32[8,128]{1,0:T(8,128)}) custom-call(s32[2]{0:T(128)S(1)} %pad_add_fusion.place_ref, bf16[1040,128]{1,0:T(8,128)(2,1)S(1)} %collective-permute-done.2.refs_0_, bf16[1040,128]{1,0:T(8,128)(2,1)S(1)} %collective-permute-done.6.refs_1_, bf16[1024,2048]{1,0:T(8,128)(2,1)S(1)} %bitcast.10, ...), custom_call_target="tpu_custom_call" | custom-call | flops 1 | bytes 1 | tf_op jit(solution)/shard_map/expert/pallas_call | solution.py:208
  39.7 4.4 %collective-permute-done.5.refs_2_ = bf16[1040,128]{1,0:T(8,128)(2,1)S(1)} collective-permute-done((bf16[1040,128]{1,0:T(8,128)(2,1)S(1)}, bf16[1040,128]{1,0:T(8,128)(2,1)S(1)}, u32[]{:S(2)}, u32[]{:S(2)}) %collective-permute-start.5) | collective-permute-done | bytes 266272 | tf_op jit(solution)/shard_map/ppermute | solution.py:237
  44.0 5.2 %expert.7 = (f32[1024,1024]{1,0:T(8,128)S(1)}, f32[8,128]{1,0:T(8,128)}) custom-call(s32[2]{0:T(128)S(1)} %pad_add_fusion.place_ref, bf16[1040,128]{1,0:T(8,128)(2,1)S(1)} %collective-permute-done.refs_0_, bf16[1040,128]{1,0:T(8,128)(2,1)S(1)} %collective-permute-done.4.refs_1_, bf16[1040,128]{1,0:T(8,128)(2,1)S(1)} %collective-permute-done.5.refs_2_, ...), custom_call_target="tpu_custom_call" | custom-call | flops 1 | bytes 1 | tf_op jit(solution)/shard_map/expert/pallas_call | solution.py:208
  49.2 2.8 %expert.8 = (f32[1024,1024]{1,0:T(8,128)S(1)}, f32[8,128]{1,0:T(8,128)}) custom-call(s32[2]{0:T(128)S(1)} %pad_add_fusion.place_ref, bf16[1040,128]{1,0:T(8,128)(2,1)S(1)} %collective-permute-done.3.refs_0_, bf16[1024,2048]{1,0:T(8,128)(2,1)S(1)} %bitcast.12, bf16[2048,1024]{1,0:T(8,128)(2,1)S(1)} %bitcast.17, f32[1024,1024]{1,0:T(8,128)S(1)} %get-tuple-element.47.refs_3_), custom_call_target="tpu_custom_call" | custom-call | flops 1 | bytes 1 | tf_op jit(solution)/shard_map/expert/pallas_call | solution.py:208
  52.0 2.6 %expert.9 = (bf16[64,1024]{1,0:T(8,128)(2,1)S(1)}, bf16[64,1024]{1,0:T(8,128)(2,1)S(1)}, bf16[64,1024]{1,0:T(8,128)(2,1)S(1)}, bf16[64,1024]{1,0:T(8,128)(2,1)S(...) custom-call(s32[2]{0:T(128)S(1)} %pad_add_fusion.place_ref, ...), custom_call_target="tpu_custom_call" | custom-call | flops 1 | bytes 1 | tf_op jit(solution)/shard_map/expert/pallas_call | solution.py:208
  56.3 2.6 %collective-permute-start.17 = (bf16[64,1024]{1,0:T(8,128)(2,1)S(1)}, bf16[64,1024]{1,0:T(8,128)(2,1)S(1)}, u32[]{:S(2)}, u32[]{:S(2)}) collective-permute-start(bf16[64,1024]{1,0:T(8,128)(2,1)S(1)} %get-tuple-element.70), channel_id=1, source_target_pairs={{0,8},{1,9},{2,10},{3,11},{4,12},{5,13},{6,14},{7,15},{8,0},{9,1},... | collective-permute-start | bytes 393224 | tf_op jit(solution)/shard_map/ppermute | solution.py:237
  62.1 2.0 %collective-permute-start.11 = (bf16[64,1024]{1,0:T(8,128)(2,1)S(1)}, bf16[64,1024]{1,0:T(8,128)(2,1)S(1)}, u32[]{:S(2)}, u32[]{:S(2)}) collective-permute-start(bf16[64,1024]{1,0:T(8,128)(2,1)S(1)} %get-tuple-element.66), channel_id=1, source_target_pairs={{0,10},{1,11},{2,8},{3,9},{4,14},{5,15},{6,12},{7,13},{8,2},{9,3},... | collective-permute-start | bytes 393224 | tf_op jit(solution)/shard_map/ppermute | solution.py:237
  64.1 1.7 %collective-permute-start.10 = (bf16[64,1024]{1,0:T(8,128)(2,1)S(1)}, bf16[64,1024]{1,0:T(8,128)(2,1)S(1)}, u32[]{:S(2)}, u32[]{:S(2)}) collective-permute-start(bf16[64,1024]{1,0:T(8,128)(2,1)S(1)} %get-tuple-element.65), channel_id=1, source_target_pairs={{0,6},{1,7},{2,4},{3,5},{4,2},{5,3},{6,0},{7,1},{8,14},{9,15},{10,... | collective-permute-start | bytes 393224 | tf_op jit(solution)/shard_map/ppermute | solution.py:237
  66.9 1.6 %collective-permute-done.13 = bf16[64,1024]{1,0:T(8,128)(2,1)S(1)} collective-permute-done((bf16[64,1024]{1,0:T(8,128)(2,1)S(1)}, bf16[64,1024]{1,0:T(8,128)(2,1)S(1)}, u32[]{:S(2)}, u32[]{:S(2)}) %collective-permute-start.13) | collective-permute-done | bytes 131104 | tf_op jit(solution)/shard_map/ppermute | solution.py:237
  68.5 1.9 %collective-permute-done.11 = bf16[64,1024]{1,0:T(8,128)(2,1)S(1)} collective-permute-done((bf16[64,1024]{1,0:T(8,128)(2,1)S(1)}, bf16[64,1024]{1,0:T(8,128)(2,1)S(1)}, u32[]{:S(2)}, u32[]{:S(2)}) %collective-permute-start.11) | collective-permute-done | bytes 131104 | tf_op jit(solution)/shard_map/ppermute | solution.py:237
  70.4 3.7 %collective-permute-done.10 = bf16[64,1024]{1,0:T(8,128)(2,1)S(1)} collective-permute-done((bf16[64,1024]{1,0:T(8,128)(2,1)S(1)}, bf16[64,1024]{1,0:T(8,128)(2,1)S(1)}, u32[]{:S(2)}, u32[]{:S(2)}) %collective-permute-start.10) | collective-permute-done | bytes 131104 | tf_op jit(solution)/shard_map/ppermute | solution.py:237
  74.4 3.2 %collective-permute-start.18 = (bf16[32,1024]{1,0:T(8,128)(2,1)S(1)}, bf16[32,1024]{1,0:T(8,128)(2,1)S(1)}, u32[]{:S(2)}, u32[]{:S(2)}) collective-permute-start(bf16[32,1024]{1,0:T(8,128)(2,1)S(1)} %slice.67), channel_id=1, source_target_pairs={{0,16},{1,17},{2,18},{3,19},{4,20},{5,21},{6,22},{7,23},{8,24},{9,... | collective-permute-start | bytes 196616 | tf_op jit(solution)/shard_map/ppermute | solution.py:237
  77.6 2.2 %collective-permute-done.18 = bf16[32,1024]{1,0:T(8,128)(2,1)S(1)} collective-permute-done((bf16[32,1024]{1,0:T(8,128)(2,1)S(1)}, bf16[32,1024]{1,0:T(8,128)(2,1)S(1)}, u32[]{:S(2)}, u32[]{:S(2)}) %collective-permute-start.18) | collective-permute-done | bytes 65568 | tf_op jit(solution)/shard_map/ppermute | solution.py:237
  (43 shorter events, 10.2 us)
Async XLA Ops:
  2.5 22.8 %collective-permute-start.2 = (bf16[1040,128]{1,0:T(8,128)(2,1)S(1)}, bf16[1040,128]{1,0:T(8,128)(2,1)S(1)}, u32[]{:S(2)}, u32[]{:S(2)}) collective-permute-start(bf16[1040,128]{1,0:T(8,128)(2,1)S(1)} %get-tuple-element.41), channel_id=1, source_target_pairs={{0,16},{1,17},{2,18},{3,19},{4,20},{5,21},{6,22},{7,23},{8,24},{9,... | collective-permute-start | bytes 798728 | tf_op jit(solution)/shard_map/ppermute | solution.py:237
  7.6 25.8 %collective-permute-start = (bf16[1040,128]{1,0:T(8,128)(2,1)S(1)}, bf16[1040,128]{1,0:T(8,128)(2,1)S(1)}, u32[]{:S(2)}, u32[]{:S(2)}) collective-permute-start(bf16[1040,128]{1,0:T(8,128)(2,1)S(1)} %get-tuple-element.38), channel_id=1, source_target_pairs={{0,20},{1,21},{2,22},{3,23},{4,16},{5,17},{6,18},{7,19},{8,28},{9,... | collective-permute-start | bytes 798728 | tf_op jit(solution)/shard_map/ppermute | solution.py:237
  9.0 30.7 %collective-permute-start.4 = (bf16[1040,128]{1,0:T(8,128)(2,1)S(1)}, bf16[1040,128]{1,0:T(8,128)(2,1)S(1)}, u32[]{:S(2)}, u32[]{:S(2)}) collective-permute-start(bf16[1040,128]{1,0:T(8,128)(2,1)S(1)} %get-tuple-element.42), channel_id=1, source_target_pairs={{0,8},{1,9},{2,10},{3,11},{4,12},{5,13},{6,14},{7,15},{8,0},{9,1},... | collective-permute-start | bytes 798728 | tf_op jit(solution)/shard_map/ppermute | solution.py:237
  10.5 33.5 %collective-permute-start.5 = (bf16[1040,128]{1,0:T(8,128)(2,1)S(1)}, bf16[1040,128]{1,0:T(8,128)(2,1)S(1)}, u32[]{:S(2)}, u32[]{:S(2)}) collective-permute-start(bf16[1040,128]{1,0:T(8,128)(2,1)S(1)} %get-tuple-element.43), channel_id=1, source_target_pairs={{0,12},{1,13},{2,14},{3,15},{4,8},{5,9},{6,10},{7,11},{8,4},{9,5},... | collective-permute-start | bytes 798728 | tf_op jit(solution)/shard_map/ppermute | solution.py:237
  10.7 25.2 %collective-permute-start.6 = (bf16[1040,128]{1,0:T(8,128)(2,1)S(1)}, bf16[1040,128]{1,0:T(8,128)(2,1)S(1)}, u32[]{:S(2)}, u32[]{:S(2)}) collective-permute-start(bf16[1040,128]{1,0:T(8,128)(2,1)S(1)} %get-tuple-element.44), channel_id=1, source_target_pairs={{0,4},{1,5},{2,6},{3,7},{4,0},{5,1},{6,2},{7,3},{8,12},{9,13},{10,... | collective-permute-start | bytes 798728 | tf_op jit(solution)/shard_map/ppermute | solution.py:237
  12.5 2.2 %copy-start = (bf16[1,1024,2048]{2,1,0:T(8,128)(2,1)S(1)}, bf16[1,1024,2048]{2,1,0:T(8,128)(2,1)}, u32[]{:S(2)}) copy-start(bf16[1,1024,2048]{2,1,0:T(8,128)(2,1)} %param.8) | copy-start | bytes 12582916
  14.6 2.2 %copy-start.2 = (bf16[1,2048,1024]{2,1,0:T(8,128)(2,1)S(1)}, bf16[1,2048,1024]{2,1,0:T(8,128)(2,1)}, u32[]{:S(2)}) copy-start(bf16[1,2048,1024]{2,1,0:T(8,128)(2,1)} %param.9) | copy-start | bytes 12582916
  16.8 19.1 %copy-start.1 = (bf16[1,1024,2048]{2,1,0:T(8,128)(2,1)S(1)}, bf16[1,1024,2048]{2,1,0:T(8,128)(2,1)}, u32[]{:S(2)}) copy-start(bf16[1,1024,2048]{2,1,0:T(8,128)(2,1)} %param.8) | copy-start | bytes 12582916
  16.8 19.1 %copy-start.3 = (bf16[1,2048,1024]{2,1,0:T(8,128)(2,1)S(1)}, bf16[1,2048,1024]{2,1,0:T(8,128)(2,1)}, u32[]{:S(2)}) copy-start(bf16[1,2048,1024]{2,1,0:T(8,128)(2,1)} %param.9) | copy-start | bytes 12582916
  25.6 23.6 %collective-permute-start.3 = (bf16[1040,128]{1,0:T(8,128)(2,1)S(1)}, bf16[1040,128]{1,0:T(8,128)(2,1)S(1)}, u32[]{:S(2)}, u32[]{:S(2)}) collective-permute-start(bf16[1040,128]{1,0:T(8,128)(2,1)S(1)} %pack_more.5), channel_id=1, source_target_pairs={{0,24},{1,25},{2,26},{3,27},{4,28},{5,29},{6,30},{7,31},{8,16},{9,... | collective-permute-start | bytes 798728 | tf_op jit(solution)/shard_map/ppermute | solution.py:237
  33.7 18.3 %collective-permute-start.1 = (bf16[1040,128]{1,0:T(8,128)(2,1)S(1)}, bf16[1040,128]{1,0:T(8,128)(2,1)S(1)}, u32[]{:S(2)}, u32[]{:S(2)}) collective-permute-start(bf16[1040,128]{1,0:T(8,128)(2,1)S(1)} %pack_more.4), channel_id=1, source_target_pairs={{0,28},{1,29},{2,30},{3,31},{4,24},{5,25},{6,26},{7,27},{8,20},{9,... | collective-permute-start | bytes 798728 | tf_op jit(solution)/shard_map/ppermute | solution.py:237
  54.6 1.6 %collective-permute-start.15 = (bf16[128,1024]{1,0:T(8,128)(2,1)S(1)}, bf16[128,1024]{1,0:T(8,128)(2,1)S(1)}, u32[]{:S(2)}, u32[]{:S(2)}) collective-permute-start(bf16[128,1024]{1,0:T(8,128)(2,1)S(1)} %pad_maximum_fusion.3), channel_id=1, source_target_pairs={{0,1},{1,0},{2,3},{3,2},{4,5},{5,4},{6,7},{7,6},{8,9},{9,8},{10,11... | collective-permute-start | bytes 786440 | tf_op jit(solution)/shard_map/ppermute | solution.py:237
  54.7 4.8 %collective-permute-start.12 = (bf16[128,1024]{1,0:T(8,128)(2,1)S(1)}, bf16[128,1024]{1,0:T(8,128)(2,1)S(1)}, u32[]{:S(2)}, u32[]{:S(2)}) collective-permute-start(bf16[128,1024]{1,0:T(8,128)(2,1)S(1)} %pad_maximum_fusion.2), channel_id=1, source_target_pairs={{0,1},{1,0},{2,3},{3,2},{4,5},{5,4},{6,7},{7,6},{8,9},{9,8},{10,11... | collective-permute-start | bytes 786440 | tf_op jit(solution)/shard_map/ppermute | solution.py:237
  55.3 5.9 %collective-permute-start.9 = (bf16[128,1024]{1,0:T(8,128)(2,1)S(1)}, bf16[128,1024]{1,0:T(8,128)(2,1)S(1)}, u32[]{:S(2)}, u32[]{:S(2)}) collective-permute-start(bf16[128,1024]{1,0:T(8,128)(2,1)S(1)} %pad_maximum_fusion.1), channel_id=1, source_target_pairs={{0,1},{1,0},{2,3},{3,2},{4,5},{5,4},{6,7},{7,6},{8,9},{9,8},{10,11... | collective-permute-start | bytes 786440 | tf_op jit(solution)/shard_map/ppermute | solution.py:237
  55.4 6.7 %collective-permute-start.7 = (bf16[128,1024]{1,0:T(8,128)(2,1)S(1)}, bf16[128,1024]{1,0:T(8,128)(2,1)S(1)}, u32[]{:S(2)}, u32[]{:S(2)}) collective-permute-start(bf16[128,1024]{1,0:T(8,128)(2,1)S(1)} %pad_maximum_fusion), channel_id=1, source_target_pairs={{0,1},{1,0},{2,3},{3,2},{4,5},{5,4},{6,7},{7,6},{8,9},{9,8},{10,11... | collective-permute-start | bytes 786440 | tf_op jit(solution)/shard_map/ppermute | solution.py:237
  56.3 7.8 %collective-permute-start.17 = (bf16[64,1024]{1,0:T(8,128)(2,1)S(1)}, bf16[64,1024]{1,0:T(8,128)(2,1)S(1)}, u32[]{:S(2)}, u32[]{:S(2)}) collective-permute-start(bf16[64,1024]{1,0:T(8,128)(2,1)S(1)} %get-tuple-element.70), channel_id=1, source_target_pairs={{0,8},{1,9},{2,10},{3,11},{4,12},{5,13},{6,14},{7,15},{8,0},{9,1},... | collective-permute-start | bytes 393224 | tf_op jit(solution)/shard_map/ppermute | solution.py:237
  58.9 7.0 %collective-permute-start.16 = (bf16[64,1024]{1,0:T(8,128)(2,1)S(1)}, bf16[64,1024]{1,0:T(8,128)(2,1)S(1)}, u32[]{:S(2)}, u32[]{:S(2)}) collective-permute-start(bf16[64,1024]{1,0:T(8,128)(2,1)S(1)} %get-tuple-element.69), channel_id=1, source_target_pairs={{0,4},{1,5},{2,6},{3,7},{4,0},{5,1},{6,2},{7,3},{8,12},{9,13},{10,... | collective-permute-start | bytes 393224 | tf_op jit(solution)/shard_map/ppermute | solution.py:237
  59.6 7.3 %collective-permute-start.14 = (bf16[64,1024]{1,0:T(8,128)(2,1)S(1)}, bf16[64,1024]{1,0:T(8,128)(2,1)S(1)}, u32[]{:S(2)}, u32[]{:S(2)}) collective-permute-start(bf16[64,1024]{1,0:T(8,128)(2,1)S(1)} %get-tuple-element.68), channel_id=1, source_target_pairs={{0,2},{1,3},{2,0},{3,1},{4,6},{5,7},{6,4},{7,5},{8,10},{9,11},{10,... | collective-permute-start | bytes 393224 | tf_op jit(solution)/shard_map/ppermute | solution.py:237
  61.2 7.3 %collective-permute-start.13 = (bf16[64,1024]{1,0:T(8,128)(2,1)S(1)}, bf16[64,1024]{1,0:T(8,128)(2,1)S(1)}, u32[]{:S(2)}, u32[]{:S(2)}) collective-permute-start(bf16[64,1024]{1,0:T(8,128)(2,1)S(1)} %get-tuple-element.67), channel_id=1, source_target_pairs={{0,12},{1,13},{2,14},{3,15},{4,8},{5,9},{6,10},{7,11},{8,4},{9,5},... | collective-permute-start | bytes 393224 | tf_op jit(solution)/shard_map/ppermute | solution.py:237
  62.1 8.3 %collective-permute-start.11 = (bf16[64,1024]{1,0:T(8,128)(2,1)S(1)}, bf16[64,1024]{1,0:T(8,128)(2,1)S(1)}, u32[]{:S(2)}, u32[]{:S(2)}) collective-permute-start(bf16[64,1024]{1,0:T(8,128)(2,1)S(1)} %get-tuple-element.66), channel_id=1, source_target_pairs={{0,10},{1,11},{2,8},{3,9},{4,14},{5,15},{6,12},{7,13},{8,2},{9,3},... | collective-permute-start | bytes 393224 | tf_op jit(solution)/shard_map/ppermute | solution.py:237
  64.1 10.0 %collective-permute-start.10 = (bf16[64,1024]{1,0:T(8,128)(2,1)S(1)}, bf16[64,1024]{1,0:T(8,128)(2,1)S(1)}, u32[]{:S(2)}, u32[]{:S(2)}) collective-permute-start(bf16[64,1024]{1,0:T(8,128)(2,1)S(1)} %get-tuple-element.65), channel_id=1, source_target_pairs={{0,6},{1,7},{2,4},{3,5},{4,2},{5,3},{6,0},{7,1},{8,14},{9,15},{10,... | collective-permute-start | bytes 393224 | tf_op jit(solution)/shard_map/ppermute | solution.py:237
  65.8 8.4 %collective-permute-start.8 = (bf16[64,1024]{1,0:T(8,128)(2,1)S(1)}, bf16[64,1024]{1,0:T(8,128)(2,1)S(1)}, u32[]{:S(2)}, u32[]{:S(2)}) collective-permute-start(bf16[64,1024]{1,0:T(8,128)(2,1)S(1)} %add_convert_fusion.6), channel_id=1, source_target_pairs={{0,14},{1,15},{2,12},{3,13},{4,10},{5,11},{6,8},{7,9},{8,6},{9,7},... | collective-permute-start | bytes 393224 | tf_op jit(solution)/shard_map/ppermute | solution.py:237
  74.4 5.4 %collective-permute-start.18 = (bf16[32,1024]{1,0:T(8,128)(2,1)S(1)}, bf16[32,1024]{1,0:T(8,128)(2,1)S(1)}, u32[]{:S(2)}, u32[]{:S(2)}) collective-permute-start(bf16[32,1024]{1,0:T(8,128)(2,1)S(1)} %slice.67), channel_id=1, source_target_pairs={{0,16},{1,17},{2,18},{3,19},{4,20},{5,21},{6,22},{7,23},{8,24},{9,... | collective-permute-start | bytes 196616 | tf_op jit(solution)/shard_map/ppermute | solution.py:237

commit v6 on v5

--- a/solution.py
+++ b/solution.py
@@ -157,21 +157,38 @@
     lax.fori_loop(0, inner // part, step, 0, unroll=8)
 
 
-def down(hidden_ref, w_second_ref, table_ref, sums_ref, outs):
+def down(hidden_ref, w_second_ref, table_ref, sums_ref, outs, kept):
     part = 256
     width = w_second_ref.shape[1]
-    piece = table_ref.shape[0] // len(outs)
+    nodes = table_ref.shape[0]
+    start = nodes // 2 if kept else 0
     messages = [
         jnp.dot(hidden_ref[...], w_second_ref[:, at : at + part], preferred_element_type=F32).astype(BF16)
         for at in range(0, width, part)
     ]
     for i, message in enumerate(messages):
         columns = slice(i * part, (i + 1) * part)
-        total = jnp.dot(table_ref[...], message, preferred_element_type=F32)
-        if sums_ref is not None:
-            total = total + sums_ref[:, columns]
-        for b, out in enumerate(outs):
-            out[:, columns] = total[b * piece : (b + 1) * piece].astype(out.dtype)
+        if kept:
+            kept[0][:, columns] = message
+        add(table_ref[start:, :], message, sums_ref, start, columns, outs)
+    if kept:
+        kept[1][...] = table_ref[:start, :]
+
+
+def add(table, message, sums_ref, start, columns, outs):
+    total = jnp.dot(table, message, preferred_element_type=F32)
+    piece = table.shape[0] // len(outs)
+    if sums_ref is not None:
+        total = total + sums_ref[start : start + table.shape[0], columns]
+    for b, out in enumerate(outs):
+        out[:, columns] = total[b * piece : (b + 1) * piece].astype(out.dtype)
+
+
+def rest_kernel(messages_ref, table_ref, sums_ref, *outs):
+    part = 256
+    for at in range(0, messages_ref.shape[1], part):
+        columns = slice(at, at + part)
+        add(table_ref[...], messages_ref[:, columns], sums_ref, 0, columns, outs)
 
 
 def expert_kernel(count, slots, groups, relations, has_sums, last, place_ref, *refs):
@@ -181,7 +198,10 @@
     if has_sums:
         sums_ref, refs = refs[0], refs[1:]
     outs, (hidden_ref, table_ref, x_ref) = refs[:-3], refs[-3:]
-    if not last:
+    kept = ()
+    if last:
+        outs, kept = outs[:8], outs[8:]
+    else:
         outs[-1][...] = jnp.zeros_like(outs[-1])
         outs = outs[:-1]
     nodes = table_ref.shape[0]
@@ -191,7 +211,7 @@
             line == lax.broadcasted_iota(I32, (nodes, slots), 0)
         ).astype(BF16)
     up(x_ref, w_first_ref, hidden_ref)
-    down(hidden_ref, w_second_ref, table_ref, sums_ref, outs)
+    down(hidden_ref, w_second_ref, table_ref, sums_ref, outs, kept)
 
 
 def expert(place, blocks, w_first, w_second, sums, groups, relations, last):
@@ -201,11 +221,13 @@
     rows = count * slots
     nodes = groups * relations * NODE_DEV
     if last:
-        shapes = [jax.ShapeDtypeStruct((nodes // 16, width), BF16)] * 16
+        pieces = [jax.ShapeDtypeStruct((nodes // 16, width), BF16)] * 8
+        shapes = pieces + [jax.ShapeDtypeStruct((rows, width), BF16), jax.ShapeDtypeStruct((nodes // 2, rows), BF16)]
     else:
         shapes = [jax.ShapeDtypeStruct((nodes, width), F32), jax.ShapeDtypeStruct((8, LANES), F32)]
     args = [place, *blocks, w_first, w_second] + ([] if sums is None else [sums])
-    return pl.pallas_call(
+    params = pltpu.CompilerParams(vmem_limit_bytes=(16 if relations <= 8 else 58) * MIB)
+    outs = pl.pallas_call(
         functools.partial(expert_kernel, count, slots, groups, relations, sums is not None, last),
         out_shape=shapes,
         in_specs=[SM] + [VM] * (len(args) - 1),
@@ -213,10 +235,22 @@
         scratch_shapes=[
             pltpu.VMEM((rows, inner), BF16), pltpu.VMEM((nodes, rows), BF16), pltpu.VMEM((rows, width), BF16),
         ],
-        compiler_params=pltpu.CompilerParams(vmem_limit_bytes=(16 if relations <= 8 else 58) * MIB),
+        compiler_params=params,
         cost_estimate=pl.CostEstimate(flops=1, bytes_accessed=1, transcendentals=0),
         name="expert",
     )(*args)
+    if not last:
+        return outs
+    stay = pl.pallas_call(
+        rest_kernel,
+        out_shape=pieces,
+        in_specs=[VM] * 3,
+        out_specs=[VM] * 8,
+        compiler_params=params,
+        cost_estimate=pl.CostEstimate(flops=1, bytes_accessed=1, transcendentals=0),
+        name="expert_rest",
+    )(outs[8], outs[9], sums)
+    return list(stay) + list(outs[:8])
 
 
 def local(edge_feats, gain, w_in, w_out, rel_type, dst_node):

time: 80.7 us -> 80.4 us (level)
  transfers between devices with their start and end apart: 19 -> 19, of which waited for: 8 -> 7; matrix products, arithmetic and copies ran while one was open for 0% -> 0% of each run, Pallas kernels for 20% -> 20%
where the time goes in v6:
time: 80.4 us; the launch traced here: 80.2 us
  starting transfers between devices  28.7 us (36%)
  waiting for transfers between devices  24.7 us (31%)
  Pallas kernels  21 us (26%)
  local copies, waits for them, and re-layouts  4.39 us (5%)
  other arithmetic  1.24 us (2%)
    ppermute x19, starting transfers between devices, move(): return lax.ppermute(value, ('rel', 'dom'), pairs)  28.7 us
    ppermute x19, waiting for transfers between devices, move(): return lax.ppermute(value, ('rel', 'dom'), pairs)  24.7 us
    pallas_call x5, Pallas kernels, expert(): pl.pallas_call(functools.partial(expert_kernel, count, slots, groups, rel...  16.5 us
    unnamed x8, local copies, waits for them, and re-layouts  4.38 us
    pallas_call x1, Pallas kernels, pack(): pl.pallas_call(functools.partial(pack_kernel, relations, slots, labels),...  2.39 us
    pallas_call x3, Pallas kernels, pack_more(): pl.pallas_call(functools.partial(pack_more_kernel, slots, labels), out_sh...  1.65 us
  transfers between devices with their start and end apart: 19, of which 7 were waited for; matrix products, arithmetic and copies ran while one was open for 0% of the time, Pallas kernels for 20%

profile of v6, /device:TPU:0, one launch (start us, length us, event | category | flops | bytes accessed | tf_op | source)
XLA Modules:
  0.0 80.2 jit_solution(1290022716065645915)
XLA Ops:
  0.1 2.4 %pack_far.1 = (bf16[1040,128]{1,0:T(8,128)(2,1)S(1)}, bf16[512,1024]{1,0:T(8,128)(2,1)S(1)}, s32[1,512]{1,0:T(1,128)S(1)}, bf16[16,512]{1,0:T(8,128)(2,1)S(1)}) custom-call(s32[2]{0:T(128)S(1)} %pad_add_fusion.place_ref, s32[1,512]{1,0:T(1,128)} %bitcast.21, s32[1,512]{1,0:T(1,128)} %dest_hbm.1, bf16[512,1024]{1,0:T(8,128)(2,1)} %bitcast.19, f32[1,1024]{1,0:T(1,128)} %bitcast.20), custom_call_target="tpu_custom_call" | custom-call | flops 1 | bytes 1 | tf_op jit(solution)/shard_map/pack_far/pallas_call | solution.py:110
  2.5 4.1 %collective-permute-start.2 = (bf16[1040,128]{1,0:T(8,128)(2,1)S(1)}, bf16[1040,128]{1,0:T(8,128)(2,1)S(1)}, u32[]{:S(2)}, u32[]{:S(2)}) collective-permute-start(bf16[1040,128]{1,0:T(8,128)(2,1)S(1)} %get-tuple-element.43), channel_id=1, source_target_pairs={{0,16},{1,17},{2,18},{3,19},{4,20},{5,21},{6,22},{7,23},{8,24},{9,... | collective-permute-start | bytes 798728 | tf_op jit(solution)/shard_map/ppermute | solution.py:271
  9.0 1.6 %collective-permute-start.4 = (bf16[1040,128]{1,0:T(8,128)(2,1)S(1)}, bf16[1040,128]{1,0:T(8,128)(2,1)S(1)}, u32[]{:S(2)}, u32[]{:S(2)}) collective-permute-start(bf16[1040,128]{1,0:T(8,128)(2,1)S(1)} %get-tuple-element.44), channel_id=1, source_target_pairs={{0,8},{1,9},{2,10},{3,11},{4,12},{5,13},{6,14},{7,15},{8,0},{9,1},... | collective-permute-start | bytes 798728 | tf_op jit(solution)/shard_map/ppermute | solution.py:271
  10.7 1.7 %collective-permute-start.6 = (bf16[1040,128]{1,0:T(8,128)(2,1)S(1)}, bf16[1040,128]{1,0:T(8,128)(2,1)S(1)}, u32[]{:S(2)}, u32[]{:S(2)}) collective-permute-start(bf16[1040,128]{1,0:T(8,128)(2,1)S(1)} %get-tuple-element.46), channel_id=1, source_target_pairs={{0,4},{1,5},{2,6},{3,7},{4,0},{5,1},{6,2},{7,3},{8,12},{9,13},{10,... | collective-permute-start | bytes 798728 | tf_op jit(solution)/shard_map/ppermute | solution.py:271
  12.5 2.2 %copy-done = bf16[1,1024,2048]{2,1,0:T(8,128)(2,1)S(1)} copy-done((bf16[1,1024,2048]{2,1,0:T(8,128)(2,1)S(1)}, bf16[1,1024,2048]{2,1,0:T(8,128)(2,1)}, u32[]{:S(2)}) %copy-start) | copy-done | bytes 4194328
  14.6 2.2 %copy-done.2 = bf16[1,2048,1024]{2,1,0:T(8,128)(2,1)S(1)} copy-done((bf16[1,2048,1024]{2,1,0:T(8,128)(2,1)S(1)}, bf16[1,2048,1024]{2,1,0:T(8,128)(2,1)}, u32[]{:S(2)}) %copy-start.2) | copy-done | bytes 4194328
  16.8 2.5 %expert.5 = (f32[1024,1024]{1,0:T(8,128)S(1)}, f32[8,128]{1,0:T(8,128)S(1)}) custom-call(s32[2]{0:T(128)S(1)} %pad_add_fusion.place_ref, bf16[1040,128]{1,0:T(8,128)(2,1)S(1)} %get-tuple-element.41.refs_0_, bf16[1024,2048]{1,0:T(8,128)(2,1)S(1)} %bitcast.9, bf16[2048,1024]{1,0:T(8,128)(2,1)S(1)} %bitcast.14), custom_call_target="tpu_custom_call" | custom-call | flops 1 | bytes 1 | tf_op jit(solution)/shard_map/expert/pallas_call | solution.py:230
  19.4 5.9 %collective-permute-done.2.refs_0_ = bf16[1040,128]{1,0:T(8,128)(2,1)S(1)} collective-permute-done((bf16[1040,128]{1,0:T(8,128)(2,1)S(1)}, bf16[1040,128]{1,0:T(8,128)(2,1)S(1)}, u32[]{:S(2)}, u32[]{:S(2)}) %collective-permute-start.2) | collective-permute-done | bytes 266272 | tf_op jit(solution)/shard_map/ppermute | solution.py:271
  25.6 2.9 %collective-permute-start.3 = (bf16[1040,128]{1,0:T(8,128)(2,1)S(1)}, bf16[1040,128]{1,0:T(8,128)(2,1)S(1)}, u32[]{:S(2)}, u32[]{:S(2)}) collective-permute-start(bf16[1040,128]{1,0:T(8,128)(2,1)S(1)} %pack_more.5), channel_id=1, source_target_pairs={{0,24},{1,25},{2,26},{3,27},{4,28},{5,29},{6,30},{7,31},{8,16},{9,... | collective-permute-start | bytes 798728 | tf_op jit(solution)/shard_map/ppermute | solution.py:271
  28.5 4.9 %collective-permute-done.refs_0_ = bf16[1040,128]{1,0:T(8,128)(2,1)S(1)} collective-permute-done((bf16[1040,128]{1,0:T(8,128)(2,1)S(1)}, bf16[1040,128]{1,0:T(8,128)(2,1)S(1)}, u32[]{:S(2)}, u32[]{:S(2)}) %collective-permute-start) | collective-permute-done | bytes 266272 | tf_op jit(solution)/shard_map/ppermute | solution.py:271
  33.7 2.2 %collective-permute-start.1 = (bf16[1040,128]{1,0:T(8,128)(2,1)S(1)}, bf16[1040,128]{1,0:T(8,128)(2,1)S(1)}, u32[]{:S(2)}, u32[]{:S(2)}) collective-permute-start(bf16[1040,128]{1,0:T(8,128)(2,1)S(1)} %pack_more.4), channel_id=1, source_target_pairs={{0,28},{1,29},{2,30},{3,31},{4,24},{5,25},{6,26},{7,27},{8,20},{9,... | collective-permute-start | bytes 798728 | tf_op jit(solution)/shard_map/ppermute | solution.py:271
  36.0 3.7 %expert.6 = (f32[1024,1024]{1,0:T(8,128)S(1)}, f32[8,128]{1,0:T(8,128)}) custom-call(s32[2]{0:T(128)S(1)} %pad_add_fusion.place_ref, bf16[1040,128]{1,0:T(8,128)(2,1)S(1)} %collective-permute-done.2.refs_0_, bf16[1040,128]{1,0:T(8,128)(2,1)S(1)} %collective-permute-done.6.refs_1_, bf16[1024,2048]{1,0:T(8,128)(2,1)S(1)} %bitcast.10, ...), custom_call_target="tpu_custom_call" | custom-call | flops 1 | bytes 1 | tf_op jit(solution)/shard_map/expert/pallas_call | solution.py:230
  39.7 4.4 %collective-permute-done.5.refs_2_ = bf16[1040,128]{1,0:T(8,128)(2,1)S(1)} collective-permute-done((bf16[1040,128]{1,0:T(8,128)(2,1)S(1)}, bf16[1040,128]{1,0:T(8,128)(2,1)S(1)}, u32[]{:S(2)}, u32[]{:S(2)}) %collective-permute-start.5) | collective-permute-done | bytes 266272 | tf_op jit(solution)/shard_map/ppermute | solution.py:271
  44.0 5.2 %expert.7 = (f32[1024,1024]{1,0:T(8,128)S(1)}, f32[8,128]{1,0:T(8,128)}) custom-call(s32[2]{0:T(128)S(1)} %pad_add_fusion.place_ref, bf16[1040,128]{1,0:T(8,128)(2,1)S(1)} %collective-permute-done.refs_0_, bf16[1040,128]{1,0:T(8,128)(2,1)S(1)} %collective-permute-done.4.refs_1_, bf16[1040,128]{1,0:T(8,128)(2,1)S(1)} %collective-permute-done.5.refs_2_, ...), custom_call_target="tpu_custom_call" | custom-call | flops 1 | bytes 1 | tf_op jit(solution)/shard_map/expert/pallas_call | solution.py:230
  49.2 2.8 %expert.8 = (f32[1024,1024]{1,0:T(8,128)S(1)}, f32[8,128]{1,0:T(8,128)}) custom-call(s32[2]{0:T(128)S(1)} %pad_add_fusion.place_ref, bf16[1040,128]{1,0:T(8,128)(2,1)S(1)} %collective-permute-done.3.refs_0_, bf16[1024,2048]{1,0:T(8,128)(2,1)S(1)} %bitcast.12, bf16[2048,1024]{1,0:T(8,128)(2,1)S(1)} %bitcast.17, f32[1024,1024]{1,0:T(8,128)S(1)} %get-tuple-element.49.refs_3_), custom_call_target="tpu_custom_call" | custom-call | flops 1 | bytes 1 | tf_op jit(solution)/shard_map/expert/pallas_call | solution.py:230
  52.0 2.3 %expert.9 = (bf16[64,1024]{1,0:T(8,128)(2,1)S(1)}, bf16[64,1024]{1,0:T(8,128)(2,1)S(1)}, bf16[64,1024]{1,0:T(8,128)(2,1)S(1)}, bf16[64,1024]{1,0:T(8,128)(2,1)S(...) custom-call(s32[2]{0:T(128)S(1)} %pad_add_fusion.place_ref, ...), custom_call_target="tpu_custom_call" | custom-call | flops 1 | bytes 1 | tf_op jit(solution)/shard_map/expert/pallas_call | solution.py:230
  56.2 2.6 %collective-permute-start.17 = (bf16[64,1024]{1,0:T(8,128)(2,1)S(1)}, bf16[64,1024]{1,0:T(8,128)(2,1)S(1)}, u32[]{:S(2)}, u32[]{:S(2)}) collective-permute-start(bf16[64,1024]{1,0:T(8,128)(2,1)S(1)} %get-tuple-element.74), channel_id=1, source_target_pairs={{0,8},{1,9},{2,10},{3,11},{4,12},{5,13},{6,14},{7,15},{8,0},{9,1},... | collective-permute-start | bytes 393224 | tf_op jit(solution)/shard_map/ppermute | solution.py:271
  62.1 2.0 %collective-permute-start.11 = (bf16[64,1024]{1,0:T(8,128)(2,1)S(1)}, bf16[64,1024]{1,0:T(8,128)(2,1)S(1)}, u32[]{:S(2)}, u32[]{:S(2)}) collective-permute-start(bf16[64,1024]{1,0:T(8,128)(2,1)S(1)} %get-tuple-element.70), channel_id=1, source_target_pairs={{0,10},{1,11},{2,8},{3,9},{4,14},{5,15},{6,12},{7,13},{8,2},{9,3},... | collective-permute-start | bytes 393224 | tf_op jit(solution)/shard_map/ppermute | solution.py:271
  64.1 1.7 %collective-permute-start.10 = (bf16[64,1024]{1,0:T(8,128)(2,1)S(1)}, bf16[64,1024]{1,0:T(8,128)(2,1)S(1)}, u32[]{:S(2)}, u32[]{:S(2)}) collective-permute-start(bf16[64,1024]{1,0:T(8,128)(2,1)S(1)} %get-tuple-element.69), channel_id=1, source_target_pairs={{0,6},{1,7},{2,4},{3,5},{4,2},{5,3},{6,0},{7,1},{8,14},{9,15},{10,... | collective-permute-start | bytes 393224 | tf_op jit(solution)/shard_map/ppermute | solution.py:271
  66.7 1.7 %collective-permute-done.13 = bf16[64,1024]{1,0:T(8,128)(2,1)S(1)} collective-permute-done((bf16[64,1024]{1,0:T(8,128)(2,1)S(1)}, bf16[64,1024]{1,0:T(8,128)(2,1)S(1)}, u32[]{:S(2)}, u32[]{:S(2)}) %collective-permute-start.13) | collective-permute-done | bytes 131104 | tf_op jit(solution)/shard_map/ppermute | solution.py:271
  68.5 1.7 %collective-permute-done.11 = bf16[64,1024]{1,0:T(8,128)(2,1)S(1)} collective-permute-done((bf16[64,1024]{1,0:T(8,128)(2,1)S(1)}, bf16[64,1024]{1,0:T(8,128)(2,1)S(1)}, u32[]{:S(2)}, u32[]{:S(2)}) %collective-permute-start.11) | collective-permute-done | bytes 131104 | tf_op jit(solution)/shard_map/ppermute | solution.py:271
  70.2 3.8 %collective-permute-done.10 = bf16[64,1024]{1,0:T(8,128)(2,1)S(1)} collective-permute-done((bf16[64,1024]{1,0:T(8,128)(2,1)S(1)}, bf16[64,1024]{1,0:T(8,128)(2,1)S(1)}, u32[]{:S(2)}, u32[]{:S(2)}) %collective-permute-start.10) | collective-permute-done | bytes 131104 | tf_op jit(solution)/shard_map/ppermute | solution.py:271
  74.2 3.1 %collective-permute-start.18 = (bf16[32,1024]{1,0:T(8,128)(2,1)S(1)}, bf16[32,1024]{1,0:T(8,128)(2,1)S(1)}, u32[]{:S(2)}, u32[]{:S(2)}) collective-permute-start(bf16[32,1024]{1,0:T(8,128)(2,1)S(1)} %slice.67), channel_id=1, source_target_pairs={{0,16},{1,17},{2,18},{3,19},{4,20},{5,21},{6,22},{7,23},{8,24},{9,... | collective-permute-start | bytes 196616 | tf_op jit(solution)/shard_map/ppermute | solution.py:271
  77.3 2.2 %collective-permute-done.18 = bf16[32,1024]{1,0:T(8,128)(2,1)S(1)} collective-permute-done((bf16[32,1024]{1,0:T(8,128)(2,1)S(1)}, bf16[32,1024]{1,0:T(8,128)(2,1)S(1)}, u32[]{:S(2)}, u32[]{:S(2)}) %collective-permute-start.18) | collective-permute-done | bytes 65568 | tf_op jit(solution)/shard_map/ppermute | solution.py:271
  (44 shorter events, 10.2 us)
Async XLA Ops:
  2.5 22.8 %collective-permute-start.2 = (bf16[1040,128]{1,0:T(8,128)(2,1)S(1)}, bf16[1040,128]{1,0:T(8,128)(2,1)S(1)}, u32[]{:S(2)}, u32[]{:S(2)}) collective-permute-start(bf16[1040,128]{1,0:T(8,128)(2,1)S(1)} %get-tuple-element.43), channel_id=1, source_target_pairs={{0,16},{1,17},{2,18},{3,19},{4,20},{5,21},{6,22},{7,23},{8,24},{9,... | collective-permute-start | bytes 798728 | tf_op jit(solution)/shard_map/ppermute | solution.py:271
  7.6 25.8 %collective-permute-start = (bf16[1040,128]{1,0:T(8,128)(2,1)S(1)}, bf16[1040,128]{1,0:T(8,128)(2,1)S(1)}, u32[]{:S(2)}, u32[]{:S(2)}) collective-permute-start(bf16[1040,128]{1,0:T(8,128)(2,1)S(1)} %get-tuple-element.40), channel_id=1, source_target_pairs={{0,20},{1,21},{2,22},{3,23},{4,16},{5,17},{6,18},{7,19},{8,28},{9,... | collective-permute-start | bytes 798728 | tf_op jit(solution)/shard_map/ppermute | solution.py:271
  9.0 30.7 %collective-permute-start.4 = (bf16[1040,128]{1,0:T(8,128)(2,1)S(1)}, bf16[1040,128]{1,0:T(8,128)(2,1)S(1)}, u32[]{:S(2)}, u32[]{:S(2)}) collective-permute-start(bf16[1040,128]{1,0:T(8,128)(2,1)S(1)} %get-tuple-element.44), channel_id=1, source_target_pairs={{0,8},{1,9},{2,10},{3,11},{4,12},{5,13},{6,14},{7,15},{8,0},{9,1},... | collective-permute-start | bytes 798728 | tf_op jit(solution)/shard_map/ppermute | solution.py:271
  10.5 33.5 %collective-permute-start.5 = (bf16[1040,128]{1,0:T(8,128)(2,1)S(1)}, bf16[1040,128]{1,0:T(8,128)(2,1)S(1)}, u32[]{:S(2)}, u32[]{:S(2)}) collective-permute-start(bf16[1040,128]{1,0:T(8,128)(2,1)S(1)} %get-tuple-element.45), channel_id=1, source_target_pairs={{0,12},{1,13},{2,14},{3,15},{4,8},{5,9},{6,10},{7,11},{8,4},{9,5},... | collective-permute-start | bytes 798728 | tf_op jit(solution)/shard_map/ppermute | solution.py:271
  10.7 25.2 %collective-permute-start.6 = (bf16[1040,128]{1,0:T(8,128)(2,1)S(1)}, bf16[1040,128]{1,0:T(8,128)(2,1)S(1)}, u32[]{:S(2)}, u32[]{:S(2)}) collective-permute-start(bf16[1040,128]{1,0:T(8,128)(2,1)S(1)} %get-tuple-element.46), channel_id=1, source_target_pairs={{0,4},{1,5},{2,6},{3,7},{4,0},{5,1},{6,2},{7,3},{8,12},{9,13},{10,... | collective-permute-start | bytes 798728 | tf_op jit(solution)/shard_map/ppermute | solution.py:271
  12.5 2.2 %copy-start = (bf16[1,1024,2048]{2,1,0:T(8,128)(2,1)S(1)}, bf16[1,1024,2048]{2,1,0:T(8,128)(2,1)}, u32[]{:S(2)}) copy-start(bf16[1,1024,2048]{2,1,0:T(8,128)(2,1)} %param.8) | copy-start | bytes 12582916
  14.6 2.2 %copy-start.2 = (bf16[1,2048,1024]{2,1,0:T(8,128)(2,1)S(1)}, bf16[1,2048,1024]{2,1,0:T(8,128)(2,1)}, u32[]{:S(2)}) copy-start(bf16[1,2048,1024]{2,1,0:T(8,128)(2,1)} %param.9) | copy-start | bytes 12582916
  16.8 19.1 %copy-start.1 = (bf16[1,1024,2048]{2,1,0:T(8,128)(2,1)S(1)}, bf16[1,1024,2048]{2,1,0:T(8,128)(2,1)}, u32[]{:S(2)}) copy-start(bf16[1,1024,2048]{2,1,0:T(8,128)(2,1)} %param.8) | copy-start | bytes 12582916
  16.8 19.1 %copy-start.3 = (bf16[1,2048,1024]{2,1,0:T(8,128)(2,1)S(1)}, bf16[1,2048,1024]{2,1,0:T(8,128)(2,1)}, u32[]{:S(2)}) copy-start(bf16[1,2048,1024]{2,1,0:T(8,128)(2,1)} %param.9) | copy-start | bytes 12582916
  25.6 23.6 %collective-permute-start.3 = (bf16[1040,128]{1,0:T(8,128)(2,1)S(1)}, bf16[1040,128]{1,0:T(8,128)(2,1)S(1)}, u32[]{:S(2)}, u32[]{:S(2)}) collective-permute-start(bf16[1040,128]{1,0:T(8,128)(2,1)S(1)} %pack_more.5), channel_id=1, source_target_pairs={{0,24},{1,25},{2,26},{3,27},{4,28},{5,29},{6,30},{7,31},{8,16},{9,... | collective-permute-start | bytes 798728 | tf_op jit(solution)/shard_map/ppermute | solution.py:271
  33.7 18.3 %collective-permute-start.1 = (bf16[1040,128]{1,0:T(8,128)(2,1)S(1)}, bf16[1040,128]{1,0:T(8,128)(2,1)S(1)}, u32[]{:S(2)}, u32[]{:S(2)}) collective-permute-start(bf16[1040,128]{1,0:T(8,128)(2,1)S(1)} %pack_more.4), channel_id=1, source_target_pairs={{0,28},{1,29},{2,30},{3,31},{4,24},{5,25},{6,26},{7,27},{8,20},{9,... | collective-permute-start | bytes 798728 | tf_op jit(solution)/shard_map/ppermute | solution.py:271
  54.4 1.8 %collective-permute-start.15 = (bf16[128,1024]{1,0:T(8,128)(2,1)S(1)}, bf16[128,1024]{1,0:T(8,128)(2,1)S(1)}, u32[]{:S(2)}, u32[]{:S(2)}) collective-permute-start(bf16[128,1024]{1,0:T(8,128)(2,1)S(1)} %pad_maximum_fusion.3), channel_id=1, source_target_pairs={{0,1},{1,0},{2,3},{3,2},{4,5},{5,4},{6,7},{7,6},{8,9},{9,8},{10,11... | collective-permute-start | bytes 786440 | tf_op jit(solution)/shard_map/ppermute | solution.py:271
  54.5 5.0 %collective-permute-start.12 = (bf16[128,1024]{1,0:T(8,128)(2,1)S(1)}, bf16[128,1024]{1,0:T(8,128)(2,1)S(1)}, u32[]{:S(2)}, u32[]{:S(2)}) collective-permute-start(bf16[128,1024]{1,0:T(8,128)(2,1)S(1)} %pad_maximum_fusion.2), channel_id=1, source_target_pairs={{0,1},{1,0},{2,3},{3,2},{4,5},{5,4},{6,7},{7,6},{8,9},{9,8},{10,11... | collective-permute-start | bytes 786440 | tf_op jit(solution)/shard_map/ppermute | solution.py:271
  55.1 6.1 %collective-permute-start.9 = (bf16[128,1024]{1,0:T(8,128)(2,1)S(1)}, bf16[128,1024]{1,0:T(8,128)(2,1)S(1)}, u32[]{:S(2)}, u32[]{:S(2)}) collective-permute-start(bf16[128,1024]{1,0:T(8,128)(2,1)S(1)} %pad_maximum_fusion.1), channel_id=1, source_target_pairs={{0,1},{1,0},{2,3},{3,2},{4,5},{5,4},{6,7},{7,6},{8,9},{9,8},{10,11... | collective-permute-start | bytes 786440 | tf_op jit(solution)/shard_map/ppermute | solution.py:271
  55.2 6.9 %collective-permute-start.7 = (bf16[128,1024]{1,0:T(8,128)(2,1)S(1)}, bf16[128,1024]{1,0:T(8,128)(2,1)S(1)}, u32[]{:S(2)}, u32[]{:S(2)}) collective-permute-start(bf16[128,1024]{1,0:T(8,128)(2,1)S(1)} %pad_maximum_fusion), channel_id=1, source_target_pairs={{0,1},{1,0},{2,3},{3,2},{4,5},{5,4},{6,7},{7,6},{8,9},{9,8},{10,11... | collective-permute-start | bytes 786440 | tf_op jit(solution)/shard_map/ppermute | solution.py:271
  56.2 7.9 %collective-permute-start.17 = (bf16[64,1024]{1,0:T(8,128)(2,1)S(1)}, bf16[64,1024]{1,0:T(8,128)(2,1)S(1)}, u32[]{:S(2)}, u32[]{:S(2)}) collective-permute-start(bf16[64,1024]{1,0:T(8,128)(2,1)S(1)} %get-tuple-element.74), channel_id=1, source_target_pairs={{0,8},{1,9},{2,10},{3,11},{4,12},{5,13},{6,14},{7,15},{8,0},{9,1},... | collective-permute-start | bytes 393224 | tf_op jit(solution)/shard_map/ppermute | solution.py:271
  58.8 7.0 %collective-permute-start.16 = (bf16[64,1024]{1,0:T(8,128)(2,1)S(1)}, bf16[64,1024]{1,0:T(8,128)(2,1)S(1)}, u32[]{:S(2)}, u32[]{:S(2)}) collective-permute-start(bf16[64,1024]{1,0:T(8,128)(2,1)S(1)} %get-tuple-element.73), channel_id=1, source_target_pairs={{0,4},{1,5},{2,6},{3,7},{4,0},{5,1},{6,2},{7,3},{8,12},{9,13},{10,... | collective-permute-start | bytes 393224 | tf_op jit(solution)/shard_map/ppermute | solution.py:271
  59.6 7.2 %collective-permute-start.14 = (bf16[64,1024]{1,0:T(8,128)(2,1)S(1)}, bf16[64,1024]{1,0:T(8,128)(2,1)S(1)}, u32[]{:S(2)}, u32[]{:S(2)}) collective-permute-start(bf16[64,1024]{1,0:T(8,128)(2,1)S(1)} %get-tuple-element.72), channel_id=1, source_target_pairs={{0,2},{1,3},{2,0},{3,1},{4,6},{5,7},{6,4},{7,5},{8,10},{9,11},{10,... | collective-permute-start | bytes 393224 | tf_op jit(solution)/shard_map/ppermute | solution.py:271
  61.1 7.3 %collective-permute-start.13 = (bf16[64,1024]{1,0:T(8,128)(2,1)S(1)}, bf16[64,1024]{1,0:T(8,128)(2,1)S(1)}, u32[]{:S(2)}, u32[]{:S(2)}) collective-permute-start(bf16[64,1024]{1,0:T(8,128)(2,1)S(1)} %get-tuple-element.71), channel_id=1, source_target_pairs={{0,12},{1,13},{2,14},{3,15},{4,8},{5,9},{6,10},{7,11},{8,4},{9,5},... | collective-permute-start | bytes 393224 | tf_op jit(solution)/shard_map/ppermute | solution.py:271
  62.1 8.1 %collective-permute-start.11 = (bf16[64,1024]{1,0:T(8,128)(2,1)S(1)}, bf16[64,1024]{1,0:T(8,128)(2,1)S(1)}, u32[]{:S(2)}, u32[]{:S(2)}) collective-permute-start(bf16[64,1024]{1,0:T(8,128)(2,1)S(1)} %get-tuple-element.70), channel_id=1, source_target_pairs={{0,10},{1,11},{2,8},{3,9},{4,14},{5,15},{6,12},{7,13},{8,2},{9,3},... | collective-permute-start | bytes 393224 | tf_op jit(solution)/shard_map/ppermute | solution.py:271
  64.1 9.9 %collective-permute-start.10 = (bf16[64,1024]{1,0:T(8,128)(2,1)S(1)}, bf16[64,1024]{1,0:T(8,128)(2,1)S(1)}, u32[]{:S(2)}, u32[]{:S(2)}) collective-permute-start(bf16[64,1024]{1,0:T(8,128)(2,1)S(1)} %get-tuple-element.69), channel_id=1, source_target_pairs={{0,6},{1,7},{2,4},{3,5},{4,2},{5,3},{6,0},{7,1},{8,14},{9,15},{10,... | collective-permute-start | bytes 393224 | tf_op jit(solution)/shard_map/ppermute | solution.py:271
  65.8 8.2 %collective-permute-start.8 = (bf16[64,1024]{1,0:T(8,128)(2,1)S(1)}, bf16[64,1024]{1,0:T(8,128)(2,1)S(1)}, u32[]{:S(2)}, u32[]{:S(2)}) collective-permute-start(bf16[64,1024]{1,0:T(8,128)(2,1)S(1)} %add_convert_fusion.6), channel_id=1, source_target_pairs={{0,14},{1,15},{2,12},{3,13},{4,10},{5,11},{6,8},{7,9},{8,6},{9,7},... | collective-permute-start | bytes 393224 | tf_op jit(solution)/shard_map/ppermute | solution.py:271
  74.2 5.4 %collective-permute-start.18 = (bf16[32,1024]{1,0:T(8,128)(2,1)S(1)}, bf16[32,1024]{1,0:T(8,128)(2,1)S(1)}, u32[]{:S(2)}, u32[]{:S(2)}) collective-permute-start(bf16[32,1024]{1,0:T(8,128)(2,1)S(1)} %slice.67), channel_id=1, source_target_pairs={{0,16},{1,17},{2,18},{3,19},{4,20},{5,21},{6,22},{7,23},{8,24},{9,... | collective-permute-start | bytes 196616 | tf_op jit(solution)/shard_map/ppermute | solution.py:271

commit v7 on v6

--- a/solution.py
+++ b/solution.py
@@ -11,7 +11,7 @@
 NODE_DEV = 32
 LANES = 128
 EXTRA = 16
-PAIRS = ((1, 2), (4, 3), (5, 6), (7, 0))
+PAIRS = ((1, 2), (4, 3, 5), (6, 7, 0))
 MIB = 1024 * 1024
 VM = pl.BlockSpec(memory_space=pltpu.VMEM)
 SM = pl.BlockSpec(memory_space=pltpu.SMEM)

time: 80.4 us -> 80.5 us (level)
    ppermute x19 -> x18, waiting for transfers between devices: 24.7 us -> 25.2 us  [move(): return lax.ppermute(value, ('rel', 'dom'), pairs)]
    ppermute x19 -> x18, starting transfers between devices: 28.7 us -> 28.3 us  [move(): return lax.ppermute(value, ('rel', 'dom'), pairs)]
  transfers between devices with their start and end apart: 19 -> 18, of which waited for: 7 -> 8; matrix products, arithmetic and copies ran while one was open for 0% -> 0% of each run, Pallas kernels for 20% -> 20%
where the time goes in v7:
time: 80.5 us; the launch traced here: 80.3 us
  starting transfers between devices  28.3 us (35%)
  waiting for transfers between devices  25.2 us (31%)
  Pallas kernels  21 us (26%)
  local copies, waits for them, and re-layouts  4.39 us (5%)
  other arithmetic  1.26 us (2%)
    ppermute x18, starting transfers between devices, move(): return lax.ppermute(value, ('rel', 'dom'), pairs)  28.3 us
    ppermute x18, waiting for transfers between devices, move(): return lax.ppermute(value, ('rel', 'dom'), pairs)  25.2 us
    pallas_call x5, Pallas kernels, expert(): pl.pallas_call(functools.partial(expert_kernel, count, slots, groups, rel...  16.5 us
    unnamed x8, local copies, waits for them, and re-layouts  4.38 us
    pallas_call x1, Pallas kernels, pack(): pl.pallas_call(functools.partial(pack_kernel, relations, slots, labels),...  2.39 us
    pallas_call x3, Pallas kernels, pack_more(): pl.pallas_call(functools.partial(pack_more_kernel, slots, labels), out_sh...  1.65 us
  transfers between devices with their start and end apart: 18, of which 8 were waited for; matrix products, arithmetic and copies ran while one was open for 0% of the time, Pallas kernels for 20%

profile of v7, /device:TPU:0, one launch (start us, length us, event | category | flops | bytes accessed | tf_op | source)
XLA Modules:
  0.0 80.3 jit_solution(2720391954966921198)
XLA Ops:
  0.1 2.4 %pack_far.1 = (bf16[1040,128]{1,0:T(8,128)(2,1)S(1)}, bf16[512,1024]{1,0:T(8,128)(2,1)S(1)}, s32[1,512]{1,0:T(1,128)S(1)}, bf16[16,512]{1,0:T(8,128)(2,1)S(1)}) custom-call(s32[2]{0:T(128)S(1)} %pad_add_fusion.place_ref, s32[1,512]{1,0:T(1,128)} %bitcast.21, s32[1,512]{1,0:T(1,128)} %dest_hbm.1, bf16[512,1024]{1,0:T(8,128)(2,1)} %bitcast.19, f32[1,1024]{1,0:T(1,128)} %bitcast.20), custom_call_target="tpu_custom_call" | custom-call | flops 1 | bytes 1 | tf_op jit(solution)/shard_map/pack_far/pallas_call | solution.py:110
  2.5 4.1 %collective-permute-start.2 = (bf16[1040,128]{1,0:T(8,128)(2,1)S(1)}, bf16[1040,128]{1,0:T(8,128)(2,1)S(1)}, u32[]{:S(2)}, u32[]{:S(2)}) collective-permute-start(bf16[1040,128]{1,0:T(8,128)(2,1)S(1)} %get-tuple-element.43), channel_id=1, source_target_pairs={{0,16},{1,17},{2,18},{3,19},{4,20},{5,21},{6,22},{7,23},{8,24},{9,... | collective-permute-start | bytes 798728 | tf_op jit(solution)/shard_map/ppermute | solution.py:271
  9.0 1.6 %collective-permute-start.4 = (bf16[1040,128]{1,0:T(8,128)(2,1)S(1)}, bf16[1040,128]{1,0:T(8,128)(2,1)S(1)}, u32[]{:S(2)}, u32[]{:S(2)}) collective-permute-start(bf16[1040,128]{1,0:T(8,128)(2,1)S(1)} %get-tuple-element.44), channel_id=1, source_target_pairs={{0,8},{1,9},{2,10},{3,11},{4,12},{5,13},{6,14},{7,15},{8,0},{9,1},... | collective-permute-start | bytes 798728 | tf_op jit(solution)/shard_map/ppermute | solution.py:271
  10.7 1.7 %collective-permute-start.6 = (bf16[1040,128]{1,0:T(8,128)(2,1)S(1)}, bf16[1040,128]{1,0:T(8,128)(2,1)S(1)}, u32[]{:S(2)}, u32[]{:S(2)}) collective-permute-start(bf16[1040,128]{1,0:T(8,128)(2,1)S(1)} %get-tuple-element.46), channel_id=1, source_target_pairs={{0,4},{1,5},{2,6},{3,7},{4,0},{5,1},{6,2},{7,3},{8,12},{9,13},{10,... | collective-permute-start | bytes 798728 | tf_op jit(solution)/shard_map/ppermute | solution.py:271
  12.5 2.2 %copy-done = bf16[1,1024,2048]{2,1,0:T(8,128)(2,1)S(1)} copy-done((bf16[1,1024,2048]{2,1,0:T(8,128)(2,1)S(1)}, bf16[1,1024,2048]{2,1,0:T(8,128)(2,1)}, u32[]{:S(2)}) %copy-start) | copy-done | bytes 4194328
  14.6 2.2 %copy-done.2 = bf16[1,2048,1024]{2,1,0:T(8,128)(2,1)S(1)} copy-done((bf16[1,2048,1024]{2,1,0:T(8,128)(2,1)S(1)}, bf16[1,2048,1024]{2,1,0:T(8,128)(2,1)}, u32[]{:S(2)}) %copy-start.2) | copy-done | bytes 4194328
  16.8 2.5 %expert.5 = (f32[1024,1024]{1,0:T(8,128)S(1)}, f32[8,128]{1,0:T(8,128)S(1)}) custom-call(s32[2]{0:T(128)S(1)} %pad_add_fusion.place_ref, bf16[1040,128]{1,0:T(8,128)(2,1)S(1)} %get-tuple-element.41.refs_0_, bf16[1024,2048]{1,0:T(8,128)(2,1)S(1)} %bitcast.9, bf16[2048,1024]{1,0:T(8,128)(2,1)S(1)} %bitcast.14), custom_call_target="tpu_custom_call" | custom-call | flops 1 | bytes 1 | tf_op jit(solution)/shard_map/expert/pallas_call | solution.py:230
  19.4 5.9 %collective-permute-done.2.refs_0_ = bf16[1040,128]{1,0:T(8,128)(2,1)S(1)} collective-permute-done((bf16[1040,128]{1,0:T(8,128)(2,1)S(1)}, bf16[1040,128]{1,0:T(8,128)(2,1)S(1)}, u32[]{:S(2)}, u32[]{:S(2)}) %collective-permute-start.2) | collective-permute-done | bytes 266272 | tf_op jit(solution)/shard_map/ppermute | solution.py:271
  25.6 2.9 %collective-permute-start.3 = (bf16[1040,128]{1,0:T(8,128)(2,1)S(1)}, bf16[1040,128]{1,0:T(8,128)(2,1)S(1)}, u32[]{:S(2)}, u32[]{:S(2)}) collective-permute-start(bf16[1040,128]{1,0:T(8,128)(2,1)S(1)} %pack_more.5), channel_id=1, source_target_pairs={{0,24},{1,25},{2,26},{3,27},{4,28},{5,29},{6,30},{7,31},{8,16},{9,... | collective-permute-start | bytes 798728 | tf_op jit(solution)/shard_map/ppermute | solution.py:271
  28.5 4.9 %collective-permute-done.refs_0_ = bf16[1040,128]{1,0:T(8,128)(2,1)S(1)} collective-permute-done((bf16[1040,128]{1,0:T(8,128)(2,1)S(1)}, bf16[1040,128]{1,0:T(8,128)(2,1)S(1)}, u32[]{:S(2)}, u32[]{:S(2)}) %collective-permute-start) | collective-permute-done | bytes 266272 | tf_op jit(solution)/shard_map/ppermute | solution.py:271
  33.7 2.2 %collective-permute-start.1 = (bf16[1040,128]{1,0:T(8,128)(2,1)S(1)}, bf16[1040,128]{1,0:T(8,128)(2,1)S(1)}, u32[]{:S(2)}, u32[]{:S(2)}) collective-permute-start(bf16[1040,128]{1,0:T(8,128)(2,1)S(1)} %pack_more.4), channel_id=1, source_target_pairs={{0,28},{1,29},{2,30},{3,31},{4,24},{5,25},{6,26},{7,27},{8,20},{9,... | collective-permute-start | bytes 798728 | tf_op jit(solution)/shard_map/ppermute | solution.py:271
  36.0 3.7 %expert.6 = (f32[1024,1024]{1,0:T(8,128)S(1)}, f32[8,128]{1,0:T(8,128)}) custom-call(s32[2]{0:T(128)S(1)} %pad_add_fusion.place_ref, bf16[1040,128]{1,0:T(8,128)(2,1)S(1)} %collective-permute-done.2.refs_0_, bf16[1040,128]{1,0:T(8,128)(2,1)S(1)} %collective-permute-done.6.refs_1_, bf16[1024,2048]{1,0:T(8,128)(2,1)S(1)} %bitcast.10, ...), custom_call_target="tpu_custom_call" | custom-call | flops 1 | bytes 1 | tf_op jit(solution)/shard_map/expert/pallas_call | solution.py:230
  39.7 4.4 %collective-permute-done.5.refs_2_ = bf16[1040,128]{1,0:T(8,128)(2,1)S(1)} collective-permute-done((bf16[1040,128]{1,0:T(8,128)(2,1)S(1)}, bf16[1040,128]{1,0:T(8,128)(2,1)S(1)}, u32[]{:S(2)}, u32[]{:S(2)}) %collective-permute-start.5) | collective-permute-done | bytes 266272 | tf_op jit(solution)/shard_map/ppermute | solution.py:271
  44.0 5.2 %expert.7 = (f32[1024,1024]{1,0:T(8,128)S(1)}, f32[8,128]{1,0:T(8,128)}) custom-call(s32[2]{0:T(128)S(1)} %pad_add_fusion.place_ref, bf16[1040,128]{1,0:T(8,128)(2,1)S(1)} %collective-permute-done.refs_0_, bf16[1040,128]{1,0:T(8,128)(2,1)S(1)} %collective-permute-done.4.refs_1_, bf16[1040,128]{1,0:T(8,128)(2,1)S(1)} %collective-permute-done.5.refs_2_, ...), custom_call_target="tpu_custom_call" | custom-call | flops 1 | bytes 1 | tf_op jit(solution)/shard_map/expert/pallas_call | solution.py:230
  49.2 2.8 %expert.8 = (f32[1024,1024]{1,0:T(8,128)S(1)}, f32[8,128]{1,0:T(8,128)}) custom-call(s32[2]{0:T(128)S(1)} %pad_add_fusion.place_ref, bf16[1040,128]{1,0:T(8,128)(2,1)S(1)} %collective-permute-done.3.refs_0_, bf16[1024,2048]{1,0:T(8,128)(2,1)S(1)} %bitcast.12, bf16[2048,1024]{1,0:T(8,128)(2,1)S(1)} %bitcast.17, f32[1024,1024]{1,0:T(8,128)S(1)} %get-tuple-element.49.refs_3_), custom_call_target="tpu_custom_call" | custom-call | flops 1 | bytes 1 | tf_op jit(solution)/shard_map/expert/pallas_call | solution.py:230
  52.0 2.3 %expert.9 = (bf16[64,1024]{1,0:T(8,128)(2,1)S(1)}, bf16[64,1024]{1,0:T(8,128)(2,1)S(1)}, bf16[64,1024]{1,0:T(8,128)(2,1)S(1)}, bf16[64,1024]{1,0:T(8,128)(2,1)S(...) custom-call(s32[2]{0:T(128)S(1)} %pad_add_fusion.place_ref, ...), custom_call_target="tpu_custom_call" | custom-call | flops 1 | bytes 1 | tf_op jit(solution)/shard_map/expert/pallas_call | solution.py:230
  56.1 2.6 %collective-permute-start.16 = (bf16[64,1024]{1,0:T(8,128)(2,1)S(1)}, bf16[64,1024]{1,0:T(8,128)(2,1)S(1)}, u32[]{:S(2)}, u32[]{:S(2)}) collective-permute-start(bf16[64,1024]{1,0:T(8,128)(2,1)S(1)} %get-tuple-element.75), channel_id=1, source_target_pairs={{0,8},{1,9},{2,10},{3,11},{4,12},{5,13},{6,14},{7,15},{8,0},{9,1},... | collective-permute-start | bytes 393224 | tf_op jit(solution)/shard_map/ppermute | solution.py:271
  61.9 1.9 %collective-permute-start.11 = (bf16[64,1024]{1,0:T(8,128)(2,1)S(1)}, bf16[64,1024]{1,0:T(8,128)(2,1)S(1)}, u32[]{:S(2)}, u32[]{:S(2)}) collective-permute-start(bf16[64,1024]{1,0:T(8,128)(2,1)S(1)} %get-tuple-element.71), channel_id=1, source_target_pairs={{0,10},{1,11},{2,8},{3,9},{4,14},{5,15},{6,12},{7,13},{8,2},{9,3},... | collective-permute-start | bytes 393224 | tf_op jit(solution)/shard_map/ppermute | solution.py:271
  63.9 1.7 %collective-permute-start.9 = (bf16[64,1024]{1,0:T(8,128)(2,1)S(1)}, bf16[64,1024]{1,0:T(8,128)(2,1)S(1)}, u32[]{:S(2)}, u32[]{:S(2)}) collective-permute-start(bf16[64,1024]{1,0:T(8,128)(2,1)S(1)} %get-tuple-element.70), channel_id=1, source_target_pairs={{0,6},{1,7},{2,4},{3,5},{4,2},{5,3},{6,0},{7,1},{8,14},{9,15},{10,... | collective-permute-start | bytes 393224 | tf_op jit(solution)/shard_map/ppermute | solution.py:271
  66.6 1.7 %collective-permute-done.12 = bf16[64,1024]{1,0:T(8,128)(2,1)S(1)} collective-permute-done((bf16[64,1024]{1,0:T(8,128)(2,1)S(1)}, bf16[64,1024]{1,0:T(8,128)(2,1)S(1)}, u32[]{:S(2)}, u32[]{:S(2)}) %collective-permute-start.12) | collective-permute-done | bytes 131104 | tf_op jit(solution)/shard_map/ppermute | solution.py:271
  68.3 1.9 %collective-permute-done.11 = bf16[64,1024]{1,0:T(8,128)(2,1)S(1)} collective-permute-done((bf16[64,1024]{1,0:T(8,128)(2,1)S(1)}, bf16[64,1024]{1,0:T(8,128)(2,1)S(1)}, u32[]{:S(2)}, u32[]{:S(2)}) %collective-permute-start.11) | collective-permute-done | bytes 131104 | tf_op jit(solution)/shard_map/ppermute | solution.py:271
  70.3 3.7 %collective-permute-done.9 = bf16[64,1024]{1,0:T(8,128)(2,1)S(1)} collective-permute-done((bf16[64,1024]{1,0:T(8,128)(2,1)S(1)}, bf16[64,1024]{1,0:T(8,128)(2,1)S(1)}, u32[]{:S(2)}, u32[]{:S(2)}) %collective-permute-start.9) | collective-permute-done | bytes 131104 | tf_op jit(solution)/shard_map/ppermute | solution.py:271
  74.2 3.2 %collective-permute-start.17 = (bf16[32,1024]{1,0:T(8,128)(2,1)S(1)}, bf16[32,1024]{1,0:T(8,128)(2,1)S(1)}, u32[]{:S(2)}, u32[]{:S(2)}) collective-permute-start(bf16[32,1024]{1,0:T(8,128)(2,1)S(1)} %slice.67), channel_id=1, source_target_pairs={{0,16},{1,17},{2,18},{3,19},{4,20},{5,21},{6,22},{7,23},{8,24},{9,... | collective-permute-start | bytes 196616 | tf_op jit(solution)/shard_map/ppermute | solution.py:271
  77.3 2.2 %collective-permute-done.17 = bf16[32,1024]{1,0:T(8,128)(2,1)S(1)} collective-permute-done((bf16[32,1024]{1,0:T(8,128)(2,1)S(1)}, bf16[32,1024]{1,0:T(8,128)(2,1)S(1)}, u32[]{:S(2)}, u32[]{:S(2)}) %collective-permute-start.17) | collective-permute-done | bytes 65568 | tf_op jit(solution)/shard_map/ppermute | solution.py:271
  (40 shorter events, 10.2 us)
Async XLA Ops:
  2.5 22.8 %collective-permute-start.2 = (bf16[1040,128]{1,0:T(8,128)(2,1)S(1)}, bf16[1040,128]{1,0:T(8,128)(2,1)S(1)}, u32[]{:S(2)}, u32[]{:S(2)}) collective-permute-start(bf16[1040,128]{1,0:T(8,128)(2,1)S(1)} %get-tuple-element.43), channel_id=1, source_target_pairs={{0,16},{1,17},{2,18},{3,19},{4,20},{5,21},{6,22},{7,23},{8,24},{9,... | collective-permute-start | bytes 798728 | tf_op jit(solution)/shard_map/ppermute | solution.py:271
  7.6 25.8 %collective-permute-start = (bf16[1040,128]{1,0:T(8,128)(2,1)S(1)}, bf16[1040,128]{1,0:T(8,128)(2,1)S(1)}, u32[]{:S(2)}, u32[]{:S(2)}) collective-permute-start(bf16[1040,128]{1,0:T(8,128)(2,1)S(1)} %get-tuple-element.40), channel_id=1, source_target_pairs={{0,20},{1,21},{2,22},{3,23},{4,16},{5,17},{6,18},{7,19},{8,28},{9,... | collective-permute-start | bytes 798728 | tf_op jit(solution)/shard_map/ppermute | solution.py:271
  9.0 30.7 %collective-permute-start.4 = (bf16[1040,128]{1,0:T(8,128)(2,1)S(1)}, bf16[1040,128]{1,0:T(8,128)(2,1)S(1)}, u32[]{:S(2)}, u32[]{:S(2)}) collective-permute-start(bf16[1040,128]{1,0:T(8,128)(2,1)S(1)} %get-tuple-element.44), channel_id=1, source_target_pairs={{0,8},{1,9},{2,10},{3,11},{4,12},{5,13},{6,14},{7,15},{8,0},{9,1},... | collective-permute-start | bytes 798728 | tf_op jit(solution)/shard_map/ppermute | solution.py:271
  10.5 33.5 %collective-permute-start.5 = (bf16[1040,128]{1,0:T(8,128)(2,1)S(1)}, bf16[1040,128]{1,0:T(8,128)(2,1)S(1)}, u32[]{:S(2)}, u32[]{:S(2)}) collective-permute-start(bf16[1040,128]{1,0:T(8,128)(2,1)S(1)} %get-tuple-element.45), channel_id=1, source_target_pairs={{0,12},{1,13},{2,14},{3,15},{4,8},{5,9},{6,10},{7,11},{8,4},{9,5},... | collective-permute-start | bytes 798728 | tf_op jit(solution)/shard_map/ppermute | solution.py:271
  10.7 25.2 %collective-permute-start.6 = (bf16[1040,128]{1,0:T(8,128)(2,1)S(1)}, bf16[1040,128]{1,0:T(8,128)(2,1)S(1)}, u32[]{:S(2)}, u32[]{:S(2)}) collective-permute-start(bf16[1040,128]{1,0:T(8,128)(2,1)S(1)} %get-tuple-element.46), channel_id=1, source_target_pairs={{0,4},{1,5},{2,6},{3,7},{4,0},{5,1},{6,2},{7,3},{8,12},{9,13},{10,... | collective-permute-start | bytes 798728 | tf_op jit(solution)/shard_map/ppermute | solution.py:271
  12.5 2.2 %copy-start = (bf16[1,1024,2048]{2,1,0:T(8,128)(2,1)S(1)}, bf16[1,1024,2048]{2,1,0:T(8,128)(2,1)}, u32[]{:S(2)}) copy-start(bf16[1,1024,2048]{2,1,0:T(8,128)(2,1)} %param.8) | copy-start | bytes 12582916
  14.6 2.2 %copy-start.2 = (bf16[1,2048,1024]{2,1,0:T(8,128)(2,1)S(1)}, bf16[1,2048,1024]{2,1,0:T(8,128)(2,1)}, u32[]{:S(2)}) copy-start(bf16[1,2048,1024]{2,1,0:T(8,128)(2,1)} %param.9) | copy-start | bytes 12582916
  16.8 19.1 %copy-start.1 = (bf16[1,1024,2048]{2,1,0:T(8,128)(2,1)S(1)}, bf16[1,1024,2048]{2,1,0:T(8,128)(2,1)}, u32[]{:S(2)}) copy-start(bf16[1,1024,2048]{2,1,0:T(8,128)(2,1)} %param.8) | copy-start | bytes 12582916
  16.8 19.1 %copy-start.3 = (bf16[1,2048,1024]{2,1,0:T(8,128)(2,1)S(1)}, bf16[1,2048,1024]{2,1,0:T(8,128)(2,1)}, u32[]{:S(2)}) copy-start(bf16[1,2048,1024]{2,1,0:T(8,128)(2,1)} %param.9) | copy-start | bytes 12582916
  25.6 23.6 %collective-permute-start.3 = (bf16[1040,128]{1,0:T(8,128)(2,1)S(1)}, bf16[1040,128]{1,0:T(8,128)(2,1)S(1)}, u32[]{:S(2)}, u32[]{:S(2)}) collective-permute-start(bf16[1040,128]{1,0:T(8,128)(2,1)S(1)} %pack_more.5), channel_id=1, source_target_pairs={{0,24},{1,25},{2,26},{3,27},{4,28},{5,29},{6,30},{7,31},{8,16},{9,... | collective-permute-start | bytes 798728 | tf_op jit(solution)/shard_map/ppermute | solution.py:271
  33.7 18.3 %collective-permute-start.1 = (bf16[1040,128]{1,0:T(8,128)(2,1)S(1)}, bf16[1040,128]{1,0:T(8,128)(2,1)S(1)}, u32[]{:S(2)}, u32[]{:S(2)}) collective-permute-start(bf16[1040,128]{1,0:T(8,128)(2,1)S(1)} %pack_more.4), channel_id=1, source_target_pairs={{0,28},{1,29},{2,30},{3,31},{4,24},{5,25},{6,26},{7,27},{8,20},{9,... | collective-permute-start | bytes 798728 | tf_op jit(solution)/shard_map/ppermute | solution.py:271
  54.4 1.6 %collective-permute-start.14 = (bf16[128,1024]{1,0:T(8,128)(2,1)S(1)}, bf16[128,1024]{1,0:T(8,128)(2,1)S(1)}, u32[]{:S(2)}, u32[]{:S(2)}) collective-permute-start(bf16[128,1024]{1,0:T(8,128)(2,1)S(1)} %pad_maximum_fusion.2), channel_id=1, source_target_pairs={{0,1},{1,0},{2,3},{3,2},{4,5},{5,4},{6,7},{7,6},{8,9},{9,8},{10,11... | collective-permute-start | bytes 786440 | tf_op jit(solution)/shard_map/ppermute | solution.py:271
  54.5 4.8 %collective-permute-start.10 = (bf16[192,1024]{1,0:T(8,128)(2,1)S(1)}, bf16[192,1024]{1,0:T(8,128)(2,1)S(1)}, u32[]{:S(2)}, u32[]{:S(2)}) collective-permute-start(bf16[192,1024]{1,0:T(8,128)(2,1)S(1)} %pad_maximum_fusion.1), channel_id=1, source_target_pairs={{0,1},{1,0},{2,3},{3,2},{4,5},{5,4},{6,7},{7,6},{8,9},{9,8},{10,11... | collective-permute-start | bytes 1179656 | tf_op jit(solution)/shard_map/ppermute | solution.py:271
  55.1 6.8 %collective-permute-start.7 = (bf16[192,1024]{1,0:T(8,128)(2,1)S(1)}, bf16[192,1024]{1,0:T(8,128)(2,1)S(1)}, u32[]{:S(2)}, u32[]{:S(2)}) collective-permute-start(bf16[192,1024]{1,0:T(8,128)(2,1)S(1)} %pad_maximum_fusion), channel_id=1, source_target_pairs={{0,1},{1,0},{2,3},{3,2},{4,5},{5,4},{6,7},{7,6},{8,9},{9,8},{10,11... | collective-permute-start | bytes 1179656 | tf_op jit(solution)/shard_map/ppermute | solution.py:271
  56.1 7.8 %collective-permute-start.16 = (bf16[64,1024]{1,0:T(8,128)(2,1)S(1)}, bf16[64,1024]{1,0:T(8,128)(2,1)S(1)}, u32[]{:S(2)}, u32[]{:S(2)}) collective-permute-start(bf16[64,1024]{1,0:T(8,128)(2,1)S(1)} %get-tuple-element.75), channel_id=1, source_target_pairs={{0,8},{1,9},{2,10},{3,11},{4,12},{5,13},{6,14},{7,15},{8,0},{9,1},... | collective-permute-start | bytes 393224 | tf_op jit(solution)/shard_map/ppermute | solution.py:271
  58.6 6.9 %collective-permute-start.15 = (bf16[64,1024]{1,0:T(8,128)(2,1)S(1)}, bf16[64,1024]{1,0:T(8,128)(2,1)S(1)}, u32[]{:S(2)}, u32[]{:S(2)}) collective-permute-start(bf16[64,1024]{1,0:T(8,128)(2,1)S(1)} %get-tuple-element.74), channel_id=1, source_target_pairs={{0,4},{1,5},{2,6},{3,7},{4,0},{5,1},{6,2},{7,3},{8,12},{9,13},{10,... | collective-permute-start | bytes 393224 | tf_op jit(solution)/shard_map/ppermute | solution.py:271
  59.4 7.2 %collective-permute-start.13 = (bf16[64,1024]{1,0:T(8,128)(2,1)S(1)}, bf16[64,1024]{1,0:T(8,128)(2,1)S(1)}, u32[]{:S(2)}, u32[]{:S(2)}) collective-permute-start(bf16[64,1024]{1,0:T(8,128)(2,1)S(1)} %get-tuple-element.72), channel_id=1, source_target_pairs={{0,2},{1,3},{2,0},{3,1},{4,6},{5,7},{6,4},{7,5},{8,10},{9,11},{10,... | collective-permute-start | bytes 393224 | tf_op jit(solution)/shard_map/ppermute | solution.py:271
  61.0 7.3 %collective-permute-start.12 = (bf16[64,1024]{1,0:T(8,128)(2,1)S(1)}, bf16[64,1024]{1,0:T(8,128)(2,1)S(1)}, u32[]{:S(2)}, u32[]{:S(2)}) collective-permute-start(bf16[64,1024]{1,0:T(8,128)(2,1)S(1)} %get-tuple-element.73), channel_id=1, source_target_pairs={{0,12},{1,13},{2,14},{3,15},{4,8},{5,9},{6,10},{7,11},{8,4},{9,5},... | collective-permute-start | bytes 393224 | tf_op jit(solution)/shard_map/ppermute | solution.py:271
  61.9 8.4 %collective-permute-start.11 = (bf16[64,1024]{1,0:T(8,128)(2,1)S(1)}, bf16[64,1024]{1,0:T(8,128)(2,1)S(1)}, u32[]{:S(2)}, u32[]{:S(2)}) collective-permute-start(bf16[64,1024]{1,0:T(8,128)(2,1)S(1)} %get-tuple-element.71), channel_id=1, source_target_pairs={{0,10},{1,11},{2,8},{3,9},{4,14},{5,15},{6,12},{7,13},{8,2},{9,3},... | collective-permute-start | bytes 393224 | tf_op jit(solution)/shard_map/ppermute | solution.py:271
  63.9 10.1 %collective-permute-start.9 = (bf16[64,1024]{1,0:T(8,128)(2,1)S(1)}, bf16[64,1024]{1,0:T(8,128)(2,1)S(1)}, u32[]{:S(2)}, u32[]{:S(2)}) collective-permute-start(bf16[64,1024]{1,0:T(8,128)(2,1)S(1)} %get-tuple-element.70), channel_id=1, source_target_pairs={{0,6},{1,7},{2,4},{3,5},{4,2},{5,3},{6,0},{7,1},{8,14},{9,15},{10,... | collective-permute-start | bytes 393224 | tf_op jit(solution)/shard_map/ppermute | solution.py:271
  65.5 8.4 %collective-permute-start.8 = (bf16[64,1024]{1,0:T(8,128)(2,1)S(1)}, bf16[64,1024]{1,0:T(8,128)(2,1)S(1)}, u32[]{:S(2)}, u32[]{:S(2)}) collective-permute-start(bf16[64,1024]{1,0:T(8,128)(2,1)S(1)} %get-tuple-element.69), channel_id=1, source_target_pairs={{0,14},{1,15},{2,12},{3,13},{4,10},{5,11},{6,8},{7,9},{8,6},{9,7},... | collective-permute-start | bytes 393224 | tf_op jit(solution)/shard_map/ppermute | solution.py:271
  74.2 5.4 %collective-permute-start.17 = (bf16[32,1024]{1,0:T(8,128)(2,1)S(1)}, bf16[32,1024]{1,0:T(8,128)(2,1)S(1)}, u32[]{:S(2)}, u32[]{:S(2)}) collective-permute-start(bf16[32,1024]{1,0:T(8,128)(2,1)S(1)} %slice.67), channel_id=1, source_target_pairs={{0,16},{1,17},{2,18},{3,19},{4,20},{5,21},{6,22},{7,23},{8,24},{9,... | collective-permute-start | bytes 196616 | tf_op jit(solution)/shard_map/ppermute | solution.py:271
